TPU v7x, 256 devices: a whole 4x4x8 slice. The times are simulated.
256 devices in a mesh: gx: 16 (over x, z_hi, core), gy: 4 (over y), gz: 4 (over z_lo).
Axes of the slice: x: 4, y: 4, z: 8 (z_hi: 2, z_lo: 4; z = z_hi * 4 + z_lo), core: 2. Of those that a mesh axis runs over, the one named last changes fastest.
Arguments:
- fine_state: bfloat16 [262144, 512], P(('gx', 'gy', 'gz')), may hold values from -6 to 6
- fine_nbrs: int32 [262144, 6], P(('gx', 'gy', 'gz')), may hold values from 0 to 1792, as said below
- send_rows: int32 [256, 6, 128], P(('gx', 'gy', 'gz')), may hold values from 0 to 1023
- ghost_counts: int32 [256, 6], P(('gx', 'gy', 'gz')), may hold values from 32 to 128, as said below
- fine_parent: int32 [262144], P(('gx', 'gy', 'gz')), may hold values from 0 to 127, as said below
- medium_state: bfloat16 [32768, 512], P(('gx', 'gy', 'gz')), may hold values from -6 to 6
- medium_parent: int32 [32768], P(('gx', 'gy', 'gz')), may hold values from 0 to 15, as said below
- coarse_state: bfloat16 [4096, 512], P(('gx', 'gy', 'gz')), may hold values from -6 to 6
- coarse_nbrs: int32 [4096, 64], P(('gx', 'gy', 'gz')), may hold values from 0 to 4095, as said below
- fine_edge_in: bfloat16 [1024, 512], replicated, may hold values from -0.1875 to 0.1875
- fine_edge_bias: float32 [512], replicated, may hold values from -3 to 3
- fine_edge_out: bfloat16 [512, 512], replicated, may hold values from -0.25 to 0.25
- fine_edge_gain: float32 [512], replicated, may hold values from 0.1 to 1.9
- fine_node_in: bfloat16 [1024, 512], replicated, may hold values from -0.1875 to 0.1875
- fine_node_bias: float32 [512], replicated, may hold values from -3 to 3
- fine_node_out: bfloat16 [512, 512], replicated, may hold values from -0.25 to 0.25
- fine_node_gain: float32 [512], replicated, may hold values from 0.1 to 1.9
- coarse_edge_in: bfloat16 [1024, 512], replicated, may hold values from -0.1875 to 0.1875
- coarse_edge_bias: float32 [512], replicated, may hold values from -3 to 3
- coarse_edge_out: bfloat16 [512, 512], replicated, may hold values from -0.25 to 0.25
- coarse_edge_gain: float32 [512], replicated, may hold values from 0.1 to 1.9
- coarse_node_in: bfloat16 [1024, 512], replicated, may hold values from -0.1875 to 0.1875
- coarse_node_bias: float32 [512], replicated, may hold values from -3 to 3
- coarse_node_out: bfloat16 [512, 512], replicated, may hold values from -0.25 to 0.25
- coarse_node_gain: float32 [512], replicated, may hold values from 0.1 to 1.9
Outputs:
- fine_out: bfloat16 [262144, 512], P(('gx', 'gy', 'gz'))
- medium_out: bfloat16 [32768, 512], P(('gx', 'gy', 'gz'))
- coarse_out: bfloat16 [4096, 512], P(('gx', 'gy', 'gz'))
Inputs may be any that keep to these rules, and one draw needn't show every extreme that they name: `fine_nbrs`: row i of device p lists node i's neighbours as rows of table_p: 0 to 1023 own nodes, then 6 ghost blocks of 128 rows in the order of ghosts; a ghost row is named only if the sending neighbour exists and the row lies below that neighbour's count for the face it sends. The value 1024 + 6 * 128 marks an empty slot; empty slots follow the used ones, and at least 4 slots of every row are used. `ghost_counts`: entry f of device p counts the used rows of the block that p sends from face f; on every device one face is full. `send_rows`: local fine rows of the sending device; rows at or past the face's count are not used. `fine_parent`: A local medium index of the same device; every medium node has at least one child. `medium_parent`: A local coarse index of the same device; every coarse node has at least one child. `coarse_nbrs`: global coarse rows anywhere on the mesh.
All inputs are finite; a program needn't handle non-finite values.
Results may differ from a plain program's by a relative error of at most 0.0075.
Values may be sent and summed in bfloat16 or wider, within the bound.
No kernel may reach another device: no remote copies, remote signals or barrier semaphores. Data moves between devices by JAX's collectives and lax.ppermute only.
A program may use at most 128 MiB of HBM per device.

v0:
```python
import jax
import jax.numpy as jnp
from jax import lax
from jax.sharding import Mesh
from jax.sharding import PartitionSpec as P

GX = ("gx_0", "gx_1", "gx_2")
GX_GY_GZ = ("gx_0", "gx_1", "gx_2", "gy", "gz")


def extended(block, sides, width):
    for axis, dim in sides:
        count = lax.axis_size(axis)
        forward = [(i, i + 1) for i in range(count - 1)]
        backward = [(target, source) for source, target in forward]
        low = lax.ppermute(
            lax.slice_in_dim(block, block.shape[dim] - width, None, axis=dim), axis, forward
        )
        high = lax.ppermute(lax.slice_in_dim(block, 0, width, axis=dim), axis, backward)
        block = jnp.concatenate([low, block, high], axis=dim)
    return block


def edges_of(length, count):
    lap = length // count
    if lap >= 8:
        lap -= lap % 8
    return [lap * k for k in range(1, count)]


def stacked_from(shard, axes, order):
    parts = shard[None]
    for k in order:
        parts = lax.all_gather(parts, axes[k], axis=0, tiled=True)
    block = [lax.axis_size(axes[k]) for k in reversed(order)]
    parts = parts.reshape(*block, *shard.shape)
    turned = sorted(range(len(order)), key=lambda place: order[len(order) - 1 - place])
    return parts.transpose(*turned, *range(len(order), parts.ndim)).reshape(-1, *shard.shape)


def joined_along(parts, dim):
    parts = jnp.moveaxis(parts, 0, dim)
    shape = parts.shape
    return parts.reshape(*shape[:dim], shape[dim] * shape[dim + 1], *shape[dim + 2 :])


def gather_at_once(shard, axes, dim):
    numbers = list(range(len(axes)))[::-1]
    widest = shard.shape.index(max(shard.shape[:-1] or shard.shape))
    edges = [0, *edges_of(shard.shape[widest], len(axes)), shard.shape[widest]]
    finished = []
    for k, (start, end) in enumerate(zip(edges, edges[1:])):
        if end > start:
            share = lax.slice_in_dim(shard, start, end, axis=widest)
            finished.append(stacked_from(share, axes, numbers[k:] + numbers[:k]))
    return joined_along(jnp.concatenate(finished, axis=widest + 1), dim)


def layer_norm(values):
    center = values - jnp.mean(values, axis=-1, keepdims=True)
    spread = jnp.mean(center * center, axis=-1, keepdims=True)
    return center * lax.rsqrt(spread + 1e-05)


def edge_messages(sender_rows, receiver, biases, out_weight, gains, slot_count):
    features = receiver.shape[1]
    combined = (
        sender_rows.astype(jnp.float32).reshape(-1, slot_count, features)
        + receiver[:, None, :]
        + biases
    )
    hidden = jax.nn.relu(combined).astype(jnp.bfloat16).reshape(-1, features)
    return layer_norm(jnp.dot(hidden, out_weight, preferred_element_type=jnp.float32)) * gains


def node_update(current, incoming, in_weight, biases, out_weight, gains):
    features = current.shape[1]
    combined = jnp.dot(current, in_weight[:features], preferred_element_type=jnp.float32)
    combined = (
        combined
        + jnp.dot(incoming, in_weight[features:], preferred_element_type=jnp.float32)
        + biases
    )
    hidden = jax.nn.relu(combined).astype(jnp.bfloat16)
    return layer_norm(jnp.dot(hidden, out_weight, preferred_element_type=jnp.float32)) * gains


def trade_states(outgoing):
    traded_first = extended(outgoing[0:2], ((GX, 0),), 1)
    traded_second = extended(outgoing[2:4], (("gy", 0),), 1)
    traded_third = extended(outgoing[4:6], (("gz", 0),), 1)
    return jnp.concatenate(
        [
            traded_first[0],
            traded_first[3],
            traded_second[0],
            traded_second[3],
            traded_third[0],
            traded_third[3],
        ],
        axis=0,
    )


def local(
    fine_state,
    fine_nbrs,
    send_rows,
    ghost_counts,
    fine_parent,
    medium_state,
    medium_parent,
    coarse_state,
    coarse_nbrs,
    fine_edge_in,
    fine_edge_bias,
    fine_edge_out,
    fine_edge_gain,
    fine_node_in,
    fine_node_bias,
    fine_node_out,
    fine_node_gain,
    coarse_edge_in,
    coarse_edge_bias,
    coarse_edge_out,
    coarse_edge_gain,
    coarse_node_in,
    coarse_node_bias,
    coarse_node_out,
    coarse_node_gain,
):
    own_rows, features = fine_state.shape
    slot_count = fine_nbrs.shape[1]
    face_rows = send_rows.shape[2]
    sender_weight = fine_edge_in[:features]
    receiver = jnp.dot(fine_state, fine_edge_in[features:], preferred_element_type=jnp.float32)
    in_count = lax.broadcasted_iota(jnp.int32, (6, face_rows), 1) < ghost_counts.reshape(6, 1)
    picked = jnp.take(fine_state, send_rows.reshape(-1), axis=0).reshape(6, face_rows, features)
    outgoing = jnp.where(in_count[:, :, None], picked, jnp.zeros_like(picked))
    ghosts = trade_states(outgoing)
    lookup = jnp.concatenate([fine_state, ghosts, jnp.zeros((1, features), jnp.bfloat16)], axis=0)
    sender = jnp.dot(lookup, sender_weight, preferred_element_type=jnp.float32).astype(jnp.bfloat16)
    messages = edge_messages(
        jnp.take(sender, fine_nbrs.reshape(-1), axis=0),
        receiver,
        fine_edge_bias,
        fine_edge_out,
        fine_edge_gain,
        slot_count,
    )
    live_slots = (fine_nbrs < own_rows + 6 * face_rows).astype(jnp.float32)
    incoming = jnp.sum(
        messages.reshape(own_rows, slot_count, features) * live_slots[:, :, None], axis=1
    ).astype(jnp.bfloat16)
    fine_new = fine_state.astype(jnp.float32) + node_update(
        fine_state, incoming, fine_node_in, fine_node_bias, fine_node_out, fine_node_gain
    )
    medium_rows = medium_state.shape[0]
    coarse_rows = coarse_state.shape[0]
    fine_member = fine_parent[None, :] == lax.broadcasted_iota(
        jnp.int32, (medium_rows, own_rows), 0
    )
    child_sum = jnp.dot(
        fine_member.astype(jnp.bfloat16), fine_state, preferred_element_type=jnp.float32
    )
    child_count = jnp.sum(fine_member.astype(jnp.float32), axis=1, keepdims=True)
    medium_pool = medium_state.astype(jnp.float32) + child_sum / child_count
    medium_member = (
        medium_parent[None, :] == lax.broadcasted_iota(jnp.int32, (coarse_rows, medium_rows), 0)
    ).astype(jnp.float32)
    coarse_sum = jnp.dot(medium_member, medium_pool, precision=lax.Precision.HIGHEST)
    coarse_pool = (
        coarse_state.astype(jnp.float32)
        + coarse_sum / jnp.sum(medium_member, axis=1, keepdims=True)
    ).astype(jnp.bfloat16)
    coarse_flat = coarse_nbrs.reshape(-1)
    link_count = coarse_nbrs.shape[1]
    coarse_sender_weight = coarse_edge_in[:features]
    all_rows = gather_at_once(coarse_pool, GX_GY_GZ, 0)
    coarse_sender = jnp.dot(
        jnp.take(all_rows, coarse_flat, axis=0),
        coarse_sender_weight,
        preferred_element_type=jnp.float32,
    ).astype(jnp.bfloat16)
    coarse_receiver = jnp.dot(
        coarse_pool, coarse_edge_in[features:], preferred_element_type=jnp.float32
    )
    coarse_msgs = edge_messages(
        coarse_sender,
        coarse_receiver,
        coarse_edge_bias,
        coarse_edge_out,
        coarse_edge_gain,
        link_count,
    )
    coarse_incoming = jnp.sum(
        coarse_msgs.reshape(coarse_rows, link_count, features), axis=1
    ).astype(jnp.bfloat16)
    coarse_delta = node_update(
        coarse_pool,
        coarse_incoming,
        coarse_node_in,
        coarse_node_bias,
        coarse_node_out,
        coarse_node_gain,
    )
    coarse_final = (coarse_pool.astype(jnp.float32) + coarse_delta).astype(jnp.bfloat16)
    medium_delta = jnp.take(coarse_delta, medium_parent, axis=0)
    medium_final = (medium_pool + medium_delta).astype(jnp.bfloat16)
    fine_final = (fine_new + jnp.take(medium_delta, fine_parent, axis=0)).astype(jnp.bfloat16)
    return (fine_final, medium_final, coarse_final)


def solution(mesh):
    torus = Mesh(
        mesh.devices.reshape(4, 2, 2, mesh.shape["gy"], mesh.shape["gz"]),
        ("gx_0", "gx_1", "gx_2", "gy", "gz"),
    )
    placed = (
        P(GX_GY_GZ, None),
        P(GX_GY_GZ, None),
        P(GX_GY_GZ, None, None),
        P(GX_GY_GZ, None),
        P(GX_GY_GZ),
        P(GX_GY_GZ, None),
        P(GX_GY_GZ),
        P(GX_GY_GZ, None),
        P(GX_GY_GZ, None),
        P(),
        P(),
        P(),
        P(),
        P(),
        P(),
        P(),
        P(),
        P(),
        P(),
        P(),
        P(),
        P(),
        P(),
        P(),
        P(),
    )
    return jax.shard_map(
        local,
        mesh=torus,
        in_specs=placed,
        out_specs=(P(GX_GY_GZ, None), P(GX_GY_GZ, None), P(GX_GY_GZ, None)),
        check_vma=False,
    )
```

profile of v0, /device:TPU:1, one launch (start us, length us, event | category | flops | bytes accessed | tf_op | source)
XLA Modules:
  0.0 499.4 jit_solution(556025854398983436)
XLA Ops:
  15.4 10.2 %collective-permute-start = (bf16[1,128,512]{2,1,0:T(8,128)(2,1)}, bf16[1,128,512]{2,1,0:T(8,128)(2,1)}, u32[]{:S(2)}, u32[]{:S(2)}) collective-permute-start(bf16[1,128,512]{2,1,0:T(8,128)(2,1)} %get-tuple-element.24), channel_id=1, source_target_pairs={{0,16},{16,32},{32,48},{48,64},{64,80},{80,96},{96,112},{112,128},... | collective-permute-start | bytes 393224 | tf_op jit(solution)/shard_map/ppermute | solution.py:16
  36.8 9.4 %all-gather.9 = bf16[4,4,512]{2,1,0:T(4,128)(2,1)S(1)} all-gather(bf16[1,4,512]{2,1,0:T(4,128)(2,1)S(1)} %slice_bitcast_fusion), channel_id=6, replica_groups=mesh['gx_0'=4,'gx_1'=2,'gx_2'=2,'gy'=4,'gz'=4] {'gx_0'}, dimensions={0}, use_global_device_ids=true | all-gather | bytes 20480 | tf_op jit(solution)/shard_map/all_gather | solution.py:34
  46.2 10.2 %all_gather.96 = bf16[16,4,512]{2,1,0:T(4,128)(2,1)S(1)} all-gather(bf16[4,4,512]{2,1,0:T(4,128)(2,1)S(1)} %all-gather.9), channel_id=1, replica_groups=mesh['gx_0'=4,'gx_1'=2,'gx_2'=2,'gy'=4,'gz'=4] {'gz'}, dimensions={0}, use_global_device_ids=true | all-gather | bytes 81920 | tf_op jit(solution)/shard_map/all_gather | solution.py:34
  56.4 10.4 %all_gather.97 = bf16[64,4,512]{2,1,0:T(4,128)(2,1)S(1)} all-gather(bf16[16,4,512]{2,1,0:T(4,128)(2,1)S(1)} %all_gather.96), channel_id=1, replica_groups=mesh['gx_0'=4,'gx_1'=2,'gx_2'=2,'gy'=4,'gz'=4] {'gy'}, dimensions={0}, use_global_device_ids=true | all-gather | bytes 327680 | tf_op jit(solution)/shard_map/all_gather | solution.py:34
  66.8 12.0 %all_gather.98 = bf16[128,4,512]{2,1,0:T(4,128)(2,1)} all-gather(bf16[64,4,512]{2,1,0:T(4,128)(2,1)S(1)} %all_gather.97), channel_id=1, replica_groups=mesh['gx_0'=4,'gx_1'=2,'gx_2'=2,'gy'=4,'gz'=4] {'gx_2'}, dimensions={0}, use_global_device_ids=true | all-gather | bytes 786432 | tf_op jit(solution)/shard_map/all_gather | solution.py:34
  94.1 9.6 %add.203 = f32[1024,6,512]{2,1,0:T(8,128)} broadcast(f32[1024,512]{1,0:T(8,128)} %fusion.33), dimensions={0,2} | broadcast | bytes 14680064 | tf_op jit(solution)/shard_map/add | solution.py:68
  103.7 15.7 %add.204 = f32[6144,512]{1,0:T(8,128)} reshape(f32[1024,6,512]{2,1,0:T(8,128)} %add.203) | data formatting | bytes 25165824 | tf_op jit(solution)/shard_map/add | solution.py:68
  138.6 10.4 %all_gather.92 = bf16[32,3,512]{2,0,1:T(8,128)(2,1)S(1)} all-gather(bf16[8,3,512]{2,0,1:T(8,128)(2,1)S(1)} %copy.72), channel_id=1, replica_groups=mesh['gx_0'=4,'gx_1'=2,'gx_2'=2,'gy'=4,'gz'=4] {'gz'}, dimensions={0}, use_global_device_ids=true | all-gather | bytes 122880 | tf_op jit(solution)/shard_map/all_gather | solution.py:34
  149.0 9.8 %all_gather.93 = bf16[128,3,512]{2,0,1:T(8,128)(2,1)S(1)} all-gather(bf16[32,3,512]{2,0,1:T(8,128)(2,1)S(1)} %all_gather.92), channel_id=1, replica_groups=mesh['gx_0'=4,'gx_1'=2,'gx_2'=2,'gy'=4,'gz'=4] {'gy'}, dimensions={0}, use_global_device_ids=true | all-gather | bytes 491520 | tf_op jit(solution)/shard_map/all_gather | solution.py:34
  158.8 12.0 %all_gather.94 = bf16[256,3,512]{2,0,1:T(8,128)(2,1)S(1)} all-gather(bf16[128,3,512]{2,0,1:T(8,128)(2,1)S(1)} %all_gather.93), channel_id=1, replica_groups=mesh['gx_0'=4,'gx_1'=2,'gx_2'=2,'gy'=4,'gz'=4] {'gx_2'}, dimensions={0}, use_global_device_ids=true | all-gather | bytes 1179648 | tf_op jit(solution)/shard_map/all_gather | solution.py:34
  190.9 10.7 %all_gather.88 = bf16[64,3,512]{2,0,1:T(8,128)(2,1)S(1)} all-gather(bf16[16,3,512]{2,0,1:T(8,128)(2,1)S(1)} %copy.70), channel_id=1, replica_groups=mesh['gx_0'=4,'gx_1'=2,'gx_2'=2,'gy'=4,'gz'=4] {'gz'}, dimensions={0}, use_global_device_ids=true | all-gather | bytes 245760 | tf_op jit(solution)/shard_map/all_gather | solution.py:34
  201.6 11.0 %all_gather.89 = bf16[256,3,512]{2,0,1:T(8,128)(2,1)S(1)} all-gather(bf16[64,3,512]{2,0,1:T(8,128)(2,1)S(1)} %all_gather.88), channel_id=1, replica_groups=mesh['gx_0'=4,'gx_1'=2,'gx_2'=2,'gy'=4,'gz'=4] {'gy'}, dimensions={0}, use_global_device_ids=true | all-gather | bytes 983040 | tf_op jit(solution)/shard_map/all_gather | solution.py:34
  214.6 9.5 %all-gather.6 = bf16[4,3,512]{2,1,0:T(4,128)(2,1)S(1)} all-gather(bf16[1,3,512]{2,1,0:T(4,128)(2,1)} %get-tuple-element.27), channel_id=3, replica_groups=mesh['gx_0'=4,'gx_1'=2,'gx_2'=2,'gy'=4,'gz'=4] {'gy'}, dimensions={0}, use_global_device_ids=true | all-gather | bytes 15360 | tf_op jit(solution)/shard_map/all_gather | solution.py:34
  224.0 13.7 %all_gather.81 = bf16[8,3,512]{2,1,0:T(4,128)(2,1)S(1)} all-gather(bf16[4,3,512]{2,1,0:T(4,128)(2,1)S(1)} %all-gather.6), channel_id=1, replica_groups=mesh['gx_0'=4,'gx_1'=2,'gx_2'=2,'gy'=4,'gz'=4] {'gx_2'}, dimensions={0}, use_global_device_ids=true | all-gather | bytes 36864 | tf_op jit(solution)/shard_map/all_gather | solution.py:34
  254.2 13.7 %all_gather.84 = bf16[256,3,512]{2,0,1:T(8,128)(2,1)S(1)} all-gather(bf16[64,3,512]{2,0,1:T(8,128)(2,1)S(1)} %all_gather.83), channel_id=1, replica_groups=mesh['gx_0'=4,'gx_1'=2,'gx_2'=2,'gy'=4,'gz'=4] {'gz'}, dimensions={0}, use_global_device_ids=true | all-gather | bytes 983040 | tf_op jit(solution)/shard_map/all_gather | solution.py:34
  269.7 10.5 %all-gather.5 = bf16[4,3,512]{2,1,0:T(4,128)(2,1)S(1)} all-gather(bf16[1,3,512]{2,1,0:T(4,128)(2,1)} %get-tuple-element.28), channel_id=2, replica_groups=mesh['gx_0'=4,'gx_1'=2,'gx_2'=2,'gy'=4,'gz'=4] {'gz'}, dimensions={0}, use_global_device_ids=true | all-gather | bytes 15360 | tf_op jit(solution)/shard_map/all_gather | solution.py:34
  280.2 9.3 %all_gather.76 = bf16[16,3,512]{2,1,0:T(4,128)(2,1)S(1)} all-gather(bf16[4,3,512]{2,1,0:T(4,128)(2,1)S(1)} %all-gather.5), channel_id=1, replica_groups=mesh['gx_0'=4,'gx_1'=2,'gx_2'=2,'gy'=4,'gz'=4] {'gy'}, dimensions={0}, use_global_device_ids=true | all-gather | bytes 61440 | tf_op jit(solution)/shard_map/all_gather | solution.py:34
  289.5 14.0 %all_gather.77 = bf16[32,3,512]{2,0,1:T(8,128)(2,1)S(1)} all-gather(bf16[16,3,512]{2,0,1:T(8,128)(2,1)S(1)} %copy.67), channel_id=1, replica_groups=mesh['gx_0'=4,'gx_1'=2,'gx_2'=2,'gy'=4,'gz'=4] {'gx_2'}, dimensions={0}, use_global_device_ids=true | all-gather | bytes 147456 | tf_op jit(solution)/shard_map/all_gather | solution.py:34
  312.3 12.2 %all_gather.79 = bf16[256,3,512]{2,0,1:T(8,128)(2,1)S(1)} all-gather(bf16[64,3,512]{2,0,1:T(8,128)(2,1)S(1)} %all_gather.78), channel_id=1, replica_groups=mesh['gx_0'=4,'gx_1'=2,'gx_2'=2,'gy'=4,'gz'=4] {'gx_0'}, dimensions={0}, use_global_device_ids=true | all-gather | bytes 983040 | tf_op jit(solution)/shard_map/all_gather | solution.py:34
  334.0 25.7 %gather_fusion.1 = bf16[6144,512]{1,0:T(8,128)(2,1)} fusion(bf16[1793,512]{1,0:T(8,128)(2,1)S(1)} %convolution_convert_fusion, s32[6144]{0:T(1024)S(1)} %copy-done.12), kind=kCustom, calls=%fused_computation.1 | custom fusion | bytes 12607488 | tf_op jit(solution)/shard_map/jit(_take)/gather | solution.py:144
  359.7 9.5 %fusion.56 = (f32[6144]{0:T(1024)S(1)}, f32[6144,512]{1,0:T(8,128)S(1)}) fusion(bf16[512,512]{1,0:T(8,128)(2,1)S(1)} %copy-done, f32[6144,512]{1,0:T(8,128)} %add.204, f32[512]{0:T(512)S(1)} %copy-done.23, bf16[6144,512]{1,0:T(8,128)(2,1)} %gather_fusion.1, pred[6144]{0:T(1024)(128)(4,1)S(1)} %copy-done.15), kind=kOutput, calls=%fused_computation.121 | convolution fusion | flops 3243239424 | bytes 32014336 | tf_op jit(solution)/shard_map/dot_general | solution.py:73
  376.9 15.1 %reshape.275 = f32[1024,6,512]{2,1,0:T(8,128)} reshape(f32[6144,512]{1,0:T(8,128)} %multiply_multiply_fusion) | data formatting | bytes 25165824 | tf_op jit(solution)/shard_map/reshape | solution.py:153
  392.0 10.4 %multiply_reduce_fusion = bf16[1024,512]{1,0:T(8,128)(2,1)} fusion(f32[1024,6,512]{2,1,0:T(8,128)} %reshape.275, f32[1024,6]{1,0:T(8,128)S(1)} %copy-done.3), kind=kLoop, calls=%fused_computation.5 | loop fusion | flops 5767168 | bytes 13656064 | tf_op jit(solution)/shard_map/reduce_sum | solution.py:152
  408.9 54.2 %concatenate.7 = bf16[256,16,512]{2,1,0:T(8,128)(2,1)} concatenate(bf16[256,3,512]{2,1,0:T(4,128)(2,1)} %copy.75, bf16[256,3,512]{2,1,0:T(4,128)(2,1)} %bitcast.81, bf16[256,3,512]{2,1,0:T(4,128)(2,1)} %bitcast.80, bf16[256,3,512]{2,1,0:T(4,128)(2,1)} %bitcast.79, bf16[256,4,512]{2,1,0:T(4,128)(2,1)} %bitcast.82), dimensions={1} | concatenate | bytes 8388608 | tf_op jit(solution)/shard_map/concatenate | solution.py:56
  (175 shorter events, 155.7 us)
Async XLA Ops:
  7.2 352.5 %copy-start = (bf16[512,512]{1,0:T(8,128)(2,1)S(1)}, bf16[512,512]{1,0:T(8,128)(2,1)}, u32[]{:S(2)}) copy-start(bf16[512,512]{1,0:T(8,128)(2,1)} %param.36) | copy-start | bytes 1572868
  7.2 399.0 %all-gather.12.cloned.1.call-start = ((), (), s32[]{:S(2)}) async-start(), calls=%async_computation | async-start | bytes 1572864 | tf_op jit(solution)/shard_map/all_gather | solution.py:34
  14.2 21.8 %copy-start.16 = (s32[1024]{0:T(1024)S(1)}, s32[1024]{0:T(1024)}, u32[]{:S(2)}) copy-start(s32[1024]{0:T(1024)} %param.29) | copy-start | bytes 12292
  14.2 21.9 %copy-start.31 = (s32[128]{0:T(128)S(1)}, s32[128]{0:T(128)}, u32[]{:S(2)}) copy-start(s32[128]{0:T(128)} %param.31) | copy-start | bytes 1540
  14.2 22.0 %copy-start.2 = (bf16[1024,512]{1,0:T(8,128)(2,1)S(1)}, bf16[1024,512]{1,0:T(8,128)(2,1)}, u32[]{:S(2)}) copy-start(bf16[1024,512]{1,0:T(8,128)(2,1)} %param.25) | copy-start | bytes 3145732
  14.2 22.0 %copy-start.34 = (bf16[128,512]{1,0:T(8,128)(2,1)S(1)}, bf16[128,512]{1,0:T(8,128)(2,1)}, u32[]{:S(2)}) copy-start(bf16[128,512]{1,0:T(8,128)(2,1)} %param.30) | copy-start | bytes 393220
  14.5 22.0 %copy-start.20 = (bf16[16,512]{1,0:T(8,128)(2,1)S(1)}, bf16[16,512]{1,0:T(8,128)(2,1)}, u32[]{:S(2)}) copy-start(bf16[16,512]{1,0:T(8,128)(2,1)} %param.32) | copy-start | bytes 49156
  15.4 311.3 %collective-permute-start = (bf16[1,128,512]{2,1,0:T(8,128)(2,1)}, bf16[1,128,512]{2,1,0:T(8,128)(2,1)}, u32[]{:S(2)}, u32[]{:S(2)}) collective-permute-start(bf16[1,128,512]{2,1,0:T(8,128)(2,1)} %get-tuple-element.24), channel_id=1, source_target_pairs={{0,16},{16,32},{32,48},{48,64},{64,80},{80,96},{96,112},{112,128},... | collective-permute-start | bytes 393224 | tf_op jit(solution)/shard_map/ppermute | solution.py:16
  25.6 303.4 %collective-permute-start.1 = (bf16[1,128,512]{2,1,0:T(8,128)(2,1)}, bf16[1,128,512]{2,1,0:T(8,128)(2,1)}, u32[]{:S(2)}, u32[]{:S(2)}) collective-permute-start(bf16[1,128,512]{2,1,0:T(8,128)(2,1)} %get-tuple-element.23), channel_id=1, source_target_pairs={{16,0},{32,16},{48,32},{64,48},{80,64},{96,80},{112,96},{128,112},... | collective-permute-start | bytes 393224 | tf_op jit(solution)/shard_map/ppermute | solution.py:19
  27.5 302.4 %collective-permute-start.2 = (bf16[1,128,512]{2,1,0:T(8,128)(2,1)}, bf16[1,128,512]{2,1,0:T(8,128)(2,1)}, u32[]{:S(2)}, u32[]{:S(2)}) collective-permute-start(bf16[1,128,512]{2,1,0:T(8,128)(2,1)} %get-tuple-element.22), channel_id=1, source_target_pairs={{0,4},{4,8},{8,12},{1,5},{5,9},{9,13},{2,6},{6,10},{10,14},{3,7},{... | collective-permute-start | bytes 393224 | tf_op jit(solution)/shard_map/ppermute | solution.py:16
  31.4 299.5 %collective-permute-start.3 = (bf16[1,128,512]{2,1,0:T(8,128)(2,1)}, bf16[1,128,512]{2,1,0:T(8,128)(2,1)}, u32[]{:S(2)}, u32[]{:S(2)}) collective-permute-start(bf16[1,128,512]{2,1,0:T(8,128)(2,1)} %get-tuple-element.21), channel_id=1, source_target_pairs={{4,0},{8,4},{12,8},{5,1},{9,5},{13,9},{6,2},{10,6},{14,10},{7,3},{... | collective-permute-start | bytes 393224 | tf_op jit(solution)/shard_map/ppermute | solution.py:19
  32.6 299.2 %collective-permute-start.4 = (bf16[1,128,512]{2,1,0:T(8,128)(2,1)}, bf16[1,128,512]{2,1,0:T(8,128)(2,1)}, u32[]{:S(2)}, u32[]{:S(2)}) collective-permute-start(bf16[1,128,512]{2,1,0:T(8,128)(2,1)} %get-tuple-element.20), channel_id=1, source_target_pairs={{0,1},{1,2},{2,3},{4,5},{5,6},{6,7},{8,9},{9,10},{10,11},{12,13},{... | collective-permute-start | bytes 393224 | tf_op jit(solution)/shard_map/ppermute | solution.py:16
  78.8 13.2 %copy-start.8 = (bf16[1024,512]{1,0:T(8,128)(2,1)S(1)}, bf16[1024,512]{1,0:T(8,128)(2,1)}, u32[]{:S(2)}) copy-start(bf16[1024,512]{1,0:T(8,128)(2,1)} %param.34) | copy-start | bytes 3145732
  103.7 15.7 %copy-start.11 = (f32[1024,6]{0,1:T(8,128)S(1)}, f32[1024,6]{0,1:T(8,128)}, u32[]{:S(2)}) copy-start(f32[1024,6]{0,1:T(8,128)} %compare_convert_fusion) | copy-start | bytes 73732
  103.7 16.7 %copy-start.10 = (bf16[1024,512]{1,0:T(8,128)(2,1)S(1)}, bf16[1024,512]{1,0:T(8,128)(2,1)}, u32[]{:S(2)}) copy-start(bf16[1024,512]{1,0:T(8,128)(2,1)} %param.38) | copy-start | bytes 3145732
  269.7 56.5 %copy-start.5 = (bf16[1024,512]{1,0:T(8,128)(2,1)S(1)}, bf16[1024,512]{1,0:T(8,128)(2,1)}, u32[]{:S(2)}) copy-start(bf16[1024,512]{1,0:T(8,128)(2,1)} %param.42) | copy-start | bytes 3145732
  269.7 56.7 %copy-start.21 = (s32[1024]{0:T(1024)S(1)}, s32[1024]{0:T(1024)}, u32[]{:S(2)}) copy-start(s32[1024]{0:T(1024)} %reshape.276) | copy-start | bytes 12292
  269.7 56.7 %copy-start.4 = (bf16[1024,512]{1,0:T(8,128)(2,1)S(1)}, bf16[1024,512]{1,0:T(8,128)(2,1)}, u32[]{:S(2)}) copy-start(bf16[1024,512]{1,0:T(8,128)(2,1)} %param.46) | copy-start | bytes 3145732
  303.5 23.0 %copy-start.33 = (s32[128]{0:T(128)S(1)}, s32[128]{0:T(128)}, u32[]{:S(2)}) copy-start(s32[128]{0:T(128)} %compare_select_fusion.7) | copy-start | bytes 1540
  326.7 6.1 %collective-permute-start.5 = (bf16[1,128,512]{2,1,0:T(8,128)(2,1)S(1)}, bf16[1,128,512]{2,1,0:T(8,128)(2,1)S(1)}, u32[]{:S(2)}, u32[]{:S(2)}) collective-permute-start(bf16[1,128,512]{2,1,0:T(8,128)(2,1)S(1)} %get-tuple-element.19), channel_id=1, source_target_pairs={{1,0},{2,1},{3,2},{5,4},{6,5},{7,6},{9,8},{10,9},{11,10},{13,12},{... | collective-permute-start | bytes 393224 | tf_op jit(solution)/shard_map/ppermute | solution.py:19
  333.9 25.8 %copy-start.15 = (pred[6144]{0:T(1024)(128)(4,1)S(1)}, pred[6144]{0:T(1024)(128)(4,1)}, u32[]{:S(2)}) copy-start(pred[6144]{0:T(1024)(128)(4,1)} %compare_and_fusion) | copy-start | bytes 18436
  334.0 25.7 %copy-start.23 = (f32[512]{0:T(512)S(1)}, f32[512]{0:T(512)}, u32[]{:S(2)}) copy-start(f32[512]{0:T(512)} %param.35) | copy-start | bytes 6148
  376.9 15.1 %copy-start.3 = (f32[1024,6]{1,0:T(8,128)S(1)}, f32[1024,6]{1,0:T(8,128)}, u32[]{:S(2)}) copy-start(f32[1024,6]{1,0:T(8,128)} %copy.66) | copy-start | bytes 73732
  408.9 54.2 %copy-start.19 = (s32[1024]{0:T(1024)S(1)}, s32[1024]{0:T(1024)}, u32[]{:S(2)}) copy-start(s32[1024]{0:T(1024)} %get-tuple-element.38) | copy-start | bytes 12292
  (19 other events, 84.9 us)
Sparse Core Ops, SparseCore 0:
  78.9 41.8 all-gather.11
where the time goes:
time: 509 us; the launch traced here: 499 us
  blocking collectives  238 us (47%)
  local copies, waits for them, and re-layouts  167 us (33%)
  other arithmetic  33.9 us (7%)
  matrix products  23.5 us (5%)
  starting transfers between devices  22 us (4%)
  between operations  14.6 us (3%)
    all_gather x24, blocking collectives, stacked_from(): parts = lax.all_gather(parts, axes[k], axis=0, tiled=True)  238 us
    concatenate x1, local copies, waits for them, and re-layouts, gather_at_once(): return joined_along(jnp.concatenate(finished, axis=widest + 1), dim)  54.2 us
    gather x1, local copies, waits for them, and re-layouts, local(): jnp.take(sender, fine_nbrs.reshape(-1), axis=0)  25.7 us
    add x2, local copies, waits for them, and re-layouts, edge_messages(): sender_rows.astype(jnp.float32).reshape(-1, slot_count, features)  25.3 us
    ppermute x3, starting transfers between devices, extended(): lax.ppermute(lax.slice_in_dim(block, block.shape[dim] - width, None, axis...  17.4 us
    reshape x1, local copies, waits for them, and re-layouts, local(): messages.reshape(own_rows, slot_count, features) * live_slots[:, :, None]  15.1 us
    reduce_sum x1, other arithmetic, local(): jnp.sum(messages.reshape(own_rows, slot_count, features) * live_slots[:,...  10.4 us
    dot_general x2, matrix products, edge_messages(): jnp.dot(hidden, out_weight, preferred_element_type=jnp.float32)  10.3 us
  transfers between devices with their start and end apart: 7, of which 0 were waited for; matrix products, arithmetic and copies ran while one was open for 26% of the time, Pallas kernels for 0%

commit v1 on v0

v1 whole, which is shorter than its diff:
```python
import functools
import itertools

import jax
import jax.numpy as jnp
from jax import lax
from jax.experimental import pallas as pl
from jax.experimental.pallas import tpu as pltpu
from jax.sharding import Mesh
from jax.sharding import PartitionSpec as P

AXES = ("x", "zh", "c", "y", "z")
SIZES = (4, 2, 2, 4, 4)
EPS = 1e-05
F32 = jnp.float32
BF16 = jnp.bfloat16
D = 512
CHUNKS = 4
BLOCK = 128


def linear(place):
    number = 0
    for size, at in zip(SIZES, place):
        number = number * size + at
    return number


def permutation(move):
    pairs = []
    for place in itertools.product(*(range(size) for size in SIZES)):
        target = move(*place)
        if target is not None:
            pairs.append((linear(place), linear(target)))
    return pairs


def along_z(x, zh, c, y, z, step):
    at = (zh * 4 + z + step) % 8
    return (x, at // 4, c, y, at % 4)


def along_plane(x, zh, c, y, z, step, first):
    if (c == 0) == first:
        return ((x + step) % 4, zh, c, y, z)
    return (x, zh, c, (y + step) % 4, z)


SWAP = permutation(lambda x, zh, c, y, z: (x, zh, 1 - c, y, z))
RING = permutation(lambda x, zh, c, y, z: along_z(x, zh, c, y, z, 1 if c == 0 else -1))
RING_END = permutation(lambda x, zh, c, y, z: along_z(x, zh, c, y, z, -1) if c == 1 else None)
UP_FIRST = permutation(functools.partial(along_plane, step=1, first=True))
DOWN_FIRST = permutation(functools.partial(along_plane, step=-1, first=True))
UP_SECOND = permutation(functools.partial(along_plane, step=1, first=False))
DOWN_SECOND = permutation(functools.partial(along_plane, step=-1, first=False))


def dot(a, b):
    return lax.dot_general(a, b, (((1,), (0,)), ((), ())), preferred_element_type=F32)


def dot_t(a, b):
    return lax.dot_general(a, b, (((0,), (0,)), ((), ())), preferred_element_type=F32)


def normed(values):
    center = values - jnp.mean(values, axis=-1, keepdims=True)
    spread = jnp.mean(center * center, axis=-1, keepdims=True)
    return center * lax.rsqrt(spread + EPS)


def pool_kernel(
    fine, parent, medium, medium_parent, coarse, nbrs, weight,
    sender_out, pool_out, medium_out, slots_out, comp_out, member_out,
):
    member = (parent[...] == lax.broadcasted_iota(jnp.int32, (128, 1024), 0)).astype(F32)
    count = jnp.sum(member, axis=1, keepdims=True)
    member = member.astype(BF16)
    medium_pool = medium[...].astype(F32) + dot(member, fine[...]) / count
    medium_out[...] = medium_pool
    upper = (medium_parent[...] == lax.broadcasted_iota(jnp.int32, (16, 128), 0)).astype(F32)
    upper_count = jnp.sum(upper, axis=1, keepdims=True)
    total = jnp.dot(upper, medium_pool, precision=lax.Precision.HIGHEST, preferred_element_type=F32)
    pool = (coarse[...].astype(F32) + total / upper_count).astype(BF16)
    pool_out[...] = pool
    sender_out[...] = dot(pool, weight[...]).astype(BF16)
    upper = upper.astype(BF16)
    member_out[...] = jnp.concatenate([upper, upper], axis=0)
    comp = dot(upper, member).astype(BF16)
    comp_out[...] = jnp.concatenate([comp, comp], axis=0)
    here = {name: lax.axis_index(name) for name in AXES}
    row = nbrs[...] & 15
    owner = nbrs[...] >> 4
    z = owner & 3
    y = (owner >> 2) & 3
    c = (owner >> 4) & 1
    zh = (owner >> 5) & 1
    x = owner >> 6
    back = (here["zh"] * 4 + here["z"] - zh * 4 - z) & 7
    stream = (back > 3).astype(jnp.int32)
    at = jnp.where(stream == 0, back, 7 - back) * 32 + c * 16 + row
    step_x = (here["x"] - x) & 3
    step_y = (here["y"] - y) & 3
    order_x = jnp.where(step_x == 2, 3, jnp.where(step_x == 3, 2, step_x))
    order_y = jnp.where(step_y == 2, 3, jnp.where(step_y == 3, 2, step_y))
    at = at + jnp.where(stream == 0, order_x * 128 + order_y * 512, order_y * 128 + order_x * 512)
    slots_out[...] = at + jnp.where(stream == here["c"], 0, 2048)


def face_kernel(fine, rows, counts, weight, edge_out, sender_out, faces_out, centred_out):
    sender = dot(fine[...], weight[...]).astype(BF16)
    sender_out[...] = sender
    wide = edge_out[...].astype(F32)
    centred_out[...] = (wide - jnp.mean(wide, axis=1, keepdims=True)).astype(BF16)
    flat = jnp.concatenate([rows[0], jnp.zeros((2, 128), jnp.int32)], axis=0)
    columns = flat.T
    place = lax.broadcasted_iota(jnp.int32, (128, 1), 0)
    for face in range(6):
        wanted = jnp.where(place < counts[0, face], columns[:, face : face + 1], -1)
        picked = (wanted == lax.broadcasted_iota(jnp.int32, (128, 1024), 1)).astype(F32).astype(BF16)
        faces_out[face] = dot(picked, sender).astype(BF16)


def edge_kernel(
    sender, g0, g1, g2, g3, g4, g5, fine, nbrs, receive, bias, centred, gain,
    node_in, node_bias, node_out, node_gain,
    new_out,
    table, centred_v, node_in_v, node_out_v, sems,
):
    copies = [pltpu.make_async_copy(sender, table.at[pl.ds(0, 1024)], sems.at[0])]
    for k, ghost in enumerate((g0, g1, g2, g3, g4, g5)):
        copies.append(pltpu.make_async_copy(ghost.at[0], table.at[pl.ds(1024 + 128 * k, 128)], sems.at[1 + k]))
    copies.append(pltpu.make_async_copy(centred, centred_v, sems.at[7]))
    copies.append(pltpu.make_async_copy(node_in, node_in_v, sems.at[8]))
    copies.append(pltpu.make_async_copy(node_out, node_out_v, sems.at[9]))
    for copy in copies:
        copy.start()
    for copy in copies:
        copy.wait()
    rows = new_out.shape[0]

    def step(block, carry):
        span = pl.ds(pl.multiple_of(block * BLOCK, BLOCK), BLOCK)
        own = fine[span, :]
        near = nbrs[span, :]
        received = dot(own, receive[...]) + bias[...]
        total = jnp.zeros((BLOCK, D), F32)
        for k in range(6):
            wanted = near[:, k : k + 1]
            picked = (wanted == lax.broadcasted_iota(jnp.int32, (BLOCK, 1792), 1)).astype(F32).astype(BF16)
            found = dot(picked, table[...]).astype(BF16).astype(F32)
            hidden = jnp.maximum(found + received, 0.0).astype(BF16)
            out = dot(hidden, centred_v[...])
            spread = jnp.mean(out * out, axis=-1, keepdims=True)
            scale = lax.rsqrt(spread + EPS) * (wanted < 1792).astype(F32)
            total = total + out * scale
        incoming = (total * gain[...]).astype(BF16)
        both = jnp.concatenate([own, incoming], axis=1)
        hidden = jnp.maximum(dot(both, node_in_v[...]) + node_bias[...], 0.0).astype(BF16)
        new_out[span, :] = own.astype(F32) + normed(dot(hidden, node_out_v[...])) * node_gain[...]
        return carry

    lax.fori_loop(0, rows // BLOCK, step, 0)


def coarse_kernel(
    mine, other, slots, pool, medium, comp, member, n0, n1, n2, n3,
    edge_in, edge_bias, edge_out, edge_gain, node_in, node_bias, node_out, node_gain,
    fine_out, medium_out, coarse_out,
):
    pool_rows = pool[...]
    received = dot(pool_rows, edge_in[...]) + edge_bias[...]
    places = slots[...]
    column = jnp.concatenate([jnp.broadcast_to(places[:, k : k + 1], (16, 128)) for k in range(64)], axis=0)
    total = jnp.zeros((1024, D), F32)
    lane = lax.broadcasted_iota(jnp.int32, (1024, 128), 1)
    for piece in range(8):
        source = mine if piece < 4 else other
        picked = jnp.concatenate(
            [(column == lane + (piece * 512 + t * 128)).astype(F32).astype(BF16) for t in range(4)], axis=1
        )
        total = total + dot(picked, source[(piece % 4) * 512 : (piece % 4 + 1) * 512, :])
    hidden = jnp.maximum(total.reshape(64, 16, D) + received[None], 0.0).astype(BF16).reshape(1024, D)
    message = normed(dot(hidden, edge_out[...])) * edge_gain[...]
    incoming = jnp.sum(message.reshape(64, 16, D), axis=0).astype(BF16)
    both = jnp.concatenate([pool_rows, incoming], axis=1)
    hidden = jnp.maximum(dot(both, node_in[...]) + node_bias[...], 0.0).astype(BF16)
    delta = normed(dot(hidden, node_out[...])) * node_gain[...]
    coarse_out[...] = (pool_rows.astype(F32) + delta).astype(BF16)
    high = delta.astype(BF16)
    low = (delta - high.astype(F32)).astype(BF16)
    parts = jnp.concatenate([high, low], axis=0)
    medium_out[...] = (medium[...] + dot_t(member[...], parts)).astype(BF16)
    spread = dot_t(comp[...], parts)
    for k, new in enumerate((n0, n1, n2, n3)):
        fine_out[k * 256 : (k + 1) * 256, :] = (new[...] + spread[k * 256 : (k + 1) * 256]).astype(BF16)


def joined(*parts):
    return jnp.concatenate(parts, axis=0)


def sent(rows, pairs):
    return lax.ppermute(rows, AXES, pairs)


def local(
    fine_state, fine_nbrs, send_rows, ghost_counts, fine_parent, medium_state, medium_parent, coarse_state,
    coarse_nbrs, fine_edge_in, fine_edge_bias, fine_edge_out, fine_edge_gain, fine_node_in, fine_node_bias,
    fine_node_out, fine_node_gain, coarse_edge_in, coarse_edge_bias, coarse_edge_out, coarse_edge_gain,
    coarse_node_in, coarse_node_bias, coarse_node_out, coarse_node_gain,
):
    vmem, smem, anywhere = pltpu.VMEM, pltpu.SMEM, pl.ANY
    row = lambda vector: vector.reshape(1, -1)
    lower = pl.BlockSpec((D, D), lambda i: (0, 0), memory_space=vmem)

    sender, pool, medium_pool, slots, comp, member = pl.pallas_call(
        pool_kernel,
        grid=(1,),
        out_shape=[
            jax.ShapeDtypeStruct((16, D), BF16),
            jax.ShapeDtypeStruct((16, D), BF16),
            jax.ShapeDtypeStruct((128, D), F32),
            jax.ShapeDtypeStruct((16, 64), jnp.int32),
            jax.ShapeDtypeStruct((32, 1024), BF16),
            jax.ShapeDtypeStruct((32, 128), BF16),
        ],
        in_specs=[pl.BlockSpec(memory_space=vmem)] * 6 + [lower],
        out_specs=[pl.BlockSpec(memory_space=vmem)] * 6,
        compiler_params=pltpu.CompilerParams(vmem_limit_bytes=32 << 20),
    )(fine_state, row(fine_parent), medium_state, row(medium_parent), coarse_state, coarse_nbrs, coarse_edge_in)

    fine_sender, faces, centred = pl.pallas_call(
        face_kernel,
        grid=(1,),
        out_shape=[
            jax.ShapeDtypeStruct((1024, D), BF16),
            jax.ShapeDtypeStruct((6, 128, D), BF16),
            jax.ShapeDtypeStruct((D, D), BF16),
        ],
        in_specs=[
            pl.BlockSpec(memory_space=vmem),
            pl.BlockSpec(memory_space=vmem),
            pl.BlockSpec(memory_space=smem),
            lower,
            pl.BlockSpec(memory_space=vmem),
        ],
        out_specs=[pl.BlockSpec(memory_space=vmem)] * 3,
        compiler_params=pltpu.CompilerParams(vmem_limit_bytes=32 << 20),
    )(fine_state, send_rows, ghost_counts, fine_edge_in, fine_edge_out)

    ghosts = []
    for face, axes in ((0, ("x", "zh", "c")), (2, "y"), (4, "z")):
        count = lax.axis_size(axes)
        forward = [(k, k + 1) for k in range(count - 1)]
        backward = [(k + 1, k) for k in range(count - 1)]
        ghosts.append(lax.ppermute(faces[face + 1 : face + 2], axes, forward))
        ghosts.append(lax.ppermute(faces[face : face + 1], axes, backward))

    core = lax.axis_index("c")
    beside = sent(sender, SWAP)
    chip = jnp.where(core == 0, joined(sender, beside), joined(beside, sender))
    ring = [chip]
    for _ in range(3):
        ring.append(sent(ring[-1], RING))
    last = sent(ring[-1], RING_END)
    column = jnp.where(core == 0, joined(*ring), joined(*ring[1:], last))
    up, down = sent(column, UP_FIRST), sent(column, DOWN_FIRST)
    line = joined(column, up, down, sent(up[:64], UP_FIRST), sent(down[64:], DOWN_FIRST))
    up, down = sent(line, UP_SECOND), sent(line, DOWN_SECOND)
    mine = joined(line, up, down, sent(up[:256], UP_SECOND), sent(down[256:], DOWN_SECOND))
    other = sent(mine, SWAP)

    news = []
    span = 1024 // CHUNKS
    for chunk in range(CHUNKS):
        part = pl.BlockSpec((span, D), lambda i, chunk=chunk: (chunk, 0), memory_space=vmem)
        near = pl.BlockSpec((span, 6), lambda i, chunk=chunk: (chunk, 0), memory_space=vmem)
        whole = pl.BlockSpec(memory_space=vmem)
        left = pl.BlockSpec(memory_space=anywhere)
        news.append(
            pl.pallas_call(
                edge_kernel,
                grid=(1,),
                out_shape=jax.ShapeDtypeStruct((span, D), F32),
                in_specs=[left] * 7
                + [part, near, pl.BlockSpec((D, D), lambda i: (1, 0), memory_space=vmem), whole, left, whole, left, whole, left, whole],
                out_specs=whole,
                scratch_shapes=[
                    pltpu.VMEM((1792, D), BF16),
                    pltpu.VMEM((D, D), BF16),
                    pltpu.VMEM((2 * D, D), BF16),
                    pltpu.VMEM((D, D), BF16),
                    pltpu.SemaphoreType.DMA((10,)),
                ],
                compiler_params=pltpu.CompilerParams(vmem_limit_bytes=32 << 20),
                cost_estimate=pl.CostEstimate(flops=3_500_000_000, bytes_accessed=5_000_000, transcendentals=0),
            )(
                fine_sender, *ghosts, fine_state, fine_nbrs, fine_edge_in, row(fine_edge_bias), centred,
                row(fine_edge_gain), fine_node_in, row(fine_node_bias), fine_node_out, row(fine_node_gain),
            )
        )

    whole = pl.BlockSpec(memory_space=vmem)
    fine_out, medium_out, coarse_out = pl.pallas_call(
        coarse_kernel,
        grid=(1,),
        out_shape=[
            jax.ShapeDtypeStruct((1024, D), BF16),
            jax.ShapeDtypeStruct((128, D), BF16),
            jax.ShapeDtypeStruct((16, D), BF16),
        ],
        in_specs=[whole] * 11 + [pl.BlockSpec((D, D), lambda i: (1, 0), memory_space=vmem)] + [whole] * 7,
        out_specs=[whole] * 3,
        compiler_params=pltpu.CompilerParams(vmem_limit_bytes=48 << 20),
    )(
        mine, other, slots, pool, medium_pool, comp, member, *news, coarse_edge_in, row(coarse_edge_bias),
        coarse_edge_out, row(coarse_edge_gain), coarse_node_in, row(coarse_node_bias), coarse_node_out,
        row(coarse_node_gain),
    )
    return fine_out, medium_out, coarse_out


def solution(mesh):
    torus = Mesh(mesh.devices.reshape(SIZES), AXES)
    rows = P(AXES, None)
    placed = (rows, rows, P(AXES, None, None), rows, P(AXES), rows, P(AXES), rows, rows) + (P(),) * 16
    return jax.shard_map(local, mesh=torus, in_specs=placed, out_specs=(rows, rows, rows), check_vma=False)
```

time: 509 us -> 147 us (0.29)
  the two profiles are of different devices: /device:TPU:1 before, /device:TPU:2 now
where the time goes in v1:
time: 147 us; the launch traced here: 146 us
  Pallas kernels  46.3 us (31%)
  waiting for transfers between devices  42.3 us (29%)
  starting transfers between devices  36.2 us (25%)
  local copies, waits for them, and re-layouts  20.4 us (14%)
    pallas_call x4, Pallas kernels, local(): pl.pallas_call(edge_kernel, grid=(1,), out_shape=jax.ShapeDtypeStruct((sp...  33.8 us
    ppermute x14, waiting for transfers between devices, sent(): return lax.ppermute(rows, AXES, pairs)  33 us
    unnamed x79, local copies, waits for them, and re-layouts  18.1 us
    ppermute x14, starting transfers between devices, sent(): return lax.ppermute(rows, AXES, pairs)  13.2 us
    ppermute x3, starting transfers between devices, local(): ghosts.append(lax.ppermute(faces[face + 1:face + 2], axes, forward))  11.9 us
    ppermute x3, starting transfers between devices, local(): ghosts.append(lax.ppermute(faces[face:face + 1], axes, backward))  11.1 us
    pallas_call x1, Pallas kernels, local(): pl.pallas_call(coarse_kernel, grid=(1,), out_shape=[jax.ShapeDtypeStruct(...  9.58 us
    ppermute x3, waiting for transfers between devices, local(): ghosts.append(lax.ppermute(faces[face + 1:face + 2], axes, forward))  6.95 us
  transfers between devices with their start and end apart: 20, of which 11 were waited for; matrix products, arithmetic and copies ran while one was open for 4% of the time, Pallas kernels for 25%

profile of v1, /device:TPU:2, one launch (start us, length us, event | category | flops | bytes accessed | tf_op | source)
XLA Modules:
  0.0 146.3 jit_solution(14883392121625081808)
XLA Ops:
  8.8 2.0 %collective-permute-start.1 = (bf16[32,512]{1,0:T(8,128)(2,1)S(1)}, bf16[32,512]{1,0:T(8,128)(2,1)S(1)}, u32[]{:S(2)}, u32[]{:S(2)}) collective-permute-start(bf16[32,512]{1,0:T(8,128)(2,1)S(1)} %maximum_select_fusion.1), channel_id=1, source_target_pairs={{0,1},{1,2},{2,3},{3,32},{4,5},{5,6},{6,7},{7,36},{8,9},{9,10},{10... | collective-permute-start | bytes 98312 | tf_op jit(solution)/shard_map/ppermute | solution.py:204
  10.8 5.8 %collective-permute-done.1 = bf16[32,512]{1,0:T(8,128)(2,1)S(1)} collective-permute-done((bf16[32,512]{1,0:T(8,128)(2,1)S(1)}, bf16[32,512]{1,0:T(8,128)(2,1)S(1)}, u32[]{:S(2)}, u32[]{:S(2)}) %collective-permute-start.1) | collective-permute-done | bytes 32800 | tf_op jit(solution)/shard_map/ppermute | solution.py:204
  16.6 5.1 %collective-permute-done.2 = bf16[32,512]{1,0:T(8,128)(2,1)S(1)} collective-permute-done((bf16[32,512]{1,0:T(8,128)(2,1)S(1)}, bf16[32,512]{1,0:T(8,128)(2,1)S(1)}, u32[]{:S(2)}, u32[]{:S(2)}) %collective-permute-start.2) | collective-permute-done | bytes 32800 | tf_op jit(solution)/shard_map/ppermute | solution.py:204
  21.7 5.1 %collective-permute-done.3 = bf16[32,512]{1,0:T(8,128)(2,1)S(1)} collective-permute-done((bf16[32,512]{1,0:T(8,128)(2,1)S(1)}, bf16[32,512]{1,0:T(8,128)(2,1)S(1)}, u32[]{:S(2)}, u32[]{:S(2)}) %collective-permute-start.3) | collective-permute-done | bytes 32800 | tf_op jit(solution)/shard_map/ppermute | solution.py:204
  28.2 1.5 %collective-permute-start.5 = (bf16[128,512]{1,0:T(8,128)(2,1)S(1)}, bf16[128,512]{1,0:T(8,128)(2,1)S(1)}, u32[]{:S(2)}, u32[]{:S(2)}) collective-permute-start(bf16[128,512]{1,0:T(8,128)(2,1)S(1)} %get-tuple-element.22), channel_id=1, source_target_pairs={{0,64},{1,65},{2,66},{3,67},{4,68},{5,69},{6,70},{7,71},{8,72},{9,... | collective-permute-start | bytes 393224 | tf_op jit(solution)/shard_map/ppermute | solution.py:204
  30.3 2.3 %collective-permute-done.6 = bf16[128,512]{1,0:T(8,128)(2,1)S(1)} collective-permute-done((bf16[128,512]{1,0:T(8,128)(2,1)S(1)}, bf16[128,512]{1,0:T(8,128)(2,1)S(1)}, u32[]{:S(2)}, u32[]{:S(2)}) %collective-permute-start.6) | collective-permute-done | bytes 131104 | tf_op jit(solution)/shard_map/ppermute | solution.py:204
  36.1 3.4 %collective-permute-done.7 = bf16[64,512]{1,0:T(8,128)(2,1)S(1)} collective-permute-done((bf16[64,512]{1,0:T(8,128)(2,1)S(1)}, bf16[64,512]{1,0:T(8,128)(2,1)S(1)}, u32[]{:S(2)}, u32[]{:S(2)}) %collective-permute-start.7) | collective-permute-done | bytes 65568 | tf_op jit(solution)/shard_map/ppermute | solution.py:204
  40.7 1.6 %collective-permute-start.9 = (bf16[512,512]{1,0:T(8,128)(2,1)S(1)}, bf16[512,512]{1,0:T(8,128)(2,1)S(1)}, u32[]{:S(2)}, u32[]{:S(2)}) collective-permute-start(bf16[512,512]{1,0:T(8,128)(2,1)S(1)} %get-tuple-element.33), channel_id=1, source_target_pairs={{0,4},{1,5},{2,6},{3,7},{4,8},{5,9},{6,10},{7,11},{8,12},{9,13},{1... | collective-permute-start | bytes 1572872 | tf_op jit(solution)/shard_map/ppermute | solution.py:204
  42.4 1.7 %collective-permute-start.10 = (bf16[512,512]{1,0:T(8,128)(2,1)S(1)}, bf16[512,512]{1,0:T(8,128)(2,1)S(1)}, u32[]{:S(2)}, u32[]{:S(2)}) collective-permute-start(bf16[512,512]{1,0:T(8,128)(2,1)S(1)} %get-tuple-element.33), channel_id=1, source_target_pairs={{0,12},{1,13},{2,14},{3,15},{4,0},{5,1},{6,2},{7,3},{8,4},{9,5},{1... | collective-permute-start | bytes 1572872 | tf_op jit(solution)/shard_map/ppermute | solution.py:204
  44.1 7.2 %collective-permute-done.9 = bf16[512,512]{1,0:T(8,128)(2,1)S(1)} collective-permute-done((bf16[512,512]{1,0:T(8,128)(2,1)S(1)}, bf16[512,512]{1,0:T(8,128)(2,1)S(1)}, u32[]{:S(2)}, u32[]{:S(2)}) %collective-permute-start.9) | collective-permute-done | bytes 524320 | tf_op jit(solution)/shard_map/ppermute | solution.py:204
  51.7 3.0 %collective-permute-start.12 = (bf16[256,512]{1,0:T(8,128)(2,1)S(1)}, bf16[256,512]{1,0:T(8,128)(2,1)S(1)}, u32[]{:S(2)}, u32[]{:S(2)}) collective-permute-start(bf16[256,512]{1,0:T(8,128)(2,1)S(1)} %slice.43), channel_id=1, source_target_pairs={{0,12},{1,13},{2,14},{3,15},{4,0},{5,1},{6,2},{7,3},{8,4},{9,5},{1... | collective-permute-start | bytes 786440 | tf_op jit(solution)/shard_map/ppermute | solution.py:204
  56.3 2.6 %collective-permute-done.11 = bf16[256,512]{1,0:T(8,128)(2,1)S(1)} collective-permute-done((bf16[256,512]{1,0:T(8,128)(2,1)S(1)}, bf16[256,512]{1,0:T(8,128)(2,1)S(1)}, u32[]{:S(2)}, u32[]{:S(2)}) %collective-permute-start.11) | collective-permute-done | bytes 262176 | tf_op jit(solution)/shard_map/ppermute | solution.py:204
  60.5 2.2 %shard_map.257 = (bf16[1024,512]{1,0:T(8,128)(2,1)S(1)}, bf16[6,128,512]{2,1,0:T(8,128)(2,1)S(1)}, bf16[512,512]{1,0:T(8,128)(2,1)S(1)}) custom-call(bf16[1024,512]{1,0:T(8,128)(2,1)S(1)} %copy-done.1, s32[1,6,128]{2,1,0:T(8,128)S(1)} %copy.28.rows, s32[1,6]{1,0:T(1,128)S(1)} %copy-done.18, bf16[1024,512]{1,0:T(8,128)(2,1)S(1)} %copy-done.4, ...), custom_call_target="tpu_custom_call" | custom-call | tf_op jit(solution)/shard_map/pallas_call | solution.py:233
  64.9 4.7 %collective-permute-start.18 = (bf16[1,128,512]{2,1,0:T(8,128)(2,1)S(1)}, bf16[1,128,512]{2,1,0:T(8,128)(2,1)S(1)}, u32[]{:S(2)}, u32[]{:S(2)}) collective-permute-start(bf16[1,128,512]{2,1,0:T(8,128)(2,1)S(1)} %get-tuple-element.24), channel_id=1, source_target_pairs={{0,1},{1,2},{2,3},{4,5},{5,6},{6,7},{8,9},{9,10},{10,11},{12,13},{... | collective-permute-start | bytes 393224 | tf_op jit(solution)/shard_map/ppermute | solution.py:257
  71.0 5.2 %collective-permute-start.16 = (bf16[1,128,512]{2,1,0:T(8,128)(2,1)}, bf16[1,128,512]{2,1,0:T(8,128)(2,1)}, u32[]{:S(2)}, u32[]{:S(2)}) collective-permute-start(bf16[1,128,512]{2,1,0:T(8,128)(2,1)} %get-tuple-element.26), channel_id=1, source_target_pairs={{0,4},{4,8},{8,12},{1,5},{5,9},{9,13},{2,6},{6,10},{10,14},{3,7},{... | collective-permute-start | bytes 393224 | tf_op jit(solution)/shard_map/ppermute | solution.py:257
  76.8 8.5 %collective-permute-start.15 = (bf16[1,128,512]{2,1,0:T(8,128)(2,1)}, bf16[1,128,512]{2,1,0:T(8,128)(2,1)}, u32[]{:S(2)}, u32[]{:S(2)}) collective-permute-start(bf16[1,128,512]{2,1,0:T(8,128)(2,1)} %get-tuple-element.27), channel_id=1, source_target_pairs={{16,0},{32,16},{48,32},{64,48},{80,64},{96,80},{112,96},{128,112},... | collective-permute-start | bytes 393224 | tf_op jit(solution)/shard_map/ppermute | solution.py:258
  86.0 1.9 %collective-permute-start.14 = (bf16[1,128,512]{2,1,0:T(8,128)(2,1)}, bf16[1,128,512]{2,1,0:T(8,128)(2,1)}, u32[]{:S(2)}, u32[]{:S(2)}) collective-permute-start(bf16[1,128,512]{2,1,0:T(8,128)(2,1)} %get-tuple-element.28), channel_id=1, source_target_pairs={{0,16},{16,32},{32,48},{48,64},{64,80},{80,96},{96,112},{112,128},... | collective-permute-start | bytes 393224 | tf_op jit(solution)/shard_map/ppermute | solution.py:257
  88.2 2.3 %collective-permute-done.15.g1 = bf16[1,128,512]{2,1,0:T(8,128)(2,1)} collective-permute-done((bf16[1,128,512]{2,1,0:T(8,128)(2,1)}, bf16[1,128,512]{2,1,0:T(8,128)(2,1)}, u32[]{:S(2)}, u32[]{:S(2)}) %collective-permute-start.15) | collective-permute-done | bytes 131104 | tf_op jit(solution)/shard_map/ppermute | solution.py:258
  90.5 6.9 %collective-permute-done.14.g0 = bf16[1,128,512]{2,1,0:T(8,128)(2,1)} collective-permute-done((bf16[1,128,512]{2,1,0:T(8,128)(2,1)}, bf16[1,128,512]{2,1,0:T(8,128)(2,1)}, u32[]{:S(2)}, u32[]{:S(2)}) %collective-permute-start.14) | collective-permute-done | bytes 131104 | tf_op jit(solution)/shard_map/ppermute | solution.py:257
  102.8 8.3 %shard_map.261.n3 = f32[256,512]{1,0:T(8,128)S(1)} custom-call(bf16[1024,512]{1,0:T(8,128)(2,1)S(1)} %copy-done.21, bf16[1,128,512]{2,1,0:T(8,128)(2,1)} %collective-permute-done.14.g0, bf16[1,128,512]{2,1,0:T(8,128)(2,1)} %collective-permute-done.15.g1, bf16[1,128,512]{2,1,0:T(8,128)(2,1)} %collective-permute-done.16.g2, ...), custom_call_target="tpu_custom_call" | custom-call | flops 3500000000 | bytes 5000000 | tf_op jit(solution)/shard_map/pallas_call | solution.py:282
  111.1 8.3 %shard_map.260.n2 = f32[256,512]{1,0:T(8,128)S(1)} custom-call(bf16[1024,512]{1,0:T(8,128)(2,1)S(1)} %copy-done.21, bf16[1,128,512]{2,1,0:T(8,128)(2,1)} %collective-permute-done.14.g0, bf16[1,128,512]{2,1,0:T(8,128)(2,1)} %collective-permute-done.15.g1, bf16[1,128,512]{2,1,0:T(8,128)(2,1)} %collective-permute-done.16.g2, ...), custom_call_target="tpu_custom_call" | custom-call | flops 3500000000 | bytes 5000000 | tf_op jit(solution)/shard_map/pallas_call | solution.py:282
  119.5 8.3 %shard_map.259.n1 = f32[256,512]{1,0:T(8,128)S(1)} custom-call(bf16[1024,512]{1,0:T(8,128)(2,1)S(1)} %copy-done.21, bf16[1,128,512]{2,1,0:T(8,128)(2,1)} %collective-permute-done.14.g0, bf16[1,128,512]{2,1,0:T(8,128)(2,1)} %collective-permute-done.15.g1, bf16[1,128,512]{2,1,0:T(8,128)(2,1)} %collective-permute-done.16.g2, ...), custom_call_target="tpu_custom_call" | custom-call | flops 3500000000 | bytes 5000000 | tf_op jit(solution)/shard_map/pallas_call | solution.py:282
  127.9 8.7 %shard_map.258.n0 = f32[256,512]{1,0:T(8,128)S(1)} custom-call(bf16[1024,512]{1,0:T(8,128)(2,1)S(1)} %copy-done.21, bf16[1,128,512]{2,1,0:T(8,128)(2,1)} %collective-permute-done.14.g0, bf16[1,128,512]{2,1,0:T(8,128)(2,1)} %collective-permute-done.15.g1, bf16[1,128,512]{2,1,0:T(8,128)(2,1)} %collective-permute-done.16.g2, ...), custom_call_target="tpu_custom_call" | custom-call | flops 3500000000 | bytes 5000000 | tf_op jit(solution)/shard_map/pallas_call | solution.py:282
  136.7 9.6 %shard_map.262 = (bf16[1024,512]{1,0:T(8,128)(2,1)}, bf16[128,512]{1,0:T(8,128)(2,1)}, bf16[16,512]{1,0:T(8,128)(2,1)}) custom-call(bf16[2048,512]{1,0:T(8,128)(2,1)} %constant_dynamic-update-slice_fusion.5.mine, bf16[2048,512]{1,0:T(8,128)(2,1)} %collective-permute-done.13.other, s32[16,64]{1,0:T(8,128)S(1)} %get-tuple-element.13.slots, ...), custom_call_target="tpu_custom_call" | custom-call | tf_op jit(solution)/shard_map/pallas_call | solution.py:305
  (111 shorter events, 28.9 us)
Async XLA Ops:
  7.5 1.3 collective-permute-start
  8.8 7.8 %collective-permute-start.1 = (bf16[32,512]{1,0:T(8,128)(2,1)S(1)}, bf16[32,512]{1,0:T(8,128)(2,1)S(1)}, u32[]{:S(2)}, u32[]{:S(2)}) collective-permute-start(bf16[32,512]{1,0:T(8,128)(2,1)S(1)} %maximum_select_fusion.1), channel_id=1, source_target_pairs={{0,1},{1,2},{2,3},{3,32},{4,5},{5,6},{6,7},{7,36},{8,9},{9,10},{10... | collective-permute-start | bytes 98312 | tf_op jit(solution)/shard_map/ppermute | solution.py:204
  16.6 5.1 %collective-permute-start.2 = (bf16[32,512]{1,0:T(8,128)(2,1)S(1)}, bf16[32,512]{1,0:T(8,128)(2,1)S(1)}, u32[]{:S(2)}, u32[]{:S(2)}) collective-permute-start(bf16[32,512]{1,0:T(8,128)(2,1)S(1)} %collective-permute-done.1), channel_id=1, source_target_pairs={{0,1},{1,2},{2,3},{3,32},{4,5},{5,6},{6,7},{7,36},{8,9},{9,10},{10... | collective-permute-start | bytes 98312 | tf_op jit(solution)/shard_map/ppermute | solution.py:204
  21.7 5.1 %collective-permute-start.3 = (bf16[32,512]{1,0:T(8,128)(2,1)S(1)}, bf16[32,512]{1,0:T(8,128)(2,1)S(1)}, u32[]{:S(2)}, u32[]{:S(2)}) collective-permute-start(bf16[32,512]{1,0:T(8,128)(2,1)S(1)} %collective-permute-done.2), channel_id=1, source_target_pairs={{0,1},{1,2},{2,3},{3,32},{4,5},{5,6},{6,7},{7,36},{8,9},{9,10},{10... | collective-permute-start | bytes 98312 | tf_op jit(solution)/shard_map/ppermute | solution.py:204
  26.9 0.7 collective-permute-start.4
  27.6 5.0 %collective-permute-start.6 = (bf16[128,512]{1,0:T(8,128)(2,1)S(1)}, bf16[128,512]{1,0:T(8,128)(2,1)S(1)}, u32[]{:S(2)}, u32[]{:S(2)}) collective-permute-start(bf16[128,512]{1,0:T(8,128)(2,1)S(1)} %get-tuple-element.22), channel_id=1, source_target_pairs={{0,192},{1,193},{2,194},{3,195},{4,196},{5,197},{6,198},{7,199},{8... | collective-permute-start | bytes 393224 | tf_op jit(solution)/shard_map/ppermute | solution.py:204
  28.2 5.7 %collective-permute-start.5 = (bf16[128,512]{1,0:T(8,128)(2,1)S(1)}, bf16[128,512]{1,0:T(8,128)(2,1)S(1)}, u32[]{:S(2)}, u32[]{:S(2)}) collective-permute-start(bf16[128,512]{1,0:T(8,128)(2,1)S(1)} %get-tuple-element.22), channel_id=1, source_target_pairs={{0,64},{1,65},{2,66},{3,67},{4,68},{5,69},{6,70},{7,71},{8,72},{9,... | collective-permute-start | bytes 393224 | tf_op jit(solution)/shard_map/ppermute | solution.py:204
  32.6 7.5 %collective-permute-start.8 = (bf16[64,512]{1,0:T(8,128)(2,1)S(1)}, bf16[64,512]{1,0:T(8,128)(2,1)S(1)}, u32[]{:S(2)}, u32[]{:S(2)}) collective-permute-start(bf16[64,512]{1,0:T(8,128)(2,1)S(1)} %slice.41), channel_id=1, source_target_pairs={{0,192},{1,193},{2,194},{3,195},{4,196},{5,197},{6,198},{7,199},{8... | collective-permute-start | bytes 196616 | tf_op jit(solution)/shard_map/ppermute | solution.py:204
  33.9 5.6 %collective-permute-start.7 = (bf16[64,512]{1,0:T(8,128)(2,1)S(1)}, bf16[64,512]{1,0:T(8,128)(2,1)S(1)}, u32[]{:S(2)}, u32[]{:S(2)}) collective-permute-start(bf16[64,512]{1,0:T(8,128)(2,1)S(1)} %slice.40), channel_id=1, source_target_pairs={{0,64},{1,65},{2,66},{3,67},{4,68},{5,69},{6,70},{7,71},{8,72},{9,... | collective-permute-start | bytes 196616 | tf_op jit(solution)/shard_map/ppermute | solution.py:204
  40.7 10.5 %collective-permute-start.9 = (bf16[512,512]{1,0:T(8,128)(2,1)S(1)}, bf16[512,512]{1,0:T(8,128)(2,1)S(1)}, u32[]{:S(2)}, u32[]{:S(2)}) collective-permute-start(bf16[512,512]{1,0:T(8,128)(2,1)S(1)} %get-tuple-element.33), channel_id=1, source_target_pairs={{0,4},{1,5},{2,6},{3,7},{4,8},{5,9},{6,10},{7,11},{8,12},{9,13},{1... | collective-permute-start | bytes 1572872 | tf_op jit(solution)/shard_map/ppermute | solution.py:204
  42.4 9.3 %collective-permute-start.10 = (bf16[512,512]{1,0:T(8,128)(2,1)S(1)}, bf16[512,512]{1,0:T(8,128)(2,1)S(1)}, u32[]{:S(2)}, u32[]{:S(2)}) collective-permute-start(bf16[512,512]{1,0:T(8,128)(2,1)S(1)} %get-tuple-element.33), channel_id=1, source_target_pairs={{0,12},{1,13},{2,14},{3,15},{4,0},{5,1},{6,2},{7,3},{8,4},{9,5},{1... | collective-permute-start | bytes 1572872 | tf_op jit(solution)/shard_map/ppermute | solution.py:204
  51.2 7.7 %collective-permute-start.11 = (bf16[256,512]{1,0:T(8,128)(2,1)S(1)}, bf16[256,512]{1,0:T(8,128)(2,1)S(1)}, u32[]{:S(2)}, u32[]{:S(2)}) collective-permute-start(bf16[256,512]{1,0:T(8,128)(2,1)S(1)} %slice.42), channel_id=1, source_target_pairs={{0,4},{1,5},{2,6},{3,7},{4,8},{5,9},{6,10},{7,11},{8,12},{9,13},{1... | collective-permute-start | bytes 786440 | tf_op jit(solution)/shard_map/ppermute | solution.py:204
  51.7 7.9 %collective-permute-start.12 = (bf16[256,512]{1,0:T(8,128)(2,1)S(1)}, bf16[256,512]{1,0:T(8,128)(2,1)S(1)}, u32[]{:S(2)}, u32[]{:S(2)}) collective-permute-start(bf16[256,512]{1,0:T(8,128)(2,1)S(1)} %slice.43), channel_id=1, source_target_pairs={{0,12},{1,13},{2,14},{3,15},{4,0},{5,1},{6,2},{7,3},{8,4},{9,5},{1... | collective-permute-start | bytes 786440 | tf_op jit(solution)/shard_map/ppermute | solution.py:204
  60.4 76.3 %collective-permute-start.13 = (bf16[2048,512]{1,0:T(8,128)(2,1)}, bf16[2048,512]{1,0:T(8,128)(2,1)}, u32[]{:S(2)}, u32[]{:S(2)}) collective-permute-start(bf16[2048,512]{1,0:T(8,128)(2,1)} %constant_dynamic-update-slice_fusion.5.mine), channel_id=1, source_target_pairs={{0,16},{1,17},{2,18},{3,19},{4,20},{5,21},{6,22},{7,23},{8,24},{9,... | collective-permute-start | bytes 6291464 | tf_op jit(solution)/shard_map/ppermute | solution.py:204
  60.4 37.0 %copy-start.22 = (bf16[512,512]{1,0:T(8,128)(2,1)S(1)}, bf16[512,512]{1,0:T(8,128)(2,1)}, u32[]{:S(2)}) copy-start(bf16[512,512]{1,0:T(8,128)(2,1)} %node_out.8) | copy-start | bytes 1572868
  60.4 37.0 %copy-start.29 = (f32[512]{0:T(512)S(1)}, f32[512]{0:T(512)}, u32[]{:S(2)}) copy-start(f32[512]{0:T(512)} %param.35) | copy-start | bytes 6148
  60.4 37.0 %copy-start.30 = (f32[512]{0:T(512)S(1)}, f32[512]{0:T(512)}, u32[]{:S(2)}) copy-start(f32[512]{0:T(512)} %param.37) | copy-start | bytes 6148
  60.5 37.0 %copy-start.31 = (f32[512]{0:T(512)S(1)}, f32[512]{0:T(512)}, u32[]{:S(2)}) copy-start(f32[512]{0:T(512)} %param.39) | copy-start | bytes 6148
  63.6 12.6 %collective-permute-start.19 = (bf16[1,128,512]{2,1,0:T(8,128)(2,1)S(1)}, bf16[1,128,512]{2,1,0:T(8,128)(2,1)S(1)}, u32[]{:S(2)}, u32[]{:S(2)}) collective-permute-start(bf16[1,128,512]{2,1,0:T(8,128)(2,1)S(1)} %get-tuple-element.23), channel_id=1, source_target_pairs={{1,0},{2,1},{3,2},{5,4},{6,5},{7,6},{9,8},{10,9},{11,10},{13,12},{... | collective-permute-start | bytes 393224 | tf_op jit(solution)/shard_map/ppermute | solution.py:258
  64.9 20.4 %collective-permute-start.18 = (bf16[1,128,512]{2,1,0:T(8,128)(2,1)S(1)}, bf16[1,128,512]{2,1,0:T(8,128)(2,1)S(1)}, u32[]{:S(2)}, u32[]{:S(2)}) collective-permute-start(bf16[1,128,512]{2,1,0:T(8,128)(2,1)S(1)} %get-tuple-element.24), channel_id=1, source_target_pairs={{0,1},{1,2},{2,3},{4,5},{5,6},{6,7},{8,9},{9,10},{10,11},{12,13},{... | collective-permute-start | bytes 393224 | tf_op jit(solution)/shard_map/ppermute | solution.py:257
  69.7 18.5 %collective-permute-start.17 = (bf16[1,128,512]{2,1,0:T(8,128)(2,1)}, bf16[1,128,512]{2,1,0:T(8,128)(2,1)}, u32[]{:S(2)}, u32[]{:S(2)}) collective-permute-start(bf16[1,128,512]{2,1,0:T(8,128)(2,1)} %get-tuple-element.25), channel_id=1, source_target_pairs={{4,0},{8,4},{12,8},{5,1},{9,5},{13,9},{6,2},{10,6},{14,10},{7,3},{... | collective-permute-start | bytes 393224 | tf_op jit(solution)/shard_map/ppermute | solution.py:258
  71.0 17.2 %collective-permute-start.16 = (bf16[1,128,512]{2,1,0:T(8,128)(2,1)}, bf16[1,128,512]{2,1,0:T(8,128)(2,1)}, u32[]{:S(2)}, u32[]{:S(2)}) collective-permute-start(bf16[1,128,512]{2,1,0:T(8,128)(2,1)} %get-tuple-element.26), channel_id=1, source_target_pairs={{0,4},{4,8},{8,12},{1,5},{5,9},{9,13},{2,6},{6,10},{10,14},{3,7},{... | collective-permute-start | bytes 393224 | tf_op jit(solution)/shard_map/ppermute | solution.py:257
  76.8 13.6 %collective-permute-start.15 = (bf16[1,128,512]{2,1,0:T(8,128)(2,1)}, bf16[1,128,512]{2,1,0:T(8,128)(2,1)}, u32[]{:S(2)}, u32[]{:S(2)}) collective-permute-start(bf16[1,128,512]{2,1,0:T(8,128)(2,1)} %get-tuple-element.27), channel_id=1, source_target_pairs={{16,0},{32,16},{48,32},{64,48},{80,64},{96,80},{112,96},{128,112},... | collective-permute-start | bytes 393224 | tf_op jit(solution)/shard_map/ppermute | solution.py:258
  86.0 11.4 %collective-permute-start.14 = (bf16[1,128,512]{2,1,0:T(8,128)(2,1)}, bf16[1,128,512]{2,1,0:T(8,128)(2,1)}, u32[]{:S(2)}, u32[]{:S(2)}) collective-permute-start(bf16[1,128,512]{2,1,0:T(8,128)(2,1)} %get-tuple-element.28), channel_id=1, source_target_pairs={{0,16},{16,32},{32,48},{48,64},{64,80},{80,96},{96,112},{112,128},... | collective-permute-start | bytes 393224 | tf_op jit(solution)/shard_map/ppermute | solution.py:257
  (31 other events, 292.8 us)

commit v2 on v1

v2 whole, which is shorter than its diff:
```python
import functools
import itertools

import jax
import jax.numpy as jnp
from jax import lax
from jax.experimental import pallas as pl
from jax.experimental.pallas import tpu as pltpu
from jax.sharding import Mesh
from jax.sharding import PartitionSpec as P

AXES = ("x", "zh", "c", "y", "z")
SIZES = (4, 2, 2, 4, 4)
EPS = 1e-05
F32 = jnp.float32
BF16 = jnp.bfloat16
D = 512
BLOCK = 128
SHARES = (2, 2, 2, 2)


def linear(place):
    number = 0
    for size, at in zip(SIZES, place):
        number = number * size + at
    return number


def permutation(move):
    pairs = []
    for place in itertools.product(*(range(size) for size in SIZES)):
        target = move(*place)
        if target is not None:
            pairs.append((linear(place), linear(target)))
    return pairs


def along_z(x, zh, c, y, z, step):
    at = (zh * 4 + z + step) % 8
    return (x, at // 4, c, y, at % 4)


def along_plane(x, zh, c, y, z, step, first):
    if (c == 0) == first:
        return ((x + step) % 4, zh, c, y, z)
    return (x, zh, c, (y + step) % 4, z)


SWAP = permutation(lambda x, zh, c, y, z: (x, zh, 1 - c, y, z))
RING = permutation(lambda x, zh, c, y, z: along_z(x, zh, c, y, z, 1 if c == 0 else -1))
RING_END = permutation(lambda x, zh, c, y, z: along_z(x, zh, c, y, z, -1) if c == 1 else None)
UP_FIRST = permutation(functools.partial(along_plane, step=1, first=True))
DOWN_FIRST = permutation(functools.partial(along_plane, step=-1, first=True))
UP_SECOND = permutation(functools.partial(along_plane, step=1, first=False))
DOWN_SECOND = permutation(functools.partial(along_plane, step=-1, first=False))


def dot(a, b):
    return lax.dot_general(a, b, (((1,), (0,)), ((), ())), preferred_element_type=F32)


def dot_t(a, b):
    return lax.dot_general(a, b, (((0,), (0,)), ((), ())), preferred_element_type=F32)


def normed(values):
    center = values - jnp.mean(values, axis=-1, keepdims=True)
    spread = jnp.mean(center * center, axis=-1, keepdims=True)
    return center * lax.rsqrt(spread + EPS)


def pool_kernel(
    fine_h, parent_h, medium_h, medium_parent_h, coarse_h, nbrs_h, weight_h,
    sender_out, pool_out, medium_out, slots_out, comp_out, member_out,
    fine, parent, medium, medium_parent, coarse, nbrs, weight, sems,
):
    pairs = (
        (parent_h, parent), (fine_h, fine), (medium_h, medium), (medium_parent_h, medium_parent),
        (coarse_h, coarse), (weight_h.at[pl.ds(0, D)], weight), (nbrs_h, nbrs),
    )
    copies = [pltpu.make_async_copy(source, target, sems.at[k]) for k, (source, target) in enumerate(pairs)]
    for copy in copies:
        copy.start()
    for copy in copies:
        copy.wait()
    member = (parent[...] == lax.broadcasted_iota(jnp.int32, (128, 1024), 0)).astype(F32)
    count = jnp.sum(member, axis=1, keepdims=True)
    member = member.astype(BF16)
    medium_pool = medium[...].astype(F32) + dot(member, fine[...]) / count
    medium_out[...] = medium_pool
    upper = (medium_parent[...] == lax.broadcasted_iota(jnp.int32, (16, 128), 0)).astype(F32)
    upper_count = jnp.sum(upper, axis=1, keepdims=True)
    total = jnp.dot(upper, medium_pool, precision=lax.Precision.HIGHEST, preferred_element_type=F32)
    pool = (coarse[...].astype(F32) + total / upper_count).astype(BF16)
    pool_out[...] = pool
    sender_out[...] = dot(pool, weight[...]).astype(BF16)
    upper = upper.astype(BF16)
    member_out[...] = jnp.concatenate([upper, upper], axis=0)
    comp = dot(upper, member).astype(BF16)
    comp_out[...] = jnp.concatenate([comp, comp], axis=0)
    here = {name: lax.axis_index(name) for name in AXES}
    row = nbrs[...] & 15
    owner = nbrs[...] >> 4
    z = owner & 3
    y = (owner >> 2) & 3
    c = (owner >> 4) & 1
    zh = (owner >> 5) & 1
    x = owner >> 6
    back = (here["zh"] * 4 + here["z"] - zh * 4 - z) & 7
    stream = (back > 3).astype(jnp.int32)
    at = jnp.where(stream == 0, back, 7 - back) * 32 + c * 16 + row
    step_x = (here["x"] - x) & 3
    step_y = (here["y"] - y) & 3
    order_x = jnp.where(step_x == 2, 3, jnp.where(step_x == 3, 2, step_x))
    order_y = jnp.where(step_y == 2, 3, jnp.where(step_y == 3, 2, step_y))
    at = at + jnp.where(stream == 0, order_x * 128 + order_y * 512, order_y * 128 + order_x * 512)
    slots_out[...] = at + jnp.where(stream == here["c"], 0, 2048)


def face_kernel(
    after, fine_h, rows_h, counts, weight_h, edge_out_h,
    sender_out, centred_out, f0, f1, f2, f3, f4, f5,
    fine, rows, weight, edge_out, sems,
):
    pairs = ((rows_h, rows), (fine_h, fine), (weight_h.at[pl.ds(0, D)], weight), (edge_out_h, edge_out))
    copies = [pltpu.make_async_copy(source, target, sems.at[k]) for k, (source, target) in enumerate(pairs)]
    for copy in copies:
        copy.start()
    for copy in copies:
        copy.wait()
    sender = dot(fine[...], weight[...]).astype(BF16)
    sender_out[...] = sender
    wide = edge_out[...].astype(F32)
    centred_out[...] = (wide - jnp.mean(wide, axis=1, keepdims=True)).astype(BF16)
    flat = jnp.concatenate(
        [rows[:, 128 * face : 128 * (face + 1)] for face in range(6)] + [jnp.zeros((2, 128), jnp.int32)], axis=0
    )
    columns = flat.T
    place = lax.broadcasted_iota(jnp.int32, (128, 1), 0)
    for face, face_out in enumerate((f0, f1, f2, f3, f4, f5)):
        wanted = jnp.where(place < counts[0, face], columns[:, face : face + 1], -1)
        picked = (wanted == lax.broadcasted_iota(jnp.int32, (128, 1024), 1)).astype(F32).astype(BF16)
        face_out[0] = dot(picked, sender).astype(BF16)


def table_kernel(sender, g0, g1, g2, g3, g4, g5, nbrs, table_out, near_out, sems):
    copies = [pltpu.make_async_copy(sender, table_out.at[pl.ds(0, 1024)], sems.at[0])]
    for k, ghost in enumerate((g0, g1, g2, g3, g4, g5)):
        copies.append(
            pltpu.make_async_copy(ghost.at[0], table_out.at[pl.ds(1024 + 128 * k, 128)], sems.at[1 + k])
        )
    for copy in copies:
        copy.start()
    padded = jnp.concatenate([nbrs[...], jnp.zeros((2, 1024), jnp.int32)], axis=0)
    for block in range(8):
        near_out[block * 128 : (block + 1) * 128, :] = padded[:, block * 128 : (block + 1) * 128].T
    for copy in copies:
        copy.wait()


def edge_kernel(
    table, fine, nbrs, receive, bias, centred, gain, node_in, node_bias, node_out, node_gain,
    new_out,
    picked, hidden,
    *, first,
):
    blocks = new_out.shape[0] // BLOCK

    def step(block, carry):
        here = pl.ds(pl.multiple_of(block * BLOCK, BLOCK), BLOCK)
        span = pl.ds(pl.multiple_of((first + block) * BLOCK, BLOCK), BLOCK)
        own = fine[span, :]
        near = nbrs[span, :]
        received = dot(own, receive[...]) + bias[...]
        for k in range(6):
            wanted = near[:, k : k + 1]
            match = wanted == lax.broadcasted_iota(jnp.int32, (BLOCK, 1792), 1)
            picked[k * BLOCK : (k + 1) * BLOCK, :] = match.astype(F32).astype(BF16)
        found = dot(picked[...], table[...]).astype(BF16).astype(F32)
        hidden[...] = jnp.maximum(found + jnp.concatenate([received] * 6, axis=0), 0.0).astype(BF16)
        out = dot(hidden[...], centred[...])
        out = out * lax.rsqrt(jnp.mean(out * out, axis=-1, keepdims=True) + EPS)
        total = jnp.zeros((BLOCK, D), F32)
        for k in range(6):
            total = total + out[k * BLOCK : (k + 1) * BLOCK] * (near[:, k : k + 1] < 1792).astype(F32)
        incoming = (total * gain[...]).astype(BF16)
        both = jnp.concatenate([own, incoming], axis=1)
        node = jnp.maximum(dot(both, node_in[...]) + node_bias[...], 0.0).astype(BF16)
        new_out[here, :] = own.astype(F32) + normed(dot(node, node_out[...])) * node_gain[...]
        return carry

    lax.fori_loop(0, blocks, step, 0)


def columns_of(slots):
    places = slots[...]
    return jnp.concatenate([jnp.broadcast_to(places[:, k : k + 1], (16, 128)) for k in range(64)], axis=0)


def found_in(column, sources):
    lane = lax.broadcasted_iota(jnp.int32, (1024, 128), 1)
    total = jnp.zeros((1024, D), F32)
    for start, source in sources:
        picked = [
            (column == lane + (start + t * 128)).astype(F32).astype(BF16) for t in range(source.shape[0] // 128)
        ]
        total = total + dot(jnp.concatenate(picked, axis=1), source[...])
    return total


def gather_kernel(slots, m0, m1, m2, m3, m4, found_out):
    sources = ((0, m0), (512, m1), (1024, m2), (1536, m3), (1792, m4))
    found_out[...] = found_in(columns_of(slots), sources).astype(BF16)


def coarse_kernel(
    found, o0, o1, o2, o3, o4, slots, pool, medium, comp, member, *rest,
):
    *news, edge_in, edge_bias, edge_out, edge_gain, node_in, node_bias, node_out, node_gain, fine_out, medium_out, coarse_out = rest
    pool_rows = pool[...]
    received = dot(pool_rows, edge_in[...]) + edge_bias[...]
    sources = ((2048, o0), (2560, o1), (3072, o2), (3584, o3), (3840, o4))
    total = found[...].astype(F32) + found_in(columns_of(slots), sources)
    hidden = jnp.maximum(total.reshape(64, 16, D) + received[None], 0.0).astype(BF16).reshape(1024, D)
    message = normed(dot(hidden, edge_out[...])) * edge_gain[...]
    incoming = jnp.sum(message.reshape(64, 16, D), axis=0).astype(BF16)
    both = jnp.concatenate([pool_rows, incoming], axis=1)
    hidden = jnp.maximum(dot(both, node_in[...]) + node_bias[...], 0.0).astype(BF16)
    delta = normed(dot(hidden, node_out[...])) * node_gain[...]
    coarse_out[...] = (pool_rows.astype(F32) + delta).astype(BF16)
    high = delta.astype(BF16)
    low = (delta - high.astype(F32)).astype(BF16)
    parts = jnp.concatenate([high, low], axis=0)
    medium_out[...] = (medium[...] + dot_t(member[...], parts)).astype(BF16)
    spread = dot_t(comp[...], parts)
    first = 0
    for new in news:
        last = first + new.shape[0]
        fine_out[first:last, :] = (new[...] + spread[first:last]).astype(BF16)
        first = last


def joined(*parts):
    return jnp.concatenate(parts, axis=0)


def sent(rows, pairs):
    return lax.ppermute(rows, AXES, pairs)


def local(
    fine_state, fine_nbrs, send_rows, ghost_counts, fine_parent, medium_state, medium_parent, coarse_state,
    coarse_nbrs, fine_edge_in, fine_edge_bias, fine_edge_out, fine_edge_gain, fine_node_in, fine_node_bias,
    fine_node_out, fine_node_gain, coarse_edge_in, coarse_edge_bias, coarse_edge_out, coarse_edge_gain,
    coarse_node_in, coarse_node_bias, coarse_node_out, coarse_node_gain,
):
    row = lambda vector: vector.reshape(1, -1)
    shaped = jax.ShapeDtypeStruct
    held = pl.BlockSpec(memory_space=pltpu.VMEM)
    far = pl.BlockSpec(memory_space=pltpu.HBM)
    scalars = pl.BlockSpec(memory_space=pltpu.SMEM)
    upper = pl.BlockSpec((D, D), lambda i: (1, 0), memory_space=pltpu.VMEM)
    tied = lax.optimization_barrier
    distant = functools.partial(pltpu.with_memory_space_constraint, memory_space=pltpu.HBM)

    def kernel(body, outs, specs, args, scratch=(), limit=32, cost=None):
        return pl.pallas_call(
            body,
            grid=(1,),
            out_shape=outs,
            in_specs=specs,
            out_specs=[held] * len(outs),
            scratch_shapes=list(scratch),
            compiler_params=pltpu.CompilerParams(vmem_limit_bytes=limit << 20),
            cost_estimate=cost,
        )(*args)

    sender, pool, medium_pool, slots, comp, member = kernel(
        pool_kernel,
        [
            shaped((16, D), BF16),
            shaped((16, D), BF16),
            shaped((128, D), F32),
            shaped((16, 64), jnp.int32),
            shaped((32, 1024), BF16),
            shaped((32, 128), BF16),
        ],
        [far] * 7,
        [
            distant(value)
            for value in (
                fine_state, row(fine_parent), medium_state, row(medium_parent), coarse_state, coarse_nbrs,
                coarse_edge_in,
            )
        ],
        [
            pltpu.VMEM((1024, D), BF16),
            pltpu.VMEM((1, 1024), jnp.int32),
            pltpu.VMEM((128, D), BF16),
            pltpu.VMEM((1, 128), jnp.int32),
            pltpu.VMEM((16, D), BF16),
            pltpu.VMEM((16, 64), jnp.int32),
            pltpu.VMEM((D, D), BF16),
            pltpu.SemaphoreType.DMA((7,)),
        ],
    )
    fine_sender, centred, *faces = kernel(
        face_kernel,
        [shaped((1024, D), BF16), shaped((D, D), BF16)] + [shaped((1, 128, D), BF16)] * 6,
        [pl.BlockSpec(memory_space=pl.ANY), far, far, scalars, far, far],
        (
            member, distant(fine_state), distant(send_rows.reshape(1, 768)), ghost_counts, distant(fine_edge_in),
            distant(fine_edge_out),
        ),
        [
            pltpu.VMEM((1024, D), BF16),
            pltpu.VMEM((1, 768), jnp.int32),
            pltpu.VMEM((D, D), BF16),
            pltpu.VMEM((D, D), BF16),
            pltpu.SemaphoreType.DMA((4,)),
        ],
    )

    def faced(block, face):
        axes = (("x", "zh", "c"), "y", "z")[face // 2]
        count = lax.axis_size(axes)
        pairs = [(k, k + 1) for k in range(count - 1)]
        return lax.ppermute(block, axes, [(b, a) for a, b in pairs] if face % 2 == 0 else pairs)

    core = lax.axis_index("c")
    beside = sent(sender, SWAP)
    chip = jnp.where(core == 0, joined(sender, beside), joined(beside, sender))
    ring = [chip]
    ghosts = {}
    for hop, group in enumerate(((1,), (0,), (3, 2), (5, 4))):
        carried = ring[-1]
        blocks = [faces[face] for face in group]
        carried, *blocks = tied((carried, *blocks))
        ring.append(sent(carried, RING if hop < 3 else RING_END))
        for face, block in zip(group, blocks):
            ghosts[face] = faced(block, face)
    last = ring.pop()
    column = jnp.where(core == 0, joined(*ring), joined(*ring[1:], last))
    near_faces = [ghosts[face] for face in (1, 0, 3, 2, 5, 4)]
    fine_sender, column = tied((fine_sender, column))
    table, near = kernel(
        table_kernel,
        [shaped((1792, D), BF16), shaped((1024, 8), jnp.int32)],
        [pl.BlockSpec(memory_space=pl.ANY)] * 7 + [held],
        (fine_sender, *near_faces, fine_nbrs.T),
        [pltpu.SemaphoreType.DMA((7,))],
    )
    news = []

    def edges(blocks):
        first = sum(new.shape[0] for new in news) // BLOCK
        news.extend(
            kernel(
                functools.partial(edge_kernel, first=first),
                [shaped((blocks * BLOCK, D), F32)],
                [held] * 3 + [upper] + [held] * 7,
                (
                    table, fine_state, near, fine_edge_in, row(fine_edge_bias), centred, row(fine_edge_gain),
                    fine_node_in, row(fine_node_bias), fine_node_out, row(fine_node_gain),
                ),
                [pltpu.VMEM((6 * BLOCK, 1792), BF16), pltpu.VMEM((6 * BLOCK, D), BF16)],
                cost=pl.CostEstimate(
                    flops=blocks * 1_700_000_000, bytes_accessed=blocks * 3_000_000, transcendentals=0
                ),
            )
        )

    up, down = sent(column, UP_FIRST), sent(column, DOWN_FIRST)
    edges(SHARES[0])
    up, down, news[-1] = tied((up, down, news[-1]))
    table, up = tied((table, up))
    rest = [sent(up[:64], UP_FIRST), sent(down[64:], DOWN_FIRST)]
    edges(SHARES[1])
    *rest, news[-1] = tied((*rest, news[-1]))
    line = joined(column, up, down, *rest)
    table, line = tied((table, line))
    up, down = sent(line, UP_SECOND), sent(line, DOWN_SECOND)
    others = [sent(line, SWAP)]
    edges(SHARES[2])
    up, down, news[-1] = tied((up, down, news[-1]))
    table, up = tied((table, up))
    rest = [sent(up[:256], UP_SECOND), sent(down[256:], DOWN_SECOND)]
    others += [sent(up, SWAP), sent(down, SWAP)]
    edges(SHARES[3])
    *rest, news[-1] = tied((*rest, news[-1]))
    others += [sent(part, SWAP) for part in rest]
    (found,) = kernel(
        gather_kernel, [shaped((1024, D), BF16)], [held] * 6, (slots, line, up, down, *rest), limit=40,
        cost=pl.CostEstimate(flops=2_000_000_000, bytes_accessed=4_000_000, transcendentals=0),
    )
    fine_out, medium_out, coarse_out = kernel(
        coarse_kernel,
        [shaped((1024, D), BF16), shaped((128, D), BF16), shaped((16, D), BF16)],
        [held] * (11 + len(news)) + [upper] + [held] * 7,
        (
            found, *others, slots, pool, medium_pool, comp, member, *news, coarse_edge_in, row(coarse_edge_bias),
            coarse_edge_out, row(coarse_edge_gain), coarse_node_in, row(coarse_node_bias), coarse_node_out,
            row(coarse_node_gain),
        ),
        limit=48,
    )
    return fine_out, medium_out, coarse_out


def solution(mesh):
    torus = Mesh(mesh.devices.reshape(SIZES), AXES)
    rows = P(AXES, None)
    placed = (rows, rows, P(AXES, None, None), rows, P(AXES), rows, P(AXES), rows, rows) + (P(),) * 16
    return jax.shard_map(local, mesh=torus, in_specs=placed, out_specs=(rows, rows, rows), check_vma=False)
```

time: 147 us -> 98.7 us (0.67)
  the two profiles are of different devices: /device:TPU:2 before, /device:TPU:1 now
where the time goes in v2:
time: 98.7 us; the launch traced here: 98.4 us
  starting transfers between devices  52.6 us (53%)
  Pallas kernels  38.9 us (39%)
  waiting for transfers between devices  4.58 us (5%)
  local copies, waits for them, and re-layouts  1.16 us (1%)
  between operations  1.15 us (1%)
    pallas_call x9, Pallas kernels, kernel(): pl.pallas_call(body, grid=(1,), out_shape=outs, in_specs=specs, out_specs...  38.9 us
    ppermute x18, starting transfers between devices, sent(): return lax.ppermute(rows, AXES, pairs)  36.7 us
    ppermute x6, starting transfers between devices, faced(): lax.ppermute(block, axes, [(b, a) for a, b in pairs] if face % 2 == 0 els...  15.9 us
    ppermute x18, waiting for transfers between devices, sent(): return lax.ppermute(rows, AXES, pairs)  4.56 us
  transfers between devices with their start and end apart: 24, of which 3 were waited for; matrix products, arithmetic and copies ran while one was open for 0% of the time, Pallas kernels for 25%

profile of v2, /device:TPU:1, one launch (start us, length us, event | category | flops | bytes accessed | tf_op | source)
XLA Modules:
  0.0 98.4 jit_solution(18349515973730769655)
XLA Ops:
  0.6 2.3 %shard_map.256 = (bf16[16,512]{1,0:T(8,128)(2,1)S(1)}, bf16[16,512]{1,0:T(8,128)(2,1)S(1)}, f32[128,512]{1,0:T(8,128)S(1)}, s32[16,64]{1,0:T(8,128)S(1)}, bf16[3...) custom-call(bf16[1024,512]{1,0:T(8,128)(2,1)} %fine.7, s32[1,1024]{1,0:T(1,128)} %bitcast.33, ...), custom_call_target="tpu_custom_call" | custom-call | tf_op jit(solution)/shard_map/pallas_call | solution.py:267
  2.9 3.3 %collective-permute-start = (bf16[16,512]{1,0:T(8,128)(2,1)S(1)}, bf16[16,512]{1,0:T(8,128)(2,1)S(1)}, u32[]{:S(2)}, u32[]{:S(2)}) collective-permute-start(bf16[16,512]{1,0:T(8,128)(2,1)S(1)} %get-tuple-element.52), channel_id=1, source_target_pairs={{0,16},{1,17},{2,18},{3,19},{4,20},{5,21},{6,22},{7,23},{8,24},{9,... | collective-permute-start | bytes 49160 | tf_op jit(solution)/shard_map/ppermute | solution.py:248
  6.3 3.8 %shard_map.257 = (bf16[1024,512]{1,0:T(8,128)(2,1)S(1)}, bf16[512,512]{1,0:T(8,128)(2,1)S(1)}, bf16[1,128,512]{2,1,0:T(8,128)(2,1)S(1)}, bf16[1,128,512]{2,1,0:T...) custom-call(bf16[32,128]{1,0:T(8,128)(2,1)S(1)} %get-tuple-element.5, ...), custom_call_target="tpu_custom_call" | custom-call | tf_op jit(solution)/shard_map/pallas_call | solution.py:267
  10.1 3.9 %collective-permute-start.1 = (bf16[32,512]{1,0:T(8,128)(2,1)S(1)}, bf16[32,512]{1,0:T(8,128)(2,1)S(1)}, u32[]{:S(2)}, u32[]{:S(2)}) collective-permute-start(bf16[32,512]{1,0:T(8,128)(2,1)S(1)} %maximum_select_fusion.1), channel_id=1, source_target_pairs={{0,1},{1,2},{2,3},{3,32},{4,5},{5,6},{6,7},{7,36},{8,9},{9,10},{10... | collective-permute-start | bytes 98312 | tf_op jit(solution)/shard_map/ppermute | solution.py:248
  14.0 4.2 %collective-permute-start.5 = (bf16[1,128,512]{2,1,0:T(8,128)(2,1)S(1)}, bf16[1,128,512]{2,1,0:T(8,128)(2,1)S(1)}, u32[]{:S(2)}, u32[]{:S(2)}) collective-permute-start(bf16[1,128,512]{2,1,0:T(8,128)(2,1)S(1)} %get-tuple-element.64), channel_id=1, source_target_pairs={{0,16},{16,32},{32,48},{48,64},{64,80},{80,96},{96,112},{112,128},... | collective-permute-start | bytes 393224 | tf_op jit(solution)/shard_map/ppermute | solution.py:328
  18.2 3.0 %collective-permute-start.2 = (bf16[32,512]{1,0:T(8,128)(2,1)S(1)}, bf16[32,512]{1,0:T(8,128)(2,1)S(1)}, u32[]{:S(2)}, u32[]{:S(2)}) collective-permute-start(bf16[32,512]{1,0:T(8,128)(2,1)S(1)} %collective-permute-done.1), channel_id=1, source_target_pairs={{0,1},{1,2},{2,3},{3,32},{4,5},{5,6},{6,7},{7,36},{8,9},{9,10},{10... | collective-permute-start | bytes 98312 | tf_op jit(solution)/shard_map/ppermute | solution.py:248
  21.2 1.9 %collective-permute-done.2 = bf16[32,512]{1,0:T(8,128)(2,1)S(1)} collective-permute-done((bf16[32,512]{1,0:T(8,128)(2,1)S(1)}, bf16[32,512]{1,0:T(8,128)(2,1)S(1)}, u32[]{:S(2)}, u32[]{:S(2)}) %collective-permute-start.2) | collective-permute-done | bytes 32800 | tf_op jit(solution)/shard_map/ppermute | solution.py:248
  23.1 2.5 %collective-permute-start.3 = (bf16[32,512]{1,0:T(8,128)(2,1)S(1)}, bf16[32,512]{1,0:T(8,128)(2,1)S(1)}, u32[]{:S(2)}, u32[]{:S(2)}) collective-permute-start(bf16[32,512]{1,0:T(8,128)(2,1)S(1)} %collective-permute-done.2), channel_id=1, source_target_pairs={{0,1},{1,2},{2,3},{3,32},{4,5},{5,6},{6,7},{7,36},{8,9},{9,10},{10... | collective-permute-start | bytes 98312 | tf_op jit(solution)/shard_map/ppermute | solution.py:248
  26.6 4.8 %collective-permute-start.4 = (bf16[32,512]{1,0:T(8,128)(2,1)S(1)}, bf16[32,512]{1,0:T(8,128)(2,1)S(1)}, u32[]{:S(2)}, u32[]{:S(2)}) collective-permute-start(bf16[32,512]{1,0:T(8,128)(2,1)S(1)} %collective-permute-done.3), channel_id=1, source_target_pairs={{16,51},{17,16},{18,17},{19,18},{20,55},{21,20},{22,21},{23,22},{2... | collective-permute-start | bytes 98312 | tf_op jit(solution)/shard_map/ppermute | solution.py:248
  31.5 1.9 %collective-permute-start.6 = (bf16[1,128,512]{2,1,0:T(8,128)(2,1)S(1)}, bf16[1,128,512]{2,1,0:T(8,128)(2,1)S(1)}, u32[]{:S(2)}, u32[]{:S(2)}) collective-permute-start(bf16[1,128,512]{2,1,0:T(8,128)(2,1)S(1)} %get-tuple-element.65), channel_id=1, source_target_pairs={{16,0},{32,16},{48,32},{64,48},{80,64},{96,80},{112,96},{128,112},... | collective-permute-start | bytes 393224 | tf_op jit(solution)/shard_map/ppermute | solution.py:328
  33.4 3.2 %collective-permute-start.7 = (bf16[1,128,512]{2,1,0:T(8,128)(2,1)S(1)}, bf16[1,128,512]{2,1,0:T(8,128)(2,1)S(1)}, u32[]{:S(2)}, u32[]{:S(2)}) collective-permute-start(bf16[1,128,512]{2,1,0:T(8,128)(2,1)S(1)} %get-tuple-element.66), channel_id=1, source_target_pairs={{0,4},{4,8},{8,12},{1,5},{5,9},{9,13},{2,6},{6,10},{10,14},{3,7},{... | collective-permute-start | bytes 393224 | tf_op jit(solution)/shard_map/ppermute | solution.py:328
  39.3 4.0 %collective-permute-start.9 = (bf16[1,128,512]{2,1,0:T(8,128)(2,1)S(1)}, bf16[1,128,512]{2,1,0:T(8,128)(2,1)S(1)}, u32[]{:S(2)}, u32[]{:S(2)}) collective-permute-start(bf16[1,128,512]{2,1,0:T(8,128)(2,1)S(1)} %get-tuple-element.68), channel_id=1, source_target_pairs={{0,1},{1,2},{2,3},{4,5},{5,6},{6,7},{8,9},{9,10},{10,11},{12,13},{... | collective-permute-start | bytes 393224 | tf_op jit(solution)/shard_map/ppermute | solution.py:328
  43.3 2.2 %collective-permute-start.11 = (bf16[128,512]{1,0:T(8,128)(2,1)S(1)}, bf16[128,512]{1,0:T(8,128)(2,1)S(1)}, u32[]{:S(2)}, u32[]{:S(2)}) collective-permute-start(bf16[128,512]{1,0:T(8,128)(2,1)S(1)} %maximum_select_fusion), channel_id=1, source_target_pairs={{0,64},{1,65},{2,66},{3,67},{4,68},{5,69},{6,70},{7,71},{8,72},{9,... | collective-permute-start | bytes 393224 | tf_op jit(solution)/shard_map/ppermute | solution.py:248
  48.5 5.5 %shard_map.259.rest_0_ = f32[256,512]{1,0:T(8,128)S(1)} custom-call(bf16[1792,512]{1,0:T(8,128)(2,1)S(1)} %get-tuple-element.85.table, bf16[1024,512]{1,0:T(8,128)(2,1)S(1)} %copy-done, s32[1024,8]{1,0:T(8,128)S(1)} %get-tuple-element.72.nbrs, bf16[1024,512]{1,0:T(8,128)(2,1)S(1)} %copy-done.2, f32[1,512]{1,0:T(1,128)S(1)} %bitcast.17, ...), custom_call_target="tpu_custom_call" | custom-call | flops 3400000000 | bytes 6000000 | tf_op jit(solution)/shard_map/pallas_call | solution.py:267
  54.1 5.5 %shard_map.260.rest_1_ = f32[256,512]{1,0:T(8,128)S(1)} custom-call(bf16[1792,512]{1,0:T(8,128)(2,1)S(1)} %get-tuple-element.85.table, bf16[1024,512]{1,0:T(8,128)(2,1)S(1)} %copy-done, s32[1024,8]{1,0:T(8,128)S(1)} %get-tuple-element.72.nbrs, bf16[1024,512]{1,0:T(8,128)(2,1)S(1)} %copy-done.2, f32[1,512]{1,0:T(1,128)S(1)} %bitcast.18, ...), custom_call_target="tpu_custom_call" | custom-call | flops 3400000000 | bytes 6000000 | tf_op jit(solution)/shard_map/pallas_call | solution.py:267
  59.9 2.5 %collective-permute-start.14 = (bf16[64,512]{1,0:T(8,128)(2,1)S(1)}, bf16[64,512]{1,0:T(8,128)(2,1)S(1)}, u32[]{:S(2)}, u32[]{:S(2)}) collective-permute-start(bf16[64,512]{1,0:T(8,128)(2,1)S(1)} %slice.13), channel_id=1, source_target_pairs={{0,192},{1,193},{2,194},{3,195},{4,196},{5,197},{6,198},{7,199},{8... | collective-permute-start | bytes 196616 | tf_op jit(solution)/shard_map/ppermute | solution.py:248
  62.4 1.6 %collective-permute-done.13 = bf16[64,512]{1,0:T(8,128)(2,1)S(1)} collective-permute-done((bf16[64,512]{1,0:T(8,128)(2,1)S(1)}, bf16[64,512]{1,0:T(8,128)(2,1)S(1)}, u32[]{:S(2)}, u32[]{:S(2)}) %collective-permute-start.13) | collective-permute-done | bytes 65568 | tf_op jit(solution)/shard_map/ppermute | solution.py:248
  66.8 3.5 %collective-permute-start.19 = (bf16[512,512]{1,0:T(8,128)(2,1)S(1)}, bf16[512,512]{1,0:T(8,128)(2,1)S(1)}, u32[]{:S(2)}, u32[]{:S(2)}) collective-permute-start(bf16[512,512]{1,0:T(8,128)(2,1)S(1)} %constant_dynamic-update-slice_fusion.m0), channel_id=1, source_target_pairs={{0,16},{1,17},{2,18},{3,19},{4,20},{5,21},{6,22},{7,23},{8,24},{9,... | collective-permute-start | bytes 1572872 | tf_op jit(solution)/shard_map/ppermute | solution.py:248
  70.4 5.5 %shard_map.261.rest_2_ = f32[256,512]{1,0:T(8,128)S(1)} custom-call(bf16[1792,512]{1,0:T(8,128)(2,1)S(1)} %get-tuple-element.85.table, bf16[1024,512]{1,0:T(8,128)(2,1)S(1)} %copy-done, s32[1024,8]{1,0:T(8,128)S(1)} %get-tuple-element.72.nbrs, bf16[1024,512]{1,0:T(8,128)(2,1)S(1)} %copy-done.2, f32[1,512]{1,0:T(1,128)S(1)} %bitcast.19, ...), custom_call_target="tpu_custom_call" | custom-call | flops 3400000000 | bytes 6000000 | tf_op jit(solution)/shard_map/pallas_call | solution.py:267
  76.0 2.2 %collective-permute-start.20 = (bf16[512,512]{1,0:T(8,128)(2,1)S(1)}, bf16[512,512]{1,0:T(8,128)(2,1)S(1)}, u32[]{:S(2)}, u32[]{:S(2)}) collective-permute-start(bf16[512,512]{1,0:T(8,128)(2,1)S(1)} %collective-permute-done.15.m1), channel_id=1, source_target_pairs={{0,16},{1,17},{2,18},{3,19},{4,20},{5,21},{6,22},{7,23},{8,24},{9,... | collective-permute-start | bytes 1572872 | tf_op jit(solution)/shard_map/ppermute | solution.py:248
  79.0 2.4 %collective-permute-start.18 = (bf16[256,512]{1,0:T(8,128)(2,1)S(1)}, bf16[256,512]{1,0:T(8,128)(2,1)S(1)}, u32[]{:S(2)}, u32[]{:S(2)}) collective-permute-start(bf16[256,512]{1,0:T(8,128)(2,1)S(1)} %slice.15), channel_id=1, source_target_pairs={{0,12},{1,13},{2,14},{3,15},{4,0},{5,1},{6,2},{7,3},{8,4},{9,5},{1... | collective-permute-start | bytes 786440 | tf_op jit(solution)/shard_map/ppermute | solution.py:248
  81.4 5.5 %shard_map.262.rest_3_ = f32[256,512]{1,0:T(8,128)S(1)} custom-call(bf16[1792,512]{1,0:T(8,128)(2,1)S(1)} %get-tuple-element.85.table, bf16[1024,512]{1,0:T(8,128)(2,1)S(1)} %copy-done, s32[1024,8]{1,0:T(8,128)S(1)} %get-tuple-element.72.nbrs, bf16[1024,512]{1,0:T(8,128)(2,1)S(1)} %copy-done.2, f32[1,512]{1,0:T(1,128)S(1)} %bitcast.20, ...), custom_call_target="tpu_custom_call" | custom-call | flops 3400000000 | bytes 6000000 | tf_op jit(solution)/shard_map/pallas_call | solution.py:267
  88.0 2.4 %shard_map.263.found = bf16[1024,512]{1,0:T(8,128)(2,1)S(1)} custom-call(s32[16,64]{1,0:T(8,128)S(1)} %get-tuple-element.49.slots, bf16[512,512]{1,0:T(8,128)(2,1)S(1)} %constant_dynamic-update-slice_fusion.m0, bf16[512,512]{1,0:T(8,128)(2,1)S(1)} %collective-permute-done.15.m1, bf16[512,512]{1,0:T(8,128)(2,1)S(1)} %collective-permute-done.16.m2, ...), custom_call_target="tpu_custom_call" | custom-call | flops 2000000000 | bytes 4000000 | tf_op jit(solution)/shard_map/pallas_call | solution.py:267
  91.5 6.9 %shard_map.264 = (bf16[1024,512]{1,0:T(8,128)(2,1)}, bf16[128,512]{1,0:T(8,128)(2,1)}, bf16[16,512]{1,0:T(8,128)(2,1)}) custom-call(bf16[1024,512]{1,0:T(8,128)(2,1)} %copy-done.1, bf16[512,512]{1,0:T(8,128)(2,1)S(1)} %collective-permute-done.19.o0, bf16[512,512]{1,0:T(8,128)(2,1)S(1)} %collective-permute-done.20.o1, ...), custom_call_target="tpu_custom_call" | custom-call | tf_op jit(solution)/shard_map/pallas_call | solution.py:267
  (78 shorter events, 12.7 us)
Async XLA Ops:
  2.9 7.2 %collective-permute-start = (bf16[16,512]{1,0:T(8,128)(2,1)S(1)}, bf16[16,512]{1,0:T(8,128)(2,1)S(1)}, u32[]{:S(2)}, u32[]{:S(2)}) collective-permute-start(bf16[16,512]{1,0:T(8,128)(2,1)S(1)} %get-tuple-element.52), channel_id=1, source_target_pairs={{0,16},{1,17},{2,18},{3,19},{4,20},{5,21},{6,22},{7,23},{8,24},{9,... | collective-permute-start | bytes 49160 | tf_op jit(solution)/shard_map/ppermute | solution.py:248
  10.1 8.1 %collective-permute-start.1 = (bf16[32,512]{1,0:T(8,128)(2,1)S(1)}, bf16[32,512]{1,0:T(8,128)(2,1)S(1)}, u32[]{:S(2)}, u32[]{:S(2)}) collective-permute-start(bf16[32,512]{1,0:T(8,128)(2,1)S(1)} %maximum_select_fusion.1), channel_id=1, source_target_pairs={{0,1},{1,2},{2,3},{3,32},{4,5},{5,6},{6,7},{7,36},{8,9},{9,10},{10... | collective-permute-start | bytes 98312 | tf_op jit(solution)/shard_map/ppermute | solution.py:248
  14.0 23.9 %collective-permute-start.5 = (bf16[1,128,512]{2,1,0:T(8,128)(2,1)S(1)}, bf16[1,128,512]{2,1,0:T(8,128)(2,1)S(1)}, u32[]{:S(2)}, u32[]{:S(2)}) collective-permute-start(bf16[1,128,512]{2,1,0:T(8,128)(2,1)S(1)} %get-tuple-element.64), channel_id=1, source_target_pairs={{0,16},{16,32},{32,48},{48,64},{64,80},{80,96},{96,112},{112,128},... | collective-permute-start | bytes 393224 | tf_op jit(solution)/shard_map/ppermute | solution.py:328
  18.2 4.8 %collective-permute-start.2 = (bf16[32,512]{1,0:T(8,128)(2,1)S(1)}, bf16[32,512]{1,0:T(8,128)(2,1)S(1)}, u32[]{:S(2)}, u32[]{:S(2)}) collective-permute-start(bf16[32,512]{1,0:T(8,128)(2,1)S(1)} %collective-permute-done.1), channel_id=1, source_target_pairs={{0,1},{1,2},{2,3},{3,32},{4,5},{5,6},{6,7},{7,36},{8,9},{9,10},{10... | collective-permute-start | bytes 98312 | tf_op jit(solution)/shard_map/ppermute | solution.py:248
  23.1 3.6 %collective-permute-start.3 = (bf16[32,512]{1,0:T(8,128)(2,1)S(1)}, bf16[32,512]{1,0:T(8,128)(2,1)S(1)}, u32[]{:S(2)}, u32[]{:S(2)}) collective-permute-start(bf16[32,512]{1,0:T(8,128)(2,1)S(1)} %collective-permute-done.2), channel_id=1, source_target_pairs={{0,1},{1,2},{2,3},{3,32},{4,5},{5,6},{6,7},{7,36},{8,9},{9,10},{10... | collective-permute-start | bytes 98312 | tf_op jit(solution)/shard_map/ppermute | solution.py:248
  26.6 12.6 %collective-permute-start.4 = (bf16[32,512]{1,0:T(8,128)(2,1)S(1)}, bf16[32,512]{1,0:T(8,128)(2,1)S(1)}, u32[]{:S(2)}, u32[]{:S(2)}) collective-permute-start(bf16[32,512]{1,0:T(8,128)(2,1)S(1)} %collective-permute-done.3), channel_id=1, source_target_pairs={{16,51},{17,16},{18,17},{19,18},{20,55},{21,20},{22,21},{23,22},{2... | collective-permute-start | bytes 98312 | tf_op jit(solution)/shard_map/ppermute | solution.py:248
  31.5 11.8 %collective-permute-start.6 = (bf16[1,128,512]{2,1,0:T(8,128)(2,1)S(1)}, bf16[1,128,512]{2,1,0:T(8,128)(2,1)S(1)}, u32[]{:S(2)}, u32[]{:S(2)}) collective-permute-start(bf16[1,128,512]{2,1,0:T(8,128)(2,1)S(1)} %get-tuple-element.65), channel_id=1, source_target_pairs={{16,0},{32,16},{48,32},{64,48},{80,64},{96,80},{112,96},{128,112},... | collective-permute-start | bytes 393224 | tf_op jit(solution)/shard_map/ppermute | solution.py:328
  33.4 12.1 %collective-permute-start.7 = (bf16[1,128,512]{2,1,0:T(8,128)(2,1)S(1)}, bf16[1,128,512]{2,1,0:T(8,128)(2,1)S(1)}, u32[]{:S(2)}, u32[]{:S(2)}) collective-permute-start(bf16[1,128,512]{2,1,0:T(8,128)(2,1)S(1)} %get-tuple-element.66), channel_id=1, source_target_pairs={{0,4},{4,8},{8,12},{1,5},{5,9},{9,13},{2,6},{6,10},{10,14},{3,7},{... | collective-permute-start | bytes 393224 | tf_op jit(solution)/shard_map/ppermute | solution.py:328
  36.6 10.4 %collective-permute-start.8 = (bf16[1,128,512]{2,1,0:T(8,128)(2,1)S(1)}, bf16[1,128,512]{2,1,0:T(8,128)(2,1)S(1)}, u32[]{:S(2)}, u32[]{:S(2)}) collective-permute-start(bf16[1,128,512]{2,1,0:T(8,128)(2,1)S(1)} %get-tuple-element.67), channel_id=1, source_target_pairs={{4,0},{8,4},{12,8},{5,1},{9,5},{13,9},{6,2},{10,6},{14,10},{7,3},{... | collective-permute-start | bytes 393224 | tf_op jit(solution)/shard_map/ppermute | solution.py:328
  38.0 9.1 %collective-permute-start.10 = (bf16[1,128,512]{2,1,0:T(8,128)(2,1)S(1)}, bf16[1,128,512]{2,1,0:T(8,128)(2,1)S(1)}, u32[]{:S(2)}, u32[]{:S(2)}) collective-permute-start(bf16[1,128,512]{2,1,0:T(8,128)(2,1)S(1)} %get-tuple-element.69), channel_id=1, source_target_pairs={{1,0},{2,1},{3,2},{5,4},{6,5},{7,6},{9,8},{10,9},{11,10},{13,12},{... | collective-permute-start | bytes 393224 | tf_op jit(solution)/shard_map/ppermute | solution.py:328
  39.3 7.8 %collective-permute-start.9 = (bf16[1,128,512]{2,1,0:T(8,128)(2,1)S(1)}, bf16[1,128,512]{2,1,0:T(8,128)(2,1)S(1)}, u32[]{:S(2)}, u32[]{:S(2)}) collective-permute-start(bf16[1,128,512]{2,1,0:T(8,128)(2,1)S(1)} %get-tuple-element.68), channel_id=1, source_target_pairs={{0,1},{1,2},{2,3},{4,5},{5,6},{6,7},{8,9},{9,10},{10,11},{12,13},{... | collective-permute-start | bytes 393224 | tf_op jit(solution)/shard_map/ppermute | solution.py:328
  43.3 10.7 %collective-permute-start.11 = (bf16[128,512]{1,0:T(8,128)(2,1)S(1)}, bf16[128,512]{1,0:T(8,128)(2,1)S(1)}, u32[]{:S(2)}, u32[]{:S(2)}) collective-permute-start(bf16[128,512]{1,0:T(8,128)(2,1)S(1)} %maximum_select_fusion), channel_id=1, source_target_pairs={{0,64},{1,65},{2,66},{3,67},{4,68},{5,69},{6,70},{7,71},{8,72},{9,... | collective-permute-start | bytes 393224 | tf_op jit(solution)/shard_map/ppermute | solution.py:248
  45.5 8.6 %collective-permute-start.12 = (bf16[128,512]{1,0:T(8,128)(2,1)S(1)}, bf16[128,512]{1,0:T(8,128)(2,1)S(1)}, u32[]{:S(2)}, u32[]{:S(2)}) collective-permute-start(bf16[128,512]{1,0:T(8,128)(2,1)S(1)} %maximum_select_fusion), channel_id=1, source_target_pairs={{0,192},{1,193},{2,194},{3,195},{4,196},{5,197},{6,198},{7,199},{8... | collective-permute-start | bytes 393224 | tf_op jit(solution)/shard_map/ppermute | solution.py:248
  59.6 4.4 %collective-permute-start.13 = (bf16[64,512]{1,0:T(8,128)(2,1)S(1)}, bf16[64,512]{1,0:T(8,128)(2,1)S(1)}, u32[]{:S(2)}, u32[]{:S(2)}) collective-permute-start(bf16[64,512]{1,0:T(8,128)(2,1)S(1)} %slice.12), channel_id=1, source_target_pairs={{0,64},{1,65},{2,66},{3,67},{4,68},{5,69},{6,70},{7,71},{8,72},{9,... | collective-permute-start | bytes 196616 | tf_op jit(solution)/shard_map/ppermute | solution.py:248
  59.9 4.1 %collective-permute-start.14 = (bf16[64,512]{1,0:T(8,128)(2,1)S(1)}, bf16[64,512]{1,0:T(8,128)(2,1)S(1)}, u32[]{:S(2)}, u32[]{:S(2)}) collective-permute-start(bf16[64,512]{1,0:T(8,128)(2,1)S(1)} %slice.13), channel_id=1, source_target_pairs={{0,192},{1,193},{2,194},{3,195},{4,196},{5,197},{6,198},{7,199},{8... | collective-permute-start | bytes 196616 | tf_op jit(solution)/shard_map/ppermute | solution.py:248
  64.1 11.8 %collective-permute-start.15 = (bf16[512,512]{1,0:T(8,128)(2,1)S(1)}, bf16[512,512]{1,0:T(8,128)(2,1)S(1)}, u32[]{:S(2)}, u32[]{:S(2)}) collective-permute-start(bf16[512,512]{1,0:T(8,128)(2,1)S(1)} %constant_dynamic-update-slice_fusion.m0), channel_id=1, source_target_pairs={{0,4},{1,5},{2,6},{3,7},{4,8},{5,9},{6,10},{7,11},{8,12},{9,13},{1... | collective-permute-start | bytes 1572872 | tf_op jit(solution)/shard_map/ppermute | solution.py:248
  65.4 10.6 %collective-permute-start.16 = (bf16[512,512]{1,0:T(8,128)(2,1)S(1)}, bf16[512,512]{1,0:T(8,128)(2,1)S(1)}, u32[]{:S(2)}, u32[]{:S(2)}) collective-permute-start(bf16[512,512]{1,0:T(8,128)(2,1)S(1)} %constant_dynamic-update-slice_fusion.m0), channel_id=1, source_target_pairs={{0,12},{1,13},{2,14},{3,15},{4,0},{5,1},{6,2},{7,3},{8,4},{9,5},{1... | collective-permute-start | bytes 1572872 | tf_op jit(solution)/shard_map/ppermute | solution.py:248
  66.8 24.5 %collective-permute-start.19 = (bf16[512,512]{1,0:T(8,128)(2,1)S(1)}, bf16[512,512]{1,0:T(8,128)(2,1)S(1)}, u32[]{:S(2)}, u32[]{:S(2)}) collective-permute-start(bf16[512,512]{1,0:T(8,128)(2,1)S(1)} %constant_dynamic-update-slice_fusion.m0), channel_id=1, source_target_pairs={{0,16},{1,17},{2,18},{3,19},{4,20},{5,21},{6,22},{7,23},{8,24},{9,... | collective-permute-start | bytes 1572872 | tf_op jit(solution)/shard_map/ppermute | solution.py:248
  76.0 15.4 %collective-permute-start.20 = (bf16[512,512]{1,0:T(8,128)(2,1)S(1)}, bf16[512,512]{1,0:T(8,128)(2,1)S(1)}, u32[]{:S(2)}, u32[]{:S(2)}) collective-permute-start(bf16[512,512]{1,0:T(8,128)(2,1)S(1)} %collective-permute-done.15.m1), channel_id=1, source_target_pairs={{0,16},{1,17},{2,18},{3,19},{4,20},{5,21},{6,22},{7,23},{8,24},{9,... | collective-permute-start | bytes 1572872 | tf_op jit(solution)/shard_map/ppermute | solution.py:248
  78.2 13.2 %collective-permute-start.21 = (bf16[512,512]{1,0:T(8,128)(2,1)S(1)}, bf16[512,512]{1,0:T(8,128)(2,1)S(1)}, u32[]{:S(2)}, u32[]{:S(2)}) collective-permute-start(bf16[512,512]{1,0:T(8,128)(2,1)S(1)} %collective-permute-done.16.m2), channel_id=1, source_target_pairs={{0,16},{1,17},{2,18},{3,19},{4,20},{5,21},{6,22},{7,23},{8,24},{9,... | collective-permute-start | bytes 1572872 | tf_op jit(solution)/shard_map/ppermute | solution.py:248
  78.3 8.7 %collective-permute-start.17 = (bf16[256,512]{1,0:T(8,128)(2,1)S(1)}, bf16[256,512]{1,0:T(8,128)(2,1)S(1)}, u32[]{:S(2)}, u32[]{:S(2)}) collective-permute-start(bf16[256,512]{1,0:T(8,128)(2,1)S(1)} %slice.14), channel_id=1, source_target_pairs={{0,4},{1,5},{2,6},{3,7},{4,8},{5,9},{6,10},{7,11},{8,12},{9,13},{1... | collective-permute-start | bytes 786440 | tf_op jit(solution)/shard_map/ppermute | solution.py:248
  79.0 7.9 %collective-permute-start.18 = (bf16[256,512]{1,0:T(8,128)(2,1)S(1)}, bf16[256,512]{1,0:T(8,128)(2,1)S(1)}, u32[]{:S(2)}, u32[]{:S(2)}) collective-permute-start(bf16[256,512]{1,0:T(8,128)(2,1)S(1)} %slice.15), channel_id=1, source_target_pairs={{0,12},{1,13},{2,14},{3,15},{4,0},{5,1},{6,2},{7,3},{8,4},{9,5},{1... | collective-permute-start | bytes 786440 | tf_op jit(solution)/shard_map/ppermute | solution.py:248
  86.9 4.4 %collective-permute-start.22 = (bf16[256,512]{1,0:T(8,128)(2,1)S(1)}, bf16[256,512]{1,0:T(8,128)(2,1)S(1)}, u32[]{:S(2)}, u32[]{:S(2)}) collective-permute-start(bf16[256,512]{1,0:T(8,128)(2,1)S(1)} %collective-permute-done.17.m3), channel_id=1, source_target_pairs={{0,16},{1,17},{2,18},{3,19},{4,20},{5,21},{6,22},{7,23},{8,24},{9,... | collective-permute-start | bytes 786440 | tf_op jit(solution)/shard_map/ppermute | solution.py:248
  87.6 3.7 %collective-permute-start.23 = (bf16[256,512]{1,0:T(8,128)(2,1)S(1)}, bf16[256,512]{1,0:T(8,128)(2,1)S(1)}, u32[]{:S(2)}, u32[]{:S(2)}) collective-permute-start(bf16[256,512]{1,0:T(8,128)(2,1)S(1)} %collective-permute-done.18.m4), channel_id=1, source_target_pairs={{0,16},{1,17},{2,18},{3,19},{4,20},{5,21},{6,22},{7,23},{8,24},{9,... | collective-permute-start | bytes 786440 | tf_op jit(solution)/shard_map/ppermute | solution.py:248
  (17 other events, 386.3 us)

commit v3 on v2

--- a/solution.py
+++ b/solution.py
@@ -47,8 +47,8 @@
 
 
 SWAP = permutation(lambda x, zh, c, y, z: (x, zh, 1 - c, y, z))
-RING = permutation(lambda x, zh, c, y, z: along_z(x, zh, c, y, z, 1 if c == 0 else -1))
-RING_END = permutation(lambda x, zh, c, y, z: along_z(x, zh, c, y, z, -1) if c == 1 else None)
+UP_Z = permutation(functools.partial(along_z, step=1))
+DOWN_Z = permutation(functools.partial(along_z, step=-1))
 UP_FIRST = permutation(functools.partial(along_plane, step=1, first=True))
 DOWN_FIRST = permutation(functools.partial(along_plane, step=-1, first=True))
 UP_SECOND = permutation(functools.partial(along_plane, step=1, first=False))
@@ -107,8 +107,8 @@
     zh = (owner >> 5) & 1
     x = owner >> 6
     back = (here["zh"] * 4 + here["z"] - zh * 4 - z) & 7
-    stream = (back > 3).astype(jnp.int32)
-    at = jnp.where(stream == 0, back, 7 - back) * 32 + c * 16 + row
+    stream = c
+    at = jnp.where(back <= 4, back, 12 - back) * 16 + row
     step_x = (here["x"] - x) & 3
     step_y = (here["y"] - y) & 3
     order_x = jnp.where(step_x == 2, 3, jnp.where(step_x == 3, 2, step_x))
@@ -321,27 +321,27 @@
         ],
     )
 
-    def faced(block, face):
-        axes = (("x", "zh", "c"), "y", "z")[face // 2]
+    def faced(face):
+        axes = (("x", "zh", "c"), "y")[face // 2]
         count = lax.axis_size(axes)
         pairs = [(k, k + 1) for k in range(count - 1)]
-        return lax.ppermute(block, axes, [(b, a) for a, b in pairs] if face % 2 == 0 else pairs)
-
-    core = lax.axis_index("c")
-    beside = sent(sender, SWAP)
-    chip = jnp.where(core == 0, joined(sender, beside), joined(beside, sender))
-    ring = [chip]
-    ghosts = {}
-    for hop, group in enumerate(((1,), (0,), (3, 2), (5, 4))):
-        carried = ring[-1]
-        blocks = [faces[face] for face in group]
-        carried, *blocks = tied((carried, *blocks))
-        ring.append(sent(carried, RING if hop < 3 else RING_END))
-        for face, block in zip(group, blocks):
-            ghosts[face] = faced(block, face)
-    last = ring.pop()
-    column = jnp.where(core == 0, joined(*ring), joined(*ring[1:], last))
-    near_faces = [ghosts[face] for face in (1, 0, 3, 2, 5, 4)]
+        return lax.ppermute(faces[face], axes, [(b, a) for a, b in pairs] if face % 2 == 0 else pairs)
+
+    ups, downs = [sent(sender, UP_Z)], [sent(sender, DOWN_Z)]
+    up, down, faces[5], faces[4], faces[1] = tied((ups[-1], downs[-1], faces[5], faces[4], faces[1]))
+    ups.append(sent(up, UP_Z))
+    downs.append(sent(down, DOWN_Z))
+    low_x, low_z, high_z = faced(1), sent(faces[5], UP_Z), sent(faces[4], DOWN_Z)
+    up, down, faces[0] = tied((ups[-1], downs[-1], faces[0]))
+    ups.append(sent(up, UP_Z))
+    downs.append(sent(down, DOWN_Z))
+    high_x = faced(0)
+    up, down, faces[3], faces[2], low_x = tied((ups[-1], downs[-1], faces[3], faces[2], low_x))
+    ups.append(sent(up, UP_Z))
+    low_y, high_y = faced(3), faced(2)
+    last, high_x = tied((ups[-1], high_x))
+    column = joined(sender, *ups[:3], last, *downs)
+    near_faces = [low_x, high_x, low_y, high_y, low_z, high_z]
     fine_sender, column = tied((fine_sender, column))
     table, near = kernel(
         table_kernel,

time: 98.7 us -> 95.1 us (0.964)
  starting transfers between devices: 52.6 us -> 48.5 us
    ppermute x18 -> x22, starting transfers between devices: 36.7 us -> 34.6 us  [sent(): return lax.ppermute(rows, AXES, pairs)]
    ppermute x6 -> x4, starting transfers between devices: 15.9 us -> 13.9 us  [faced(): lax.ppermute(faces[face], axes, [(b, a) for a, b in pairs] if face % 2 ==...]
    ppermute x18 -> x22, waiting for transfers between devices: 4.56 us -> 5.14 us  [sent(): return lax.ppermute(rows, AXES, pairs)]
  transfers between devices with their start and end apart: 24 -> 26, of which waited for: 3 -> 3; matrix products, arithmetic and copies ran while one was open for 0% -> 0% of each run, Pallas kernels for 25% -> 25%
where the time goes in v3:
time: 95.1 us; the launch traced here: 94.9 us
  starting transfers between devices  48.5 us (51%)
  Pallas kernels  38.9 us (41%)
  waiting for transfers between devices  5.15 us (5%)
  between operations  1.2 us (1%)
  local copies, waits for them, and re-layouts  1.19 us (1%)
    pallas_call x9, Pallas kernels, kernel(): pl.pallas_call(body, grid=(1,), out_shape=outs, in_specs=specs, out_specs...  38.9 us
    ppermute x22, starting transfers between devices, sent(): return lax.ppermute(rows, AXES, pairs)  34.6 us
    ppermute x4, starting transfers between devices, faced(): lax.ppermute(faces[face], axes, [(b, a) for a, b in pairs] if face % 2 ==...  13.9 us
    ppermute x22, waiting for transfers between devices, sent(): return lax.ppermute(rows, AXES, pairs)  5.14 us
  transfers between devices with their start and end apart: 26, of which 3 were waited for; matrix products, arithmetic and copies ran while one was open for 0% of the time, Pallas kernels for 25%

profile of v3, /device:TPU:1, one launch (start us, length us, event | category | flops | bytes accessed | tf_op | source)
XLA Modules:
  0.0 94.9 jit_solution(12336720499532819137)
XLA Ops:
  0.6 2.3 %shard_map.256 = (bf16[16,512]{1,0:T(8,128)(2,1)S(1)}, bf16[16,512]{1,0:T(8,128)(2,1)S(1)}, f32[128,512]{1,0:T(8,128)S(1)}, s32[16,64]{1,0:T(8,128)S(1)}, bf16[3...) custom-call(bf16[1024,512]{1,0:T(8,128)(2,1)} %fine.7, s32[1,1024]{1,0:T(1,128)} %bitcast.33, ...), custom_call_target="tpu_custom_call" | custom-call | tf_op jit(solution)/shard_map/pallas_call | solution.py:267
  2.9 2.5 %collective-permute-start = (bf16[16,512]{1,0:T(8,128)(2,1)S(1)}, bf16[16,512]{1,0:T(8,128)(2,1)S(1)}, u32[]{:S(2)}, u32[]{:S(2)}) collective-permute-start(bf16[16,512]{1,0:T(8,128)(2,1)S(1)} %get-tuple-element.56), channel_id=1, source_target_pairs={{0,1},{1,2},{2,3},{3,32},{4,5},{5,6},{6,7},{7,36},{8,9},{9,10},{10... | collective-permute-start | bytes 49160 | tf_op jit(solution)/shard_map/ppermute | solution.py:248
  5.5 4.0 %collective-permute-start.1 = (bf16[16,512]{1,0:T(8,128)(2,1)S(1)}, bf16[16,512]{1,0:T(8,128)(2,1)S(1)}, u32[]{:S(2)}, u32[]{:S(2)}) collective-permute-start(bf16[16,512]{1,0:T(8,128)(2,1)S(1)} %get-tuple-element.56), channel_id=1, source_target_pairs={{0,35},{1,0},{2,1},{3,2},{4,39},{5,4},{6,5},{7,6},{8,43},{9,8},{10... | collective-permute-start | bytes 49160 | tf_op jit(solution)/shard_map/ppermute | solution.py:248
  9.5 3.8 %shard_map.257 = (bf16[1024,512]{1,0:T(8,128)(2,1)S(1)}, bf16[512,512]{1,0:T(8,128)(2,1)S(1)}, bf16[1,128,512]{2,1,0:T(8,128)(2,1)S(1)}, bf16[1,128,512]{2,1,0:T...) custom-call(bf16[32,128]{1,0:T(8,128)(2,1)S(1)} %get-tuple-element.5, ...), custom_call_target="tpu_custom_call" | custom-call | tf_op jit(solution)/shard_map/pallas_call | solution.py:267
  13.5 2.7 %collective-permute-start.3 = (bf16[16,512]{1,0:T(8,128)(2,1)S(1)}, bf16[16,512]{1,0:T(8,128)(2,1)S(1)}, u32[]{:S(2)}, u32[]{:S(2)}) collective-permute-start(bf16[16,512]{1,0:T(8,128)(2,1)S(1)} %collective-permute-done.1), channel_id=1, source_target_pairs={{0,35},{1,0},{2,1},{3,2},{4,39},{5,4},{6,5},{7,6},{8,43},{9,8},{10... | collective-permute-start | bytes 49160 | tf_op jit(solution)/shard_map/ppermute | solution.py:248
  16.1 7.5 %collective-permute-start.6 = (bf16[1,128,512]{2,1,0:T(8,128)(2,1)S(1)}, bf16[1,128,512]{2,1,0:T(8,128)(2,1)S(1)}, u32[]{:S(2)}, u32[]{:S(2)}) collective-permute-start(bf16[1,128,512]{2,1,0:T(8,128)(2,1)S(1)} %get-tuple-element.67), channel_id=1, source_target_pairs={{0,16},{16,32},{32,48},{48,64},{64,80},{80,96},{96,112},{112,128},... | collective-permute-start | bytes 393224 | tf_op jit(solution)/shard_map/ppermute | solution.py:328
  23.9 2.7 %collective-permute-start.5 = (bf16[16,512]{1,0:T(8,128)(2,1)S(1)}, bf16[16,512]{1,0:T(8,128)(2,1)S(1)}, u32[]{:S(2)}, u32[]{:S(2)}) collective-permute-start(bf16[16,512]{1,0:T(8,128)(2,1)S(1)} %collective-permute-done.3), channel_id=1, source_target_pairs={{0,35},{1,0},{2,1},{3,2},{4,39},{5,4},{6,5},{7,6},{8,43},{9,8},{10... | collective-permute-start | bytes 49160 | tf_op jit(solution)/shard_map/ppermute | solution.py:248
  26.6 1.9 %collective-permute-start.8 = (bf16[1,128,512]{2,1,0:T(8,128)(2,1)S(1)}, bf16[1,128,512]{2,1,0:T(8,128)(2,1)S(1)}, u32[]{:S(2)}, u32[]{:S(2)}) collective-permute-start(bf16[1,128,512]{2,1,0:T(8,128)(2,1)S(1)} %get-tuple-element.69), channel_id=1, source_target_pairs={{16,0},{32,16},{48,32},{64,48},{80,64},{96,80},{112,96},{128,112},... | collective-permute-start | bytes 393224 | tf_op jit(solution)/shard_map/ppermute | solution.py:328
  28.5 1.6 %collective-permute-done.4 = bf16[16,512]{1,0:T(8,128)(2,1)S(1)} collective-permute-done((bf16[16,512]{1,0:T(8,128)(2,1)S(1)}, bf16[16,512]{1,0:T(8,128)(2,1)S(1)}, u32[]{:S(2)}, u32[]{:S(2)}) %collective-permute-start.4) | collective-permute-done | bytes 16416 | tf_op jit(solution)/shard_map/ppermute | solution.py:248
  32.9 1.8 %collective-permute-done.7 = bf16[16,512]{1,0:T(8,128)(2,1)S(1)} collective-permute-done((bf16[16,512]{1,0:T(8,128)(2,1)S(1)}, bf16[16,512]{1,0:T(8,128)(2,1)S(1)}, u32[]{:S(2)}, u32[]{:S(2)}) %collective-permute-start.7) | collective-permute-done | bytes 16416 | tf_op jit(solution)/shard_map/ppermute | solution.py:248
  34.7 3.2 %collective-permute-start.9 = (bf16[1,128,512]{2,1,0:T(8,128)(2,1)S(1)}, bf16[1,128,512]{2,1,0:T(8,128)(2,1)S(1)}, u32[]{:S(2)}, u32[]{:S(2)}) collective-permute-start(bf16[1,128,512]{2,1,0:T(8,128)(2,1)S(1)} %get-tuple-element.74), channel_id=1, source_target_pairs={{0,4},{4,8},{8,12},{1,5},{5,9},{9,13},{2,6},{6,10},{10,14},{3,7},{... | collective-permute-start | bytes 393224 | tf_op jit(solution)/shard_map/ppermute | solution.py:328
  39.4 1.6 %collective-permute-start.14 = (bf16[128,512]{1,0:T(8,128)(2,1)S(1)}, bf16[128,512]{1,0:T(8,128)(2,1)S(1)}, u32[]{:S(2)}, u32[]{:S(2)}) collective-permute-start(bf16[128,512]{1,0:T(8,128)(2,1)S(1)} %constant_dynamic-update-slice_fusion), channel_id=1, source_target_pairs={{0,192},{1,193},{2,194},{3,195},{4,196},{5,197},{6,198},{7,199},{8... | collective-permute-start | bytes 393224 | tf_op jit(solution)/shard_map/ppermute | solution.py:248
  42.5 5.5 %shard_map.259.rest_0_ = f32[256,512]{1,0:T(8,128)S(1)} custom-call(bf16[1792,512]{1,0:T(8,128)(2,1)S(1)} %get-tuple-element.93.table, bf16[1024,512]{1,0:T(8,128)(2,1)S(1)} %copy-done, s32[1024,8]{1,0:T(8,128)S(1)} %get-tuple-element.80.nbrs, bf16[1024,512]{1,0:T(8,128)(2,1)S(1)} %copy-done.2, f32[1,512]{1,0:T(1,128)S(1)} %bitcast.17, ...), custom_call_target="tpu_custom_call" | custom-call | flops 3400000000 | bytes 6000000 | tf_op jit(solution)/shard_map/pallas_call | solution.py:267
  48.1 5.5 %shard_map.260.rest_1_ = f32[256,512]{1,0:T(8,128)S(1)} custom-call(bf16[1792,512]{1,0:T(8,128)(2,1)S(1)} %get-tuple-element.93.table, bf16[1024,512]{1,0:T(8,128)(2,1)S(1)} %copy-done, s32[1024,8]{1,0:T(8,128)S(1)} %get-tuple-element.80.nbrs, bf16[1024,512]{1,0:T(8,128)(2,1)S(1)} %copy-done.2, f32[1,512]{1,0:T(1,128)S(1)} %bitcast.18, ...), custom_call_target="tpu_custom_call" | custom-call | flops 3400000000 | bytes 6000000 | tf_op jit(solution)/shard_map/pallas_call | solution.py:267
  54.4 2.0 %collective-permute-start.16 = (bf16[64,512]{1,0:T(8,128)(2,1)S(1)}, bf16[64,512]{1,0:T(8,128)(2,1)S(1)}, u32[]{:S(2)}, u32[]{:S(2)}) collective-permute-start(bf16[64,512]{1,0:T(8,128)(2,1)S(1)} %slice.13), channel_id=1, source_target_pairs={{0,192},{1,193},{2,194},{3,195},{4,196},{5,197},{6,198},{7,199},{8... | collective-permute-start | bytes 196616 | tf_op jit(solution)/shard_map/ppermute | solution.py:248
  56.5 1.6 %collective-permute-done.15 = bf16[64,512]{1,0:T(8,128)(2,1)S(1)} collective-permute-done((bf16[64,512]{1,0:T(8,128)(2,1)S(1)}, bf16[64,512]{1,0:T(8,128)(2,1)S(1)}, u32[]{:S(2)}, u32[]{:S(2)}) %collective-permute-start.15) | collective-permute-done | bytes 65568 | tf_op jit(solution)/shard_map/ppermute | solution.py:248
  58.1 1.7 %collective-permute-start.17 = (bf16[512,512]{1,0:T(8,128)(2,1)S(1)}, bf16[512,512]{1,0:T(8,128)(2,1)S(1)}, u32[]{:S(2)}, u32[]{:S(2)}) collective-permute-start(bf16[512,512]{1,0:T(8,128)(2,1)S(1)} %constant_dynamic-update-slice_fusion.8.m0), channel_id=1, source_target_pairs={{0,4},{1,5},{2,6},{3,7},{4,8},{5,9},{6,10},{7,11},{8,12},{9,13},{1... | collective-permute-start | bytes 1572872 | tf_op jit(solution)/shard_map/ppermute | solution.py:248
  61.1 5.9 %collective-permute-start.21 = (bf16[512,512]{1,0:T(8,128)(2,1)S(1)}, bf16[512,512]{1,0:T(8,128)(2,1)S(1)}, u32[]{:S(2)}, u32[]{:S(2)}) collective-permute-start(bf16[512,512]{1,0:T(8,128)(2,1)S(1)} %constant_dynamic-update-slice_fusion.8.m0), channel_id=1, source_target_pairs={{0,16},{1,17},{2,18},{3,19},{4,20},{5,21},{6,22},{7,23},{8,24},{9,... | collective-permute-start | bytes 1572872 | tf_op jit(solution)/shard_map/ppermute | solution.py:248
  67.0 5.5 %shard_map.261.rest_2_ = f32[256,512]{1,0:T(8,128)S(1)} custom-call(bf16[1792,512]{1,0:T(8,128)(2,1)S(1)} %get-tuple-element.93.table, bf16[1024,512]{1,0:T(8,128)(2,1)S(1)} %copy-done, s32[1024,8]{1,0:T(8,128)S(1)} %get-tuple-element.80.nbrs, bf16[1024,512]{1,0:T(8,128)(2,1)S(1)} %copy-done.2, f32[1,512]{1,0:T(1,128)S(1)} %bitcast.19, ...), custom_call_target="tpu_custom_call" | custom-call | flops 3400000000 | bytes 6000000 | tf_op jit(solution)/shard_map/pallas_call | solution.py:267
  72.6 2.2 %collective-permute-start.22 = (bf16[512,512]{1,0:T(8,128)(2,1)S(1)}, bf16[512,512]{1,0:T(8,128)(2,1)S(1)}, u32[]{:S(2)}, u32[]{:S(2)}) collective-permute-start(bf16[512,512]{1,0:T(8,128)(2,1)S(1)} %collective-permute-done.17.m1), channel_id=1, source_target_pairs={{0,16},{1,17},{2,18},{3,19},{4,20},{5,21},{6,22},{7,23},{8,24},{9,... | collective-permute-start | bytes 1572872 | tf_op jit(solution)/shard_map/ppermute | solution.py:248
  75.9 2.4 %collective-permute-start.20 = (bf16[256,512]{1,0:T(8,128)(2,1)S(1)}, bf16[256,512]{1,0:T(8,128)(2,1)S(1)}, u32[]{:S(2)}, u32[]{:S(2)}) collective-permute-start(bf16[256,512]{1,0:T(8,128)(2,1)S(1)} %slice.15), channel_id=1, source_target_pairs={{0,12},{1,13},{2,14},{3,15},{4,0},{5,1},{6,2},{7,3},{8,4},{9,5},{1... | collective-permute-start | bytes 786440 | tf_op jit(solution)/shard_map/ppermute | solution.py:248
  78.3 5.5 %shard_map.262.rest_3_ = f32[256,512]{1,0:T(8,128)S(1)} custom-call(bf16[1792,512]{1,0:T(8,128)(2,1)S(1)} %get-tuple-element.93.table, bf16[1024,512]{1,0:T(8,128)(2,1)S(1)} %copy-done, s32[1024,8]{1,0:T(8,128)S(1)} %get-tuple-element.80.nbrs, bf16[1024,512]{1,0:T(8,128)(2,1)S(1)} %copy-done.2, f32[1,512]{1,0:T(1,128)S(1)} %bitcast.20, ...), custom_call_target="tpu_custom_call" | custom-call | flops 3400000000 | bytes 6000000 | tf_op jit(solution)/shard_map/pallas_call | solution.py:267
  84.5 2.4 %shard_map.263.found = bf16[1024,512]{1,0:T(8,128)(2,1)S(1)} custom-call(s32[16,64]{1,0:T(8,128)S(1)} %get-tuple-element.53.slots, bf16[512,512]{1,0:T(8,128)(2,1)S(1)} %constant_dynamic-update-slice_fusion.8.m0, bf16[512,512]{1,0:T(8,128)(2,1)S(1)} %collective-permute-done.17.m1, bf16[512,512]{1,0:T(8,128)(2,1)S(1)} %collective-permute-done.18.m2, ...), custom_call_target="tpu_custom_call" | custom-call | flops 2000000000 | bytes 4000000 | tf_op jit(solution)/shard_map/pallas_call | solution.py:267
  87.9 6.9 %shard_map.264 = (bf16[1024,512]{1,0:T(8,128)(2,1)}, bf16[128,512]{1,0:T(8,128)(2,1)}, bf16[16,512]{1,0:T(8,128)(2,1)}) custom-call(bf16[1024,512]{1,0:T(8,128)(2,1)} %copy-done.1, bf16[512,512]{1,0:T(8,128)(2,1)S(1)} %collective-permute-done.21.o0, bf16[512,512]{1,0:T(8,128)(2,1)S(1)} %collective-permute-done.22.o1, ...), custom_call_target="tpu_custom_call" | custom-call | tf_op jit(solution)/shard_map/pallas_call | solution.py:267
  (88 shorter events, 10.7 us)
Async XLA Ops:
  2.9 10.4 %collective-permute-start = (bf16[16,512]{1,0:T(8,128)(2,1)S(1)}, bf16[16,512]{1,0:T(8,128)(2,1)S(1)}, u32[]{:S(2)}, u32[]{:S(2)}) collective-permute-start(bf16[16,512]{1,0:T(8,128)(2,1)S(1)} %get-tuple-element.56), channel_id=1, source_target_pairs={{0,1},{1,2},{2,3},{3,32},{4,5},{5,6},{6,7},{7,36},{8,9},{9,10},{10... | collective-permute-start | bytes 49160 | tf_op jit(solution)/shard_map/ppermute | solution.py:248
  5.5 7.9 %collective-permute-start.1 = (bf16[16,512]{1,0:T(8,128)(2,1)S(1)}, bf16[16,512]{1,0:T(8,128)(2,1)S(1)}, u32[]{:S(2)}, u32[]{:S(2)}) collective-permute-start(bf16[16,512]{1,0:T(8,128)(2,1)S(1)} %get-tuple-element.56), channel_id=1, source_target_pairs={{0,35},{1,0},{2,1},{3,2},{4,39},{5,4},{6,5},{7,6},{8,43},{9,8},{10... | collective-permute-start | bytes 49160 | tf_op jit(solution)/shard_map/ppermute | solution.py:248
  13.4 10.4 %collective-permute-start.2 = (bf16[16,512]{1,0:T(8,128)(2,1)S(1)}, bf16[16,512]{1,0:T(8,128)(2,1)S(1)}, u32[]{:S(2)}, u32[]{:S(2)}) collective-permute-start(bf16[16,512]{1,0:T(8,128)(2,1)S(1)} %collective-permute-done), channel_id=1, source_target_pairs={{0,1},{1,2},{2,3},{3,32},{4,5},{5,6},{6,7},{7,36},{8,9},{9,10},{10... | collective-permute-start | bytes 49160 | tf_op jit(solution)/shard_map/ppermute | solution.py:248
  13.5 10.3 %collective-permute-start.3 = (bf16[16,512]{1,0:T(8,128)(2,1)S(1)}, bf16[16,512]{1,0:T(8,128)(2,1)S(1)}, u32[]{:S(2)}, u32[]{:S(2)}) collective-permute-start(bf16[16,512]{1,0:T(8,128)(2,1)S(1)} %collective-permute-done.1), channel_id=1, source_target_pairs={{0,35},{1,0},{2,1},{3,2},{4,39},{5,4},{6,5},{7,6},{8,43},{9,8},{10... | collective-permute-start | bytes 49160 | tf_op jit(solution)/shard_map/ppermute | solution.py:248
  16.1 14.0 %collective-permute-start.6 = (bf16[1,128,512]{2,1,0:T(8,128)(2,1)S(1)}, bf16[1,128,512]{2,1,0:T(8,128)(2,1)S(1)}, u32[]{:S(2)}, u32[]{:S(2)}) collective-permute-start(bf16[1,128,512]{2,1,0:T(8,128)(2,1)S(1)} %get-tuple-element.67), channel_id=1, source_target_pairs={{0,16},{16,32},{32,48},{48,64},{64,80},{80,96},{96,112},{112,128},... | collective-permute-start | bytes 393224 | tf_op jit(solution)/shard_map/ppermute | solution.py:328
  23.6 15.7 %collective-permute-start.11 = (bf16[1,128,512]{2,1,0:T(8,128)(2,1)S(1)}, bf16[1,128,512]{2,1,0:T(8,128)(2,1)S(1)}, u32[]{:S(2)}, u32[]{:S(2)}) collective-permute-start(bf16[1,128,512]{2,1,0:T(8,128)(2,1)S(1)} %get-tuple-element.76), channel_id=1, source_target_pairs={{0,1},{1,2},{2,3},{3,32},{4,5},{5,6},{6,7},{7,36},{8,9},{9,10},{10... | collective-permute-start | bytes 393224 | tf_op jit(solution)/shard_map/ppermute | solution.py:248
  23.8 6.4 %collective-permute-start.4 = (bf16[16,512]{1,0:T(8,128)(2,1)S(1)}, bf16[16,512]{1,0:T(8,128)(2,1)S(1)}, u32[]{:S(2)}, u32[]{:S(2)}) collective-permute-start(bf16[16,512]{1,0:T(8,128)(2,1)S(1)} %collective-permute-done.2), channel_id=1, source_target_pairs={{0,1},{1,2},{2,3},{3,32},{4,5},{5,6},{6,7},{7,36},{8,9},{9,10},{10... | collective-permute-start | bytes 49160 | tf_op jit(solution)/shard_map/ppermute | solution.py:248
  23.9 6.3 %collective-permute-start.5 = (bf16[16,512]{1,0:T(8,128)(2,1)S(1)}, bf16[16,512]{1,0:T(8,128)(2,1)S(1)}, u32[]{:S(2)}, u32[]{:S(2)}) collective-permute-start(bf16[16,512]{1,0:T(8,128)(2,1)S(1)} %collective-permute-done.3), channel_id=1, source_target_pairs={{0,35},{1,0},{2,1},{3,2},{4,39},{5,4},{6,5},{7,6},{8,43},{9,8},{10... | collective-permute-start | bytes 49160 | tf_op jit(solution)/shard_map/ppermute | solution.py:248
  26.6 11.4 %collective-permute-start.8 = (bf16[1,128,512]{2,1,0:T(8,128)(2,1)S(1)}, bf16[1,128,512]{2,1,0:T(8,128)(2,1)S(1)}, u32[]{:S(2)}, u32[]{:S(2)}) collective-permute-start(bf16[1,128,512]{2,1,0:T(8,128)(2,1)S(1)} %get-tuple-element.69), channel_id=1, source_target_pairs={{16,0},{32,16},{48,32},{64,48},{80,64},{96,80},{112,96},{128,112},... | collective-permute-start | bytes 393224 | tf_op jit(solution)/shard_map/ppermute | solution.py:328
  30.1 10.9 %collective-permute-start.12 = (bf16[1,128,512]{2,1,0:T(8,128)(2,1)S(1)}, bf16[1,128,512]{2,1,0:T(8,128)(2,1)S(1)}, u32[]{:S(2)}, u32[]{:S(2)}) collective-permute-start(bf16[1,128,512]{2,1,0:T(8,128)(2,1)S(1)} %get-tuple-element.77), channel_id=1, source_target_pairs={{0,35},{1,0},{2,1},{3,2},{4,39},{5,4},{6,5},{7,6},{8,43},{9,8},{10... | collective-permute-start | bytes 393224 | tf_op jit(solution)/shard_map/ppermute | solution.py:248
  30.1 4.6 %collective-permute-start.7 = (bf16[16,512]{1,0:T(8,128)(2,1)S(1)}, bf16[16,512]{1,0:T(8,128)(2,1)S(1)}, u32[]{:S(2)}, u32[]{:S(2)}) collective-permute-start(bf16[16,512]{1,0:T(8,128)(2,1)S(1)} %collective-permute-done.4), channel_id=1, source_target_pairs={{0,1},{1,2},{2,3},{3,32},{4,5},{5,6},{6,7},{7,36},{8,9},{9,10},{10... | collective-permute-start | bytes 49160 | tf_op jit(solution)/shard_map/ppermute | solution.py:248
  31.6 9.4 %collective-permute-start.10 = (bf16[1,128,512]{2,1,0:T(8,128)(2,1)S(1)}, bf16[1,128,512]{2,1,0:T(8,128)(2,1)S(1)}, u32[]{:S(2)}, u32[]{:S(2)}) collective-permute-start(bf16[1,128,512]{2,1,0:T(8,128)(2,1)S(1)} %get-tuple-element.75), channel_id=1, source_target_pairs={{4,0},{8,4},{12,8},{5,1},{9,5},{13,9},{6,2},{10,6},{14,10},{7,3},{... | collective-permute-start | bytes 393224 | tf_op jit(solution)/shard_map/ppermute | solution.py:328
  34.7 6.3 %collective-permute-start.9 = (bf16[1,128,512]{2,1,0:T(8,128)(2,1)S(1)}, bf16[1,128,512]{2,1,0:T(8,128)(2,1)S(1)}, u32[]{:S(2)}, u32[]{:S(2)}) collective-permute-start(bf16[1,128,512]{2,1,0:T(8,128)(2,1)S(1)} %get-tuple-element.74), channel_id=1, source_target_pairs={{0,4},{4,8},{8,12},{1,5},{5,9},{9,13},{2,6},{6,10},{10,14},{3,7},{... | collective-permute-start | bytes 393224 | tf_op jit(solution)/shard_map/ppermute | solution.py:328
  38.0 10.1 %collective-permute-start.13 = (bf16[128,512]{1,0:T(8,128)(2,1)S(1)}, bf16[128,512]{1,0:T(8,128)(2,1)S(1)}, u32[]{:S(2)}, u32[]{:S(2)}) collective-permute-start(bf16[128,512]{1,0:T(8,128)(2,1)S(1)} %constant_dynamic-update-slice_fusion), channel_id=1, source_target_pairs={{0,64},{1,65},{2,66},{3,67},{4,68},{5,69},{6,70},{7,71},{8,72},{9,... | collective-permute-start | bytes 393224 | tf_op jit(solution)/shard_map/ppermute | solution.py:248
  39.4 8.7 %collective-permute-start.14 = (bf16[128,512]{1,0:T(8,128)(2,1)S(1)}, bf16[128,512]{1,0:T(8,128)(2,1)S(1)}, u32[]{:S(2)}, u32[]{:S(2)}) collective-permute-start(bf16[128,512]{1,0:T(8,128)(2,1)S(1)} %constant_dynamic-update-slice_fusion), channel_id=1, source_target_pairs={{0,192},{1,193},{2,194},{3,195},{4,196},{5,197},{6,198},{7,199},{8... | collective-permute-start | bytes 393224 | tf_op jit(solution)/shard_map/ppermute | solution.py:248
  53.7 4.4 %collective-permute-start.15 = (bf16[64,512]{1,0:T(8,128)(2,1)S(1)}, bf16[64,512]{1,0:T(8,128)(2,1)S(1)}, u32[]{:S(2)}, u32[]{:S(2)}) collective-permute-start(bf16[64,512]{1,0:T(8,128)(2,1)S(1)} %slice.12), channel_id=1, source_target_pairs={{0,64},{1,65},{2,66},{3,67},{4,68},{5,69},{6,70},{7,71},{8,72},{9,... | collective-permute-start | bytes 196616 | tf_op jit(solution)/shard_map/ppermute | solution.py:248
  58.1 14.5 %collective-permute-start.17 = (bf16[512,512]{1,0:T(8,128)(2,1)S(1)}, bf16[512,512]{1,0:T(8,128)(2,1)S(1)}, u32[]{:S(2)}, u32[]{:S(2)}) collective-permute-start(bf16[512,512]{1,0:T(8,128)(2,1)S(1)} %constant_dynamic-update-slice_fusion.8.m0), channel_id=1, source_target_pairs={{0,4},{1,5},{2,6},{3,7},{4,8},{5,9},{6,10},{7,11},{8,12},{9,13},{1... | collective-permute-start | bytes 1572872 | tf_op jit(solution)/shard_map/ppermute | solution.py:248
  59.8 12.8 %collective-permute-start.18 = (bf16[512,512]{1,0:T(8,128)(2,1)S(1)}, bf16[512,512]{1,0:T(8,128)(2,1)S(1)}, u32[]{:S(2)}, u32[]{:S(2)}) collective-permute-start(bf16[512,512]{1,0:T(8,128)(2,1)S(1)} %constant_dynamic-update-slice_fusion.8.m0), channel_id=1, source_target_pairs={{0,12},{1,13},{2,14},{3,15},{4,0},{5,1},{6,2},{7,3},{8,4},{9,5},{1... | collective-permute-start | bytes 1572872 | tf_op jit(solution)/shard_map/ppermute | solution.py:248
  61.1 26.7 %collective-permute-start.21 = (bf16[512,512]{1,0:T(8,128)(2,1)S(1)}, bf16[512,512]{1,0:T(8,128)(2,1)S(1)}, u32[]{:S(2)}, u32[]{:S(2)}) collective-permute-start(bf16[512,512]{1,0:T(8,128)(2,1)S(1)} %constant_dynamic-update-slice_fusion.8.m0), channel_id=1, source_target_pairs={{0,16},{1,17},{2,18},{3,19},{4,20},{5,21},{6,22},{7,23},{8,24},{9,... | collective-permute-start | bytes 1572872 | tf_op jit(solution)/shard_map/ppermute | solution.py:248
  72.6 15.3 %collective-permute-start.22 = (bf16[512,512]{1,0:T(8,128)(2,1)S(1)}, bf16[512,512]{1,0:T(8,128)(2,1)S(1)}, u32[]{:S(2)}, u32[]{:S(2)}) collective-permute-start(bf16[512,512]{1,0:T(8,128)(2,1)S(1)} %collective-permute-done.17.m1), channel_id=1, source_target_pairs={{0,16},{1,17},{2,18},{3,19},{4,20},{5,21},{6,22},{7,23},{8,24},{9,... | collective-permute-start | bytes 1572872 | tf_op jit(solution)/shard_map/ppermute | solution.py:248
  74.8 13.1 %collective-permute-start.23 = (bf16[512,512]{1,0:T(8,128)(2,1)S(1)}, bf16[512,512]{1,0:T(8,128)(2,1)S(1)}, u32[]{:S(2)}, u32[]{:S(2)}) collective-permute-start(bf16[512,512]{1,0:T(8,128)(2,1)S(1)} %collective-permute-done.18.m2), channel_id=1, source_target_pairs={{0,16},{1,17},{2,18},{3,19},{4,20},{5,21},{6,22},{7,23},{8,24},{9,... | collective-permute-start | bytes 1572872 | tf_op jit(solution)/shard_map/ppermute | solution.py:248
  74.9 8.9 %collective-permute-start.19 = (bf16[256,512]{1,0:T(8,128)(2,1)S(1)}, bf16[256,512]{1,0:T(8,128)(2,1)S(1)}, u32[]{:S(2)}, u32[]{:S(2)}) collective-permute-start(bf16[256,512]{1,0:T(8,128)(2,1)S(1)} %slice.14), channel_id=1, source_target_pairs={{0,4},{1,5},{2,6},{3,7},{4,8},{5,9},{6,10},{7,11},{8,12},{9,13},{1... | collective-permute-start | bytes 786440 | tf_op jit(solution)/shard_map/ppermute | solution.py:248
  75.9 8.0 %collective-permute-start.20 = (bf16[256,512]{1,0:T(8,128)(2,1)S(1)}, bf16[256,512]{1,0:T(8,128)(2,1)S(1)}, u32[]{:S(2)}, u32[]{:S(2)}) collective-permute-start(bf16[256,512]{1,0:T(8,128)(2,1)S(1)} %slice.15), channel_id=1, source_target_pairs={{0,12},{1,13},{2,14},{3,15},{4,0},{5,1},{6,2},{7,3},{8,4},{9,5},{1... | collective-permute-start | bytes 786440 | tf_op jit(solution)/shard_map/ppermute | solution.py:248
  83.8 4.0 %collective-permute-start.24 = (bf16[256,512]{1,0:T(8,128)(2,1)S(1)}, bf16[256,512]{1,0:T(8,128)(2,1)S(1)}, u32[]{:S(2)}, u32[]{:S(2)}) collective-permute-start(bf16[256,512]{1,0:T(8,128)(2,1)S(1)} %collective-permute-done.19.m3), channel_id=1, source_target_pairs={{0,16},{1,17},{2,18},{3,19},{4,20},{5,21},{6,22},{7,23},{8,24},{9,... | collective-permute-start | bytes 786440 | tf_op jit(solution)/shard_map/ppermute | solution.py:248
  (19 other events, 316.9 us)

commit v4 on v3

--- a/solution.py
+++ b/solution.py
@@ -16,7 +16,7 @@
 BF16 = jnp.bfloat16
 D = 512
 BLOCK = 128
-SHARES = (2, 2, 2, 2)
+SHARES = (3, 3, 2)
 
 
 def linear(place):
@@ -49,6 +49,8 @@
 SWAP = permutation(lambda x, zh, c, y, z: (x, zh, 1 - c, y, z))
 UP_Z = permutation(functools.partial(along_z, step=1))
 DOWN_Z = permutation(functools.partial(along_z, step=-1))
+UP_3Z = permutation(functools.partial(along_z, step=3))
+DOWN_3Z = permutation(functools.partial(along_z, step=-3))
 UP_FIRST = permutation(functools.partial(along_plane, step=1, first=True))
 DOWN_FIRST = permutation(functools.partial(along_plane, step=-1, first=True))
 UP_SECOND = permutation(functools.partial(along_plane, step=1, first=False))
@@ -108,7 +110,7 @@
     x = owner >> 6
     back = (here["zh"] * 4 + here["z"] - zh * 4 - z) & 7
     stream = c
-    at = jnp.where(back <= 4, back, 12 - back) * 16 + row
+    at = ((back + 1) & 7) * 16 + row
     step_x = (here["x"] - x) & 3
     step_y = (here["y"] - y) & 3
     order_x = jnp.where(step_x == 2, 3, jnp.where(step_x == 3, 2, step_x))
@@ -118,11 +120,14 @@
 
 
 def face_kernel(
-    after, fine_h, rows_h, counts, weight_h, edge_out_h,
-    sender_out, centred_out, f0, f1, f2, f3, f4, f5,
-    fine, rows, weight, edge_out, sems,
+    pool, fine_h, rows_h, counts, weight_h, edge_out_h, coarse_in_h, coarse_bias,
+    sender_out, centred_out, received_out, f0, f1, f2, f3, f4, f5,
+    fine, rows, weight, edge_out, coarse_in, sems,
 ):
-    pairs = ((rows_h, rows), (fine_h, fine), (weight_h.at[pl.ds(0, D)], weight), (edge_out_h, edge_out))
+    pairs = (
+        (rows_h, rows), (fine_h, fine), (weight_h.at[pl.ds(0, D)], weight), (edge_out_h, edge_out),
+        (coarse_in_h.at[pl.ds(D, D)], coarse_in),
+    )
     copies = [pltpu.make_async_copy(source, target, sems.at[k]) for k, (source, target) in enumerate(pairs)]
     for copy in copies:
         copy.start()
@@ -130,6 +135,7 @@
         copy.wait()
     sender = dot(fine[...], weight[...]).astype(BF16)
     sender_out[...] = sender
+    received_out[...] = dot(pool[...], coarse_in[...]) + coarse_bias[...]
     wide = edge_out[...].astype(F32)
     centred_out[...] = (wide - jnp.mean(wide, axis=1, keepdims=True)).astype(BF16)
     flat = jnp.concatenate(
@@ -216,12 +222,11 @@
 def coarse_kernel(
     found, o0, o1, o2, o3, o4, slots, pool, medium, comp, member, *rest,
 ):
-    *news, edge_in, edge_bias, edge_out, edge_gain, node_in, node_bias, node_out, node_gain, fine_out, medium_out, coarse_out = rest
+    *news, received, edge_out, edge_gain, node_in, node_bias, node_out, node_gain, fine_out, medium_out, coarse_out = rest
     pool_rows = pool[...]
-    received = dot(pool_rows, edge_in[...]) + edge_bias[...]
     sources = ((2048, o0), (2560, o1), (3072, o2), (3584, o3), (3840, o4))
     total = found[...].astype(F32) + found_in(columns_of(slots), sources)
-    hidden = jnp.maximum(total.reshape(64, 16, D) + received[None], 0.0).astype(BF16).reshape(1024, D)
+    hidden = jnp.maximum(total.reshape(64, 16, D) + received[...][None], 0.0).astype(BF16).reshape(1024, D)
     message = normed(dot(hidden, edge_out[...])) * edge_gain[...]
     incoming = jnp.sum(message.reshape(64, 16, D), axis=0).astype(BF16)
     both = jnp.concatenate([pool_rows, incoming], axis=1)
@@ -304,20 +309,21 @@
             pltpu.SemaphoreType.DMA((7,)),
         ],
     )
-    fine_sender, centred, *faces = kernel(
+    fine_sender, centred, received, *faces = kernel(
         face_kernel,
-        [shaped((1024, D), BF16), shaped((D, D), BF16)] + [shaped((1, 128, D), BF16)] * 6,
-        [pl.BlockSpec(memory_space=pl.ANY), far, far, scalars, far, far],
+        [shaped((1024, D), BF16), shaped((D, D), BF16), shaped((16, D), F32)] + [shaped((1, 128, D), BF16)] * 6,
+        [held, far, far, scalars, far, far, far, held],
         (
-            member, distant(fine_state), distant(send_rows.reshape(1, 768)), ghost_counts, distant(fine_edge_in),
-            distant(fine_edge_out),
+            pool, distant(fine_state), distant(send_rows.reshape(1, 768)), ghost_counts, distant(fine_edge_in),
+            distant(fine_edge_out), distant(coarse_edge_in), row(coarse_edge_bias),
         ),
         [
             pltpu.VMEM((1024, D), BF16),
             pltpu.VMEM((1, 768), jnp.int32),
             pltpu.VMEM((D, D), BF16),
             pltpu.VMEM((D, D), BF16),
-            pltpu.SemaphoreType.DMA((4,)),
+            pltpu.VMEM((D, D), BF16),
+            pltpu.SemaphoreType.DMA((5,)),
         ],
     )
 
@@ -327,22 +333,18 @@
         pairs = [(k, k + 1) for k in range(count - 1)]
         return lax.ppermute(faces[face], axes, [(b, a) for a, b in pairs] if face % 2 == 0 else pairs)
 
-    ups, downs = [sent(sender, UP_Z)], [sent(sender, DOWN_Z)]
-    up, down, faces[5], faces[4], faces[1] = tied((ups[-1], downs[-1], faces[5], faces[4], faces[1]))
-    ups.append(sent(up, UP_Z))
-    downs.append(sent(down, DOWN_Z))
-    low_x, low_z, high_z = faced(1), sent(faces[5], UP_Z), sent(faces[4], DOWN_Z)
-    up, down, faces[0] = tied((ups[-1], downs[-1], faces[0]))
-    ups.append(sent(up, UP_Z))
-    downs.append(sent(down, DOWN_Z))
-    high_x = faced(0)
-    up, down, faces[3], faces[2], low_x = tied((ups[-1], downs[-1], faces[3], faces[2], low_x))
-    ups.append(sent(up, UP_Z))
+    low, high = sent(sender, UP_Z), sent(sender, DOWN_Z)
+    low, high, faces[0], faces[1] = tied((low, high, faces[0], faces[1]))
+    three = joined(high, sender, low)
+    lower, higher = sent(three, UP_3Z), sent(three[16:], DOWN_3Z)
+    low_x, high_x = faced(1), faced(0)
+    lower, higher, *faces[2:] = tied((lower, higher, *faces[2:]))
+    column = joined(three, lower, higher)
+    up, down = sent(column, UP_FIRST), sent(column, DOWN_FIRST)
     low_y, high_y = faced(3), faced(2)
-    last, high_x = tied((ups[-1], high_x))
-    column = joined(sender, *ups[:3], last, *downs)
+    low_z, high_z = sent(faces[5], UP_Z), sent(faces[4], DOWN_Z)
+    up, down, low_x, high_x = tied((up, down, low_x, high_x))
     near_faces = [low_x, high_x, low_y, high_y, low_z, high_z]
-    fine_sender, column = tied((fine_sender, column))
     table, near = kernel(
         table_kernel,
         [shaped((1792, D), BF16), shaped((1024, 8), jnp.int32)],
@@ -370,25 +372,21 @@
             )
         )
 
-    up, down = sent(column, UP_FIRST), sent(column, DOWN_FIRST)
-    edges(SHARES[0])
-    up, down, news[-1] = tied((up, down, news[-1]))
-    table, up = tied((table, up))
     rest = [sent(up[:64], UP_FIRST), sent(down[64:], DOWN_FIRST)]
-    edges(SHARES[1])
-    *rest, news[-1] = tied((*rest, news[-1]))
     line = joined(column, up, down, *rest)
     table, line = tied((table, line))
     up, down = sent(line, UP_SECOND), sent(line, DOWN_SECOND)
     others = [sent(line, SWAP)]
-    edges(SHARES[2])
+    edges(SHARES[0])
     up, down, news[-1] = tied((up, down, news[-1]))
     table, up = tied((table, up))
     rest = [sent(up[:256], UP_SECOND), sent(down[256:], DOWN_SECOND)]
     others += [sent(up, SWAP), sent(down, SWAP)]
-    edges(SHARES[3])
+    edges(SHARES[1])
     *rest, news[-1] = tied((*rest, news[-1]))
+    table, rest[0] = tied((table, rest[0]))
     others += [sent(part, SWAP) for part in rest]
+    edges(SHARES[2])
     (found,) = kernel(
         gather_kernel, [shaped((1024, D), BF16)], [held] * 6, (slots, line, up, down, *rest), limit=40,
         cost=pl.CostEstimate(flops=2_000_000_000, bytes_accessed=4_000_000, transcendentals=0),
@@ -396,9 +394,9 @@
     fine_out, medium_out, coarse_out = kernel(
         coarse_kernel,
         [shaped((1024, D), BF16), shaped((128, D), BF16), shaped((16, D), BF16)],
-        [held] * (11 + len(news)) + [upper] + [held] * 7,
+        [held] * (18 + len(news)),
         (
-            found, *others, slots, pool, medium_pool, comp, member, *news, coarse_edge_in, row(coarse_edge_bias),
+            found, *others, slots, pool, medium_pool, comp, member, *news, received,
             coarse_edge_out, row(coarse_edge_gain), coarse_node_in, row(coarse_node_bias), coarse_node_out,
             row(coarse_node_gain),
         ),

time: 95.1 us -> 88.9 us (0.935)
  starting transfers between devices: 48.5 us -> 43.7 us
  local copies, waits for them, and re-layouts: 1.19 us -> 0.21 us
    ppermute x22 -> x19, waiting for transfers between devices: 5.14 us -> 0.05 us  [sent(): return lax.ppermute(rows, AXES, pairs)]
    ppermute x4, waiting for transfers between devices: 0.01 us -> 4.51 us  [faced(): lax.ppermute(faces[face], axes, [(b, a) for a, b in pairs] if face % 2 ==...]
    ppermute x22 -> x19, starting transfers between devices: 34.6 us -> 30.3 us  [sent(): return lax.ppermute(rows, AXES, pairs)]
    unnamed x45 -> x42, local copies, waits for them, and re-layouts: 1.13 us -> 0.16 us
    pallas_call x9 -> x8, Pallas kernels: 38.9 us -> 39 us  [kernel(): pl.pallas_call(body, grid=(1,), out_shape=outs, in_specs=specs, out_specs...]
  transfers between devices with their start and end apart: 26 -> 23, of which waited for: 3 -> 2; matrix products, arithmetic and copies ran while one was open for 0% -> 0% of each run, Pallas kernels for 25% -> 34%
where the time goes in v4:
time: 88.9 us; the launch traced here: 88.6 us
  starting transfers between devices  43.7 us (49%)
  Pallas kernels  39 us (44%)
  waiting for transfers between devices  4.56 us (5%)
  between operations  1.2 us (1%)
    pallas_call x8, Pallas kernels, kernel(): pl.pallas_call(body, grid=(1,), out_shape=outs, in_specs=specs, out_specs...  39 us
    ppermute x19, starting transfers between devices, sent(): return lax.ppermute(rows, AXES, pairs)  30.3 us
    ppermute x4, starting transfers between devices, faced(): lax.ppermute(faces[face], axes, [(b, a) for a, b in pairs] if face % 2 ==...  13.3 us
    ppermute x4, waiting for transfers between devices, faced(): lax.ppermute(faces[face], axes, [(b, a) for a, b in pairs] if face % 2 ==...  4.51 us
  transfers between devices with their start and end apart: 23, of which 2 were waited for; matrix products, arithmetic and copies ran while one was open for 0% of the time, Pallas kernels for 34%

profile of v4, /device:TPU:1, one launch (start us, length us, event | category | flops | bytes accessed | tf_op | source)
XLA Modules:
  0.0 88.6 jit_solution(7618421987741346708)
XLA Ops:
  0.7 2.3 %shard_map.256 = (bf16[16,512]{1,0:T(8,128)(2,1)S(1)}, bf16[16,512]{1,0:T(8,128)(2,1)S(1)}, f32[128,512]{1,0:T(8,128)S(1)}, s32[16,64]{1,0:T(8,128)S(1)}, bf16[3...) custom-call(bf16[1024,512]{1,0:T(8,128)(2,1)} %fine.5, s32[1,1024]{1,0:T(1,128)} %bitcast.29, ...), custom_call_target="tpu_custom_call" | custom-call | tf_op jit(solution)/shard_map/pallas_call | solution.py:272
  3.0 2.5 %collective-permute-start = (bf16[16,512]{1,0:T(8,128)(2,1)S(1)}, bf16[16,512]{1,0:T(8,128)(2,1)S(1)}, u32[]{:S(2)}, u32[]{:S(2)}) collective-permute-start(bf16[16,512]{1,0:T(8,128)(2,1)S(1)} %get-tuple-element.49), channel_id=1, source_target_pairs={{0,1},{1,2},{2,3},{3,32},{4,5},{5,6},{6,7},{7,36},{8,9},{9,10},{10... | collective-permute-start | bytes 49160 | tf_op jit(solution)/shard_map/ppermute | solution.py:253
  5.5 4.0 %collective-permute-start.1 = (bf16[16,512]{1,0:T(8,128)(2,1)S(1)}, bf16[16,512]{1,0:T(8,128)(2,1)S(1)}, u32[]{:S(2)}, u32[]{:S(2)}) collective-permute-start(bf16[16,512]{1,0:T(8,128)(2,1)S(1)} %get-tuple-element.49), channel_id=1, source_target_pairs={{0,35},{1,0},{2,1},{3,2},{4,39},{5,4},{6,5},{7,6},{8,43},{9,8},{10... | collective-permute-start | bytes 49160 | tf_op jit(solution)/shard_map/ppermute | solution.py:253
  9.5 4.0 %shard_map.257 = (bf16[1024,512]{1,0:T(8,128)(2,1)S(1)}, bf16[512,512]{1,0:T(8,128)(2,1)S(1)}, f32[16,512]{1,0:T(8,128)S(1)}, bf16[1,128,512]{2,1,0:T(8,128)(2,1...) custom-call(bf16[16,512]{1,0:T(8,128)(2,1)S(1)} %get-tuple-element.4, ...), custom_call_target="tpu_custom_call" | custom-call | tf_op jit(solution)/shard_map/pallas_call | solution.py:272
  13.7 1.6 %collective-permute-start.2 = (bf16[48,512]{1,0:T(8,128)(2,1)S(1)}, bf16[48,512]{1,0:T(8,128)(2,1)S(1)}, u32[]{:S(2)}, u32[]{:S(2)}) collective-permute-start(bf16[48,512]{1,0:T(8,128)(2,1)S(1)} %pad_maximum_fusion), channel_id=1, source_target_pairs={{0,3},{1,32},{2,33},{3,34},{4,7},{5,36},{6,37},{7,38},{8,11},{9,40... | collective-permute-start | bytes 147464 | tf_op jit(solution)/shard_map/ppermute | solution.py:253
  15.3 2.9 %collective-permute-start.3 = (bf16[32,512]{1,0:T(8,128)(2,1)S(1)}, bf16[32,512]{1,0:T(8,128)(2,1)S(1)}, u32[]{:S(2)}, u32[]{:S(2)}) collective-permute-start(bf16[32,512]{1,0:T(8,128)(2,1)S(1)} %pad_maximum_fusion.1), channel_id=1, source_target_pairs={{0,33},{1,34},{2,35},{3,0},{4,37},{5,38},{6,39},{7,4},{8,41},{9,42... | collective-permute-start | bytes 98312 | tf_op jit(solution)/shard_map/ppermute | solution.py:253
  18.2 7.5 %collective-permute-start.6 = (bf16[1,128,512]{2,1,0:T(8,128)(2,1)S(1)}, bf16[1,128,512]{2,1,0:T(8,128)(2,1)S(1)}, u32[]{:S(2)}, u32[]{:S(2)}) collective-permute-start(bf16[1,128,512]{2,1,0:T(8,128)(2,1)S(1)} %get-tuple-element.60), channel_id=1, source_target_pairs={{0,16},{16,32},{32,48},{48,64},{64,80},{80,96},{96,112},{112,128},... | collective-permute-start | bytes 393224 | tf_op jit(solution)/shard_map/ppermute | solution.py:334
  25.7 1.9 %collective-permute-start.7 = (bf16[1,128,512]{2,1,0:T(8,128)(2,1)S(1)}, bf16[1,128,512]{2,1,0:T(8,128)(2,1)S(1)}, u32[]{:S(2)}, u32[]{:S(2)}) collective-permute-start(bf16[1,128,512]{2,1,0:T(8,128)(2,1)S(1)} %get-tuple-element.61), channel_id=1, source_target_pairs={{16,0},{32,16},{48,32},{64,48},{80,64},{96,80},{112,96},{128,112},... | collective-permute-start | bytes 393224 | tf_op jit(solution)/shard_map/ppermute | solution.py:334
  27.7 1.4 %collective-permute-start.4 = (bf16[128,512]{1,0:T(8,128)(2,1)S(1)}, bf16[128,512]{1,0:T(8,128)(2,1)S(1)}, u32[]{:S(2)}, u32[]{:S(2)}) collective-permute-start(bf16[128,512]{1,0:T(8,128)(2,1)S(1)} %get-tuple-element.92), channel_id=1, source_target_pairs={{0,64},{1,65},{2,66},{3,67},{4,68},{5,69},{6,70},{7,71},{8,72},{9,... | collective-permute-start | bytes 393224 | tf_op jit(solution)/shard_map/ppermute | solution.py:253
  29.1 1.5 %collective-permute-start.5 = (bf16[128,512]{1,0:T(8,128)(2,1)S(1)}, bf16[128,512]{1,0:T(8,128)(2,1)S(1)}, u32[]{:S(2)}, u32[]{:S(2)}) collective-permute-start(bf16[128,512]{1,0:T(8,128)(2,1)S(1)} %get-tuple-element.92), channel_id=1, source_target_pairs={{0,192},{1,193},{2,194},{3,195},{4,196},{5,197},{6,198},{7,199},{8... | collective-permute-start | bytes 393224 | tf_op jit(solution)/shard_map/ppermute | solution.py:253
  30.6 2.7 %collective-permute-start.11 = (bf16[1,128,512]{2,1,0:T(8,128)(2,1)S(1)}, bf16[1,128,512]{2,1,0:T(8,128)(2,1)S(1)}, u32[]{:S(2)}, u32[]{:S(2)}) collective-permute-start(bf16[1,128,512]{2,1,0:T(8,128)(2,1)S(1)} %get-tuple-element.67), channel_id=1, source_target_pairs={{0,35},{1,0},{2,1},{3,2},{4,39},{5,4},{6,5},{7,6},{8,43},{9,8},{10... | collective-permute-start | bytes 393224 | tf_op jit(solution)/shard_map/ppermute | solution.py:253
  33.3 3.3 %collective-permute-done.7.g1 = bf16[1,128,512]{2,1,0:T(8,128)(2,1)S(1)} collective-permute-done((bf16[1,128,512]{2,1,0:T(8,128)(2,1)S(1)}, bf16[1,128,512]{2,1,0:T(8,128)(2,1)S(1)}, u32[]{:S(2)}, u32[]{:S(2)}) %collective-permute-start.7) | collective-permute-done | bytes 131104 | tf_op jit(solution)/shard_map/ppermute | solution.py:334
  36.6 2.6 %collective-permute-start.8 = (bf16[1,128,512]{2,1,0:T(8,128)(2,1)S(1)}, bf16[1,128,512]{2,1,0:T(8,128)(2,1)S(1)}, u32[]{:S(2)}, u32[]{:S(2)}) collective-permute-start(bf16[1,128,512]{2,1,0:T(8,128)(2,1)S(1)} %get-tuple-element.64), channel_id=1, source_target_pairs={{0,4},{4,8},{8,12},{1,5},{5,9},{9,13},{2,6},{6,10},{10,14},{3,7},{... | collective-permute-start | bytes 393224 | tf_op jit(solution)/shard_map/ppermute | solution.py:334
  40.5 2.2 %collective-permute-start.12 = (bf16[64,512]{1,0:T(8,128)(2,1)S(1)}, bf16[64,512]{1,0:T(8,128)(2,1)S(1)}, u32[]{:S(2)}, u32[]{:S(2)}) collective-permute-start(bf16[64,512]{1,0:T(8,128)(2,1)S(1)} %slice.14), channel_id=1, source_target_pairs={{0,64},{1,65},{2,66},{3,67},{4,68},{5,69},{6,70},{7,71},{8,72},{9,... | collective-permute-start | bytes 196616 | tf_op jit(solution)/shard_map/ppermute | solution.py:253
  42.7 1.5 %collective-permute-start.13 = (bf16[64,512]{1,0:T(8,128)(2,1)S(1)}, bf16[64,512]{1,0:T(8,128)(2,1)S(1)}, u32[]{:S(2)}, u32[]{:S(2)}) collective-permute-start(bf16[64,512]{1,0:T(8,128)(2,1)S(1)} %slice.15), channel_id=1, source_target_pairs={{0,192},{1,193},{2,194},{3,195},{4,196},{5,197},{6,198},{7,199},{8... | collective-permute-start | bytes 196616 | tf_op jit(solution)/shard_map/ppermute | solution.py:253
  46.9 2.4 %collective-permute-start.14 = (bf16[512,512]{1,0:T(8,128)(2,1)S(1)}, bf16[512,512]{1,0:T(8,128)(2,1)S(1)}, u32[]{:S(2)}, u32[]{:S(2)}) collective-permute-start(bf16[512,512]{1,0:T(8,128)(2,1)S(1)} %constant_dynamic-update-slice_fusion.5.m0), channel_id=1, source_target_pairs={{0,4},{1,5},{2,6},{3,7},{4,8},{5,9},{6,10},{7,11},{8,12},{9,13},{1... | collective-permute-start | bytes 1572872 | tf_op jit(solution)/shard_map/ppermute | solution.py:253
  49.3 1.6 %collective-permute-start.15 = (bf16[512,512]{1,0:T(8,128)(2,1)S(1)}, bf16[512,512]{1,0:T(8,128)(2,1)S(1)}, u32[]{:S(2)}, u32[]{:S(2)}) collective-permute-start(bf16[512,512]{1,0:T(8,128)(2,1)S(1)} %constant_dynamic-update-slice_fusion.5.m0), channel_id=1, source_target_pairs={{0,12},{1,13},{2,14},{3,15},{4,0},{5,1},{6,2},{7,3},{8,4},{9,5},{1... | collective-permute-start | bytes 1572872 | tf_op jit(solution)/shard_map/ppermute | solution.py:253
  51.0 1.5 %collective-permute-start.18 = (bf16[512,512]{1,0:T(8,128)(2,1)S(1)}, bf16[512,512]{1,0:T(8,128)(2,1)S(1)}, u32[]{:S(2)}, u32[]{:S(2)}) collective-permute-start(bf16[512,512]{1,0:T(8,128)(2,1)S(1)} %constant_dynamic-update-slice_fusion.5.m0), channel_id=1, source_target_pairs={{0,16},{1,17},{2,18},{3,19},{4,20},{5,21},{6,22},{7,23},{8,24},{9,... | collective-permute-start | bytes 1572872 | tf_op jit(solution)/shard_map/ppermute | solution.py:253
  52.5 8.4 %shard_map.259.rest_0_ = f32[384,512]{1,0:T(8,128)S(1)} custom-call(bf16[1792,512]{1,0:T(8,128)(2,1)S(1)} %get-tuple-element.87.table, bf16[1024,512]{1,0:T(8,128)(2,1)S(1)} %copy-done, s32[1024,8]{1,0:T(8,128)S(1)} %get-tuple-element.73.nbrs, bf16[1024,512]{1,0:T(8,128)(2,1)S(1)} %copy-done.1, f32[1,512]{1,0:T(1,128)S(1)} %bitcast.17, ...), custom_call_target="tpu_custom_call" | custom-call | flops 5100000256 | bytes 9000000 | tf_op jit(solution)/shard_map/pallas_call | solution.py:272
  61.7 2.7 %collective-permute-start.17 = (bf16[256,512]{1,0:T(8,128)(2,1)S(1)}, bf16[256,512]{1,0:T(8,128)(2,1)S(1)}, u32[]{:S(2)}, u32[]{:S(2)}) collective-permute-start(bf16[256,512]{1,0:T(8,128)(2,1)S(1)} %slice.17), channel_id=1, source_target_pairs={{0,12},{1,13},{2,14},{3,15},{4,0},{5,1},{6,2},{7,3},{8,4},{9,5},{1... | collective-permute-start | bytes 786440 | tf_op jit(solution)/shard_map/ppermute | solution.py:253
  64.3 8.4 %shard_map.260.rest_1_ = f32[384,512]{1,0:T(8,128)S(1)} custom-call(bf16[1792,512]{1,0:T(8,128)(2,1)S(1)} %get-tuple-element.87.table, bf16[1024,512]{1,0:T(8,128)(2,1)S(1)} %copy-done, s32[1024,8]{1,0:T(8,128)S(1)} %get-tuple-element.73.nbrs, bf16[1024,512]{1,0:T(8,128)(2,1)S(1)} %copy-done.1, f32[1,512]{1,0:T(1,128)S(1)} %bitcast.18, ...), custom_call_target="tpu_custom_call" | custom-call | flops 5100000256 | bytes 9000000 | tf_op jit(solution)/shard_map/pallas_call | solution.py:272
  73.8 2.4 %shard_map.261.found = bf16[1024,512]{1,0:T(8,128)(2,1)S(1)} custom-call(s32[16,64]{1,0:T(8,128)S(1)} %get-tuple-element.46.slots, bf16[512,512]{1,0:T(8,128)(2,1)S(1)} %constant_dynamic-update-slice_fusion.5.m0, bf16[512,512]{1,0:T(8,128)(2,1)S(1)} %collective-permute-done.14.m1, bf16[512,512]{1,0:T(8,128)(2,1)S(1)} %collective-permute-done.15.m2, ...), custom_call_target="tpu_custom_call" | custom-call | flops 2000000000 | bytes 4000000 | tf_op jit(solution)/shard_map/pallas_call | solution.py:272
  76.2 5.6 %shard_map.262.rest_2_ = f32[256,512]{1,0:T(8,128)S(1)} custom-call(bf16[1792,512]{1,0:T(8,128)(2,1)S(1)} %get-tuple-element.87.table, bf16[1024,512]{1,0:T(8,128)(2,1)S(1)} %copy-done, s32[1024,8]{1,0:T(8,128)S(1)} %get-tuple-element.73.nbrs, bf16[1024,512]{1,0:T(8,128)(2,1)S(1)} %copy-done.1, f32[1,512]{1,0:T(1,128)S(1)} %bitcast.19, ...), custom_call_target="tpu_custom_call" | custom-call | flops 3400000000 | bytes 6000000 | tf_op jit(solution)/shard_map/pallas_call | solution.py:272
  81.9 6.7 %shard_map.263 = (bf16[1024,512]{1,0:T(8,128)(2,1)}, bf16[128,512]{1,0:T(8,128)(2,1)}, bf16[16,512]{1,0:T(8,128)(2,1)}) custom-call(bf16[1024,512]{1,0:T(8,128)(2,1)} %copy-done.2, bf16[512,512]{1,0:T(8,128)(2,1)S(1)} %collective-permute-done.18.o0, bf16[512,512]{1,0:T(8,128)(2,1)S(1)} %collective-permute-done.19.o1, ...), custom_call_target="tpu_custom_call" | custom-call | tf_op jit(solution)/shard_map/pallas_call | solution.py:272
  (79 shorter events, 5.9 us)
Async XLA Ops:
  3.0 10.7 %collective-permute-start = (bf16[16,512]{1,0:T(8,128)(2,1)S(1)}, bf16[16,512]{1,0:T(8,128)(2,1)S(1)}, u32[]{:S(2)}, u32[]{:S(2)}) collective-permute-start(bf16[16,512]{1,0:T(8,128)(2,1)S(1)} %get-tuple-element.49), channel_id=1, source_target_pairs={{0,1},{1,2},{2,3},{3,32},{4,5},{5,6},{6,7},{7,36},{8,9},{9,10},{10... | collective-permute-start | bytes 49160 | tf_op jit(solution)/shard_map/ppermute | solution.py:253
  5.5 8.1 %collective-permute-start.1 = (bf16[16,512]{1,0:T(8,128)(2,1)S(1)}, bf16[16,512]{1,0:T(8,128)(2,1)S(1)}, u32[]{:S(2)}, u32[]{:S(2)}) collective-permute-start(bf16[16,512]{1,0:T(8,128)(2,1)S(1)} %get-tuple-element.49), channel_id=1, source_target_pairs={{0,35},{1,0},{2,1},{3,2},{4,39},{5,4},{6,5},{7,6},{8,43},{9,8},{10... | collective-permute-start | bytes 49160 | tf_op jit(solution)/shard_map/ppermute | solution.py:253
  9.5 42.9 %copy-start.12 = (bf16[512,512]{1,0:T(8,128)(2,1)S(1)}, bf16[512,512]{1,0:T(8,128)(2,1)}, u32[]{:S(2)}) copy-start(bf16[512,512]{1,0:T(8,128)(2,1)} %node_out.5) | copy-start | bytes 1572868
  13.7 14.0 %collective-permute-start.2 = (bf16[48,512]{1,0:T(8,128)(2,1)S(1)}, bf16[48,512]{1,0:T(8,128)(2,1)S(1)}, u32[]{:S(2)}, u32[]{:S(2)}) collective-permute-start(bf16[48,512]{1,0:T(8,128)(2,1)S(1)} %pad_maximum_fusion), channel_id=1, source_target_pairs={{0,3},{1,32},{2,33},{3,34},{4,7},{5,36},{6,37},{7,38},{8,11},{9,40... | collective-permute-start | bytes 147464 | tf_op jit(solution)/shard_map/ppermute | solution.py:253
  15.3 12.4 %collective-permute-start.3 = (bf16[32,512]{1,0:T(8,128)(2,1)S(1)}, bf16[32,512]{1,0:T(8,128)(2,1)S(1)}, u32[]{:S(2)}, u32[]{:S(2)}) collective-permute-start(bf16[32,512]{1,0:T(8,128)(2,1)S(1)} %pad_maximum_fusion.1), channel_id=1, source_target_pairs={{0,33},{1,34},{2,35},{3,0},{4,37},{5,38},{6,39},{7,4},{8,41},{9,42... | collective-permute-start | bytes 98312 | tf_op jit(solution)/shard_map/ppermute | solution.py:253
  18.2 12.4 %collective-permute-start.6 = (bf16[1,128,512]{2,1,0:T(8,128)(2,1)S(1)}, bf16[1,128,512]{2,1,0:T(8,128)(2,1)S(1)}, u32[]{:S(2)}, u32[]{:S(2)}) collective-permute-start(bf16[1,128,512]{2,1,0:T(8,128)(2,1)S(1)} %get-tuple-element.60), channel_id=1, source_target_pairs={{0,16},{16,32},{32,48},{48,64},{64,80},{80,96},{96,112},{112,128},... | collective-permute-start | bytes 393224 | tf_op jit(solution)/shard_map/ppermute | solution.py:334
  25.7 10.9 %collective-permute-start.7 = (bf16[1,128,512]{2,1,0:T(8,128)(2,1)S(1)}, bf16[1,128,512]{2,1,0:T(8,128)(2,1)S(1)}, u32[]{:S(2)}, u32[]{:S(2)}) collective-permute-start(bf16[1,128,512]{2,1,0:T(8,128)(2,1)S(1)} %get-tuple-element.61), channel_id=1, source_target_pairs={{16,0},{32,16},{48,32},{64,48},{80,64},{96,80},{112,96},{128,112},... | collective-permute-start | bytes 393224 | tf_op jit(solution)/shard_map/ppermute | solution.py:334
  27.7 11.5 %collective-permute-start.4 = (bf16[128,512]{1,0:T(8,128)(2,1)S(1)}, bf16[128,512]{1,0:T(8,128)(2,1)S(1)}, u32[]{:S(2)}, u32[]{:S(2)}) collective-permute-start(bf16[128,512]{1,0:T(8,128)(2,1)S(1)} %get-tuple-element.92), channel_id=1, source_target_pairs={{0,64},{1,65},{2,66},{3,67},{4,68},{5,69},{6,70},{7,71},{8,72},{9,... | collective-permute-start | bytes 393224 | tf_op jit(solution)/shard_map/ppermute | solution.py:253
  29.1 11.4 %collective-permute-start.5 = (bf16[128,512]{1,0:T(8,128)(2,1)S(1)}, bf16[128,512]{1,0:T(8,128)(2,1)S(1)}, u32[]{:S(2)}, u32[]{:S(2)}) collective-permute-start(bf16[128,512]{1,0:T(8,128)(2,1)S(1)} %get-tuple-element.92), channel_id=1, source_target_pairs={{0,192},{1,193},{2,194},{3,195},{4,196},{5,197},{6,198},{7,199},{8... | collective-permute-start | bytes 393224 | tf_op jit(solution)/shard_map/ppermute | solution.py:253
  30.6 12.1 %collective-permute-start.10 = (bf16[1,128,512]{2,1,0:T(8,128)(2,1)S(1)}, bf16[1,128,512]{2,1,0:T(8,128)(2,1)S(1)}, u32[]{:S(2)}, u32[]{:S(2)}) collective-permute-start(bf16[1,128,512]{2,1,0:T(8,128)(2,1)S(1)} %get-tuple-element.66), channel_id=1, source_target_pairs={{0,1},{1,2},{2,3},{3,32},{4,5},{5,6},{6,7},{7,36},{8,9},{9,10},{10... | collective-permute-start | bytes 393224 | tf_op jit(solution)/shard_map/ppermute | solution.py:253
  30.6 13.6 %collective-permute-start.11 = (bf16[1,128,512]{2,1,0:T(8,128)(2,1)S(1)}, bf16[1,128,512]{2,1,0:T(8,128)(2,1)S(1)}, u32[]{:S(2)}, u32[]{:S(2)}) collective-permute-start(bf16[1,128,512]{2,1,0:T(8,128)(2,1)S(1)} %get-tuple-element.67), channel_id=1, source_target_pairs={{0,35},{1,0},{2,1},{3,2},{4,39},{5,4},{6,5},{7,6},{8,43},{9,8},{10... | collective-permute-start | bytes 393224 | tf_op jit(solution)/shard_map/ppermute | solution.py:253
  36.6 7.7 %collective-permute-start.8 = (bf16[1,128,512]{2,1,0:T(8,128)(2,1)S(1)}, bf16[1,128,512]{2,1,0:T(8,128)(2,1)S(1)}, u32[]{:S(2)}, u32[]{:S(2)}) collective-permute-start(bf16[1,128,512]{2,1,0:T(8,128)(2,1)S(1)} %get-tuple-element.64), channel_id=1, source_target_pairs={{0,4},{4,8},{8,12},{1,5},{5,9},{9,13},{2,6},{6,10},{10,14},{3,7},{... | collective-permute-start | bytes 393224 | tf_op jit(solution)/shard_map/ppermute | solution.py:334
  39.2 6.3 %collective-permute-start.9 = (bf16[1,128,512]{2,1,0:T(8,128)(2,1)S(1)}, bf16[1,128,512]{2,1,0:T(8,128)(2,1)S(1)}, u32[]{:S(2)}, u32[]{:S(2)}) collective-permute-start(bf16[1,128,512]{2,1,0:T(8,128)(2,1)S(1)} %get-tuple-element.65), channel_id=1, source_target_pairs={{4,0},{8,4},{12,8},{5,1},{9,5},{13,9},{6,2},{10,6},{14,10},{7,3},{... | collective-permute-start | bytes 393224 | tf_op jit(solution)/shard_map/ppermute | solution.py:334
  40.5 6.4 %collective-permute-start.12 = (bf16[64,512]{1,0:T(8,128)(2,1)S(1)}, bf16[64,512]{1,0:T(8,128)(2,1)S(1)}, u32[]{:S(2)}, u32[]{:S(2)}) collective-permute-start(bf16[64,512]{1,0:T(8,128)(2,1)S(1)} %slice.14), channel_id=1, source_target_pairs={{0,64},{1,65},{2,66},{3,67},{4,68},{5,69},{6,70},{7,71},{8,72},{9,... | collective-permute-start | bytes 196616 | tf_op jit(solution)/shard_map/ppermute | solution.py:253
  42.7 4.2 %collective-permute-start.13 = (bf16[64,512]{1,0:T(8,128)(2,1)S(1)}, bf16[64,512]{1,0:T(8,128)(2,1)S(1)}, u32[]{:S(2)}, u32[]{:S(2)}) collective-permute-start(bf16[64,512]{1,0:T(8,128)(2,1)S(1)} %slice.15), channel_id=1, source_target_pairs={{0,192},{1,193},{2,194},{3,195},{4,196},{5,197},{6,198},{7,199},{8... | collective-permute-start | bytes 196616 | tf_op jit(solution)/shard_map/ppermute | solution.py:253
  46.9 13.9 %collective-permute-start.14 = (bf16[512,512]{1,0:T(8,128)(2,1)S(1)}, bf16[512,512]{1,0:T(8,128)(2,1)S(1)}, u32[]{:S(2)}, u32[]{:S(2)}) collective-permute-start(bf16[512,512]{1,0:T(8,128)(2,1)S(1)} %constant_dynamic-update-slice_fusion.5.m0), channel_id=1, source_target_pairs={{0,4},{1,5},{2,6},{3,7},{4,8},{5,9},{6,10},{7,11},{8,12},{9,13},{1... | collective-permute-start | bytes 1572872 | tf_op jit(solution)/shard_map/ppermute | solution.py:253
  49.3 11.6 %collective-permute-start.15 = (bf16[512,512]{1,0:T(8,128)(2,1)S(1)}, bf16[512,512]{1,0:T(8,128)(2,1)S(1)}, u32[]{:S(2)}, u32[]{:S(2)}) collective-permute-start(bf16[512,512]{1,0:T(8,128)(2,1)S(1)} %constant_dynamic-update-slice_fusion.5.m0), channel_id=1, source_target_pairs={{0,12},{1,13},{2,14},{3,15},{4,0},{5,1},{6,2},{7,3},{8,4},{9,5},{1... | collective-permute-start | bytes 1572872 | tf_op jit(solution)/shard_map/ppermute | solution.py:253
  51.0 30.8 %collective-permute-start.18 = (bf16[512,512]{1,0:T(8,128)(2,1)S(1)}, bf16[512,512]{1,0:T(8,128)(2,1)S(1)}, u32[]{:S(2)}, u32[]{:S(2)}) collective-permute-start(bf16[512,512]{1,0:T(8,128)(2,1)S(1)} %constant_dynamic-update-slice_fusion.5.m0), channel_id=1, source_target_pairs={{0,16},{1,17},{2,18},{3,19},{4,20},{5,21},{6,22},{7,23},{8,24},{9,... | collective-permute-start | bytes 1572872 | tf_op jit(solution)/shard_map/ppermute | solution.py:253
  60.9 20.9 %collective-permute-start.19 = (bf16[512,512]{1,0:T(8,128)(2,1)S(1)}, bf16[512,512]{1,0:T(8,128)(2,1)S(1)}, u32[]{:S(2)}, u32[]{:S(2)}) collective-permute-start(bf16[512,512]{1,0:T(8,128)(2,1)S(1)} %collective-permute-done.14.m1), channel_id=1, source_target_pairs={{0,16},{1,17},{2,18},{3,19},{4,20},{5,21},{6,22},{7,23},{8,24},{9,... | collective-permute-start | bytes 1572872 | tf_op jit(solution)/shard_map/ppermute | solution.py:253
  61.1 20.8 %collective-permute-start.20 = (bf16[512,512]{1,0:T(8,128)(2,1)S(1)}, bf16[512,512]{1,0:T(8,128)(2,1)S(1)}, u32[]{:S(2)}, u32[]{:S(2)}) collective-permute-start(bf16[512,512]{1,0:T(8,128)(2,1)S(1)} %collective-permute-done.15.m2), channel_id=1, source_target_pairs={{0,16},{1,17},{2,18},{3,19},{4,20},{5,21},{6,22},{7,23},{8,24},{9,... | collective-permute-start | bytes 1572872 | tf_op jit(solution)/shard_map/ppermute | solution.py:253
  61.6 11.0 %collective-permute-start.16 = (bf16[256,512]{1,0:T(8,128)(2,1)S(1)}, bf16[256,512]{1,0:T(8,128)(2,1)S(1)}, u32[]{:S(2)}, u32[]{:S(2)}) collective-permute-start(bf16[256,512]{1,0:T(8,128)(2,1)S(1)} %slice.16), channel_id=1, source_target_pairs={{0,4},{1,5},{2,6},{3,7},{4,8},{5,9},{6,10},{7,11},{8,12},{9,13},{1... | collective-permute-start | bytes 786440 | tf_op jit(solution)/shard_map/ppermute | solution.py:253
  61.7 11.0 %collective-permute-start.17 = (bf16[256,512]{1,0:T(8,128)(2,1)S(1)}, bf16[256,512]{1,0:T(8,128)(2,1)S(1)}, u32[]{:S(2)}, u32[]{:S(2)}) collective-permute-start(bf16[256,512]{1,0:T(8,128)(2,1)S(1)} %slice.17), channel_id=1, source_target_pairs={{0,12},{1,13},{2,14},{3,15},{4,0},{5,1},{6,2},{7,3},{8,4},{9,5},{1... | collective-permute-start | bytes 786440 | tf_op jit(solution)/shard_map/ppermute | solution.py:253
  72.7 9.1 %collective-permute-start.21 = (bf16[256,512]{1,0:T(8,128)(2,1)S(1)}, bf16[256,512]{1,0:T(8,128)(2,1)S(1)}, u32[]{:S(2)}, u32[]{:S(2)}) collective-permute-start(bf16[256,512]{1,0:T(8,128)(2,1)S(1)} %collective-permute-done.16.m3), channel_id=1, source_target_pairs={{0,16},{1,17},{2,18},{3,19},{4,20},{5,21},{6,22},{7,23},{8,24},{9,... | collective-permute-start | bytes 786440 | tf_op jit(solution)/shard_map/ppermute | solution.py:253
  73.5 8.4 %collective-permute-start.22 = (bf16[256,512]{1,0:T(8,128)(2,1)S(1)}, bf16[256,512]{1,0:T(8,128)(2,1)S(1)}, u32[]{:S(2)}, u32[]{:S(2)}) collective-permute-start(bf16[256,512]{1,0:T(8,128)(2,1)S(1)} %collective-permute-done.17.m4), channel_id=1, source_target_pairs={{0,16},{1,17},{2,18},{3,19},{4,20},{5,21},{6,22},{7,23},{8,24},{9,... | collective-permute-start | bytes 786440 | tf_op jit(solution)/shard_map/ppermute | solution.py:253
  (16 other events, 360.4 us)

commit v5 on v4

--- a/solution.py
+++ b/solution.py
@@ -343,7 +343,6 @@
     up, down = sent(column, UP_FIRST), sent(column, DOWN_FIRST)
     low_y, high_y = faced(3), faced(2)
     low_z, high_z = sent(faces[5], UP_Z), sent(faces[4], DOWN_Z)
-    up, down, low_x, high_x = tied((up, down, low_x, high_x))
     near_faces = [low_x, high_x, low_y, high_y, low_z, high_z]
     table, near = kernel(
         table_kernel,

time: 88.9 us -> 86.3 us (0.971)
  starting transfers between devices: 43.7 us -> 42.3 us
  waiting for transfers between devices: 4.56 us -> 3.35 us
    ppermute x4, waiting for transfers between devices: 4.51 us -> 2.78 us  [faced(): lax.ppermute(faces[face], axes, [(b, a) for a, b in pairs] if face % 2 ==...]
  transfers between devices with their start and end apart: 23 -> 23, of which waited for: 2 -> 2; matrix products, arithmetic and copies ran while one was open for 0% -> 0% of each run, Pallas kernels for 34% -> 35%
where the time goes in v5:
time: 86.3 us; the launch traced here: 86 us
  starting transfers between devices  42.3 us (49%)
  Pallas kernels  39 us (45%)
  waiting for transfers between devices  3.35 us (4%)
  between operations  1.17 us (1%)
    pallas_call x8, Pallas kernels, kernel(): pl.pallas_call(body, grid=(1,), out_shape=outs, in_specs=specs, out_specs...  39 us
    ppermute x19, starting transfers between devices, sent(): return lax.ppermute(rows, AXES, pairs)  29.8 us
    ppermute x4, starting transfers between devices, faced(): lax.ppermute(faces[face], axes, [(b, a) for a, b in pairs] if face % 2 ==...  12.6 us
    ppermute x4, waiting for transfers between devices, faced(): lax.ppermute(faces[face], axes, [(b, a) for a, b in pairs] if face % 2 ==...  2.78 us
  transfers between devices with their start and end apart: 23, of which 2 were waited for; matrix products, arithmetic and copies ran while one was open for 0% of the time, Pallas kernels for 35%

profile of v5, /device:TPU:1, one launch (start us, length us, event | category | flops | bytes accessed | tf_op | source)
XLA Modules:
  0.0 86.0 jit_solution(924368422212077773)
XLA Ops:
  0.7 2.3 %shard_map.256 = (bf16[16,512]{1,0:T(8,128)(2,1)S(1)}, bf16[16,512]{1,0:T(8,128)(2,1)S(1)}, f32[128,512]{1,0:T(8,128)S(1)}, s32[16,64]{1,0:T(8,128)S(1)}, bf16[3...) custom-call(bf16[1024,512]{1,0:T(8,128)(2,1)} %fine.5, s32[1,1024]{1,0:T(1,128)} %bitcast.29, ...), custom_call_target="tpu_custom_call" | custom-call | tf_op jit(solution)/shard_map/pallas_call | solution.py:272
  3.0 2.5 %collective-permute-start = (bf16[16,512]{1,0:T(8,128)(2,1)S(1)}, bf16[16,512]{1,0:T(8,128)(2,1)S(1)}, u32[]{:S(2)}, u32[]{:S(2)}) collective-permute-start(bf16[16,512]{1,0:T(8,128)(2,1)S(1)} %get-tuple-element.45), channel_id=1, source_target_pairs={{0,1},{1,2},{2,3},{3,32},{4,5},{5,6},{6,7},{7,36},{8,9},{9,10},{10... | collective-permute-start | bytes 49160 | tf_op jit(solution)/shard_map/ppermute | solution.py:253
  5.5 4.0 %collective-permute-start.1 = (bf16[16,512]{1,0:T(8,128)(2,1)S(1)}, bf16[16,512]{1,0:T(8,128)(2,1)S(1)}, u32[]{:S(2)}, u32[]{:S(2)}) collective-permute-start(bf16[16,512]{1,0:T(8,128)(2,1)S(1)} %get-tuple-element.45), channel_id=1, source_target_pairs={{0,35},{1,0},{2,1},{3,2},{4,39},{5,4},{6,5},{7,6},{8,43},{9,8},{10... | collective-permute-start | bytes 49160 | tf_op jit(solution)/shard_map/ppermute | solution.py:253
  9.5 4.0 %shard_map.257 = (bf16[1024,512]{1,0:T(8,128)(2,1)S(1)}, bf16[512,512]{1,0:T(8,128)(2,1)S(1)}, f32[16,512]{1,0:T(8,128)S(1)}, bf16[1,128,512]{2,1,0:T(8,128)(2,1...) custom-call(bf16[16,512]{1,0:T(8,128)(2,1)S(1)} %get-tuple-element.4, ...), custom_call_target="tpu_custom_call" | custom-call | tf_op jit(solution)/shard_map/pallas_call | solution.py:272
  13.7 1.6 %collective-permute-start.4 = (bf16[48,512]{1,0:T(8,128)(2,1)S(1)}, bf16[48,512]{1,0:T(8,128)(2,1)S(1)}, u32[]{:S(2)}, u32[]{:S(2)}) collective-permute-start(bf16[48,512]{1,0:T(8,128)(2,1)S(1)} %pad_maximum_fusion), channel_id=1, source_target_pairs={{0,3},{1,32},{2,33},{3,34},{4,7},{5,36},{6,37},{7,38},{8,11},{9,40... | collective-permute-start | bytes 147464 | tf_op jit(solution)/shard_map/ppermute | solution.py:253
  15.3 2.9 %collective-permute-start.5 = (bf16[32,512]{1,0:T(8,128)(2,1)S(1)}, bf16[32,512]{1,0:T(8,128)(2,1)S(1)}, u32[]{:S(2)}, u32[]{:S(2)}) collective-permute-start(bf16[32,512]{1,0:T(8,128)(2,1)S(1)} %pad_maximum_fusion.1), channel_id=1, source_target_pairs={{0,33},{1,34},{2,35},{3,0},{4,37},{5,38},{6,39},{7,4},{8,41},{9,42... | collective-permute-start | bytes 98312 | tf_op jit(solution)/shard_map/ppermute | solution.py:253
  18.2 7.5 %collective-permute-start.2 = (bf16[1,128,512]{2,1,0:T(8,128)(2,1)S(1)}, bf16[1,128,512]{2,1,0:T(8,128)(2,1)S(1)}, u32[]{:S(2)}, u32[]{:S(2)}) collective-permute-start(bf16[1,128,512]{2,1,0:T(8,128)(2,1)S(1)} %get-tuple-element.48), channel_id=1, source_target_pairs={{0,16},{16,32},{32,48},{48,64},{64,80},{80,96},{96,112},{112,128},... | collective-permute-start | bytes 393224 | tf_op jit(solution)/shard_map/ppermute | solution.py:334
  25.8 1.4 %collective-permute-start.10 = (bf16[128,512]{1,0:T(8,128)(2,1)S(1)}, bf16[128,512]{1,0:T(8,128)(2,1)S(1)}, u32[]{:S(2)}, u32[]{:S(2)}) collective-permute-start(bf16[128,512]{1,0:T(8,128)(2,1)S(1)} %get-tuple-element.83), channel_id=1, source_target_pairs={{0,64},{1,65},{2,66},{3,67},{4,68},{5,69},{6,70},{7,71},{8,72},{9,... | collective-permute-start | bytes 393224 | tf_op jit(solution)/shard_map/ppermute | solution.py:253
  27.2 1.5 %collective-permute-start.11 = (bf16[128,512]{1,0:T(8,128)(2,1)S(1)}, bf16[128,512]{1,0:T(8,128)(2,1)S(1)}, u32[]{:S(2)}, u32[]{:S(2)}) collective-permute-start(bf16[128,512]{1,0:T(8,128)(2,1)S(1)} %get-tuple-element.83), channel_id=1, source_target_pairs={{0,192},{1,193},{2,194},{3,195},{4,196},{5,197},{6,198},{7,199},{8... | collective-permute-start | bytes 393224 | tf_op jit(solution)/shard_map/ppermute | solution.py:253
  28.7 1.9 %collective-permute-start.3 = (bf16[1,128,512]{2,1,0:T(8,128)(2,1)S(1)}, bf16[1,128,512]{2,1,0:T(8,128)(2,1)S(1)}, u32[]{:S(2)}, u32[]{:S(2)}) collective-permute-start(bf16[1,128,512]{2,1,0:T(8,128)(2,1)S(1)} %get-tuple-element.49), channel_id=1, source_target_pairs={{16,0},{32,16},{48,32},{64,48},{80,64},{96,80},{112,96},{128,112},... | collective-permute-start | bytes 393224 | tf_op jit(solution)/shard_map/ppermute | solution.py:334
  30.6 1.9 %collective-permute-start.6 = (bf16[1,128,512]{2,1,0:T(8,128)(2,1)S(1)}, bf16[1,128,512]{2,1,0:T(8,128)(2,1)S(1)}, u32[]{:S(2)}, u32[]{:S(2)}) collective-permute-start(bf16[1,128,512]{2,1,0:T(8,128)(2,1)S(1)} %get-tuple-element.56), channel_id=1, source_target_pairs={{0,4},{4,8},{8,12},{1,5},{5,9},{9,13},{2,6},{6,10},{10,14},{3,7},{... | collective-permute-start | bytes 393224 | tf_op jit(solution)/shard_map/ppermute | solution.py:334
  33.8 2.5 %collective-permute-start.8 = (bf16[1,128,512]{2,1,0:T(8,128)(2,1)S(1)}, bf16[1,128,512]{2,1,0:T(8,128)(2,1)S(1)}, u32[]{:S(2)}, u32[]{:S(2)}) collective-permute-start(bf16[1,128,512]{2,1,0:T(8,128)(2,1)S(1)} %get-tuple-element.58), channel_id=1, source_target_pairs={{0,1},{1,2},{2,3},{3,32},{4,5},{5,6},{6,7},{7,36},{8,9},{9,10},{10... | collective-permute-start | bytes 393224 | tf_op jit(solution)/shard_map/ppermute | solution.py:253
  36.6 2.8 %collective-permute-done.3.g1 = bf16[1,128,512]{2,1,0:T(8,128)(2,1)S(1)} collective-permute-done((bf16[1,128,512]{2,1,0:T(8,128)(2,1)S(1)}, bf16[1,128,512]{2,1,0:T(8,128)(2,1)S(1)}, u32[]{:S(2)}, u32[]{:S(2)}) %collective-permute-start.3) | collective-permute-done | bytes 131104 | tf_op jit(solution)/shard_map/ppermute | solution.py:334
  39.4 2.7 %collective-permute-start.13 = (bf16[64,512]{1,0:T(8,128)(2,1)S(1)}, bf16[64,512]{1,0:T(8,128)(2,1)S(1)}, u32[]{:S(2)}, u32[]{:S(2)}) collective-permute-start(bf16[64,512]{1,0:T(8,128)(2,1)S(1)} %slice.19), channel_id=1, source_target_pairs={{0,192},{1,193},{2,194},{3,195},{4,196},{5,197},{6,198},{7,199},{8... | collective-permute-start | bytes 196616 | tf_op jit(solution)/shard_map/ppermute | solution.py:253
  42.1 1.4 %shard_map.258 = (bf16[1792,512]{1,0:T(8,128)(2,1)S(1)}, s32[1024,8]{1,0:T(8,128)S(1)}) custom-call(bf16[1024,512]{1,0:T(8,128)(2,1)S(1)} %get-tuple-element.44.sender, bf16[1,128,512]{2,1,0:T(8,128)(2,1)S(1)} %collective-permute-done.2.g0, bf16[1,128,512]{2,1,0:T(8,128)(2,1)S(1)} %collective-permute-done.3.g1, ...), custom_call_target="tpu_custom_call" | custom-call | tf_op jit(solution)/shard_map/pallas_call | solution.py:272
  44.0 2.8 %collective-permute-start.14 = (bf16[512,512]{1,0:T(8,128)(2,1)S(1)}, bf16[512,512]{1,0:T(8,128)(2,1)S(1)}, u32[]{:S(2)}, u32[]{:S(2)}) collective-permute-start(bf16[512,512]{1,0:T(8,128)(2,1)S(1)} %constant_dynamic-update-slice_fusion.5.m0), channel_id=1, source_target_pairs={{0,4},{1,5},{2,6},{3,7},{4,8},{5,9},{6,10},{7,11},{8,12},{9,13},{1... | collective-permute-start | bytes 1572872 | tf_op jit(solution)/shard_map/ppermute | solution.py:253
  46.8 1.4 %collective-permute-start.15 = (bf16[512,512]{1,0:T(8,128)(2,1)S(1)}, bf16[512,512]{1,0:T(8,128)(2,1)S(1)}, u32[]{:S(2)}, u32[]{:S(2)}) collective-permute-start(bf16[512,512]{1,0:T(8,128)(2,1)S(1)} %constant_dynamic-update-slice_fusion.5.m0), channel_id=1, source_target_pairs={{0,12},{1,13},{2,14},{3,15},{4,0},{5,1},{6,2},{7,3},{8,4},{9,5},{1... | collective-permute-start | bytes 1572872 | tf_op jit(solution)/shard_map/ppermute | solution.py:253
  48.2 1.7 %collective-permute-start.18 = (bf16[512,512]{1,0:T(8,128)(2,1)S(1)}, bf16[512,512]{1,0:T(8,128)(2,1)S(1)}, u32[]{:S(2)}, u32[]{:S(2)}) collective-permute-start(bf16[512,512]{1,0:T(8,128)(2,1)S(1)} %constant_dynamic-update-slice_fusion.5.m0), channel_id=1, source_target_pairs={{0,16},{1,17},{2,18},{3,19},{4,20},{5,21},{6,22},{7,23},{8,24},{9,... | collective-permute-start | bytes 1572872 | tf_op jit(solution)/shard_map/ppermute | solution.py:253
  50.0 8.4 %shard_map.259.rest_0_ = f32[384,512]{1,0:T(8,128)S(1)} custom-call(bf16[1792,512]{1,0:T(8,128)(2,1)S(1)} %get-tuple-element.79.table, bf16[1024,512]{1,0:T(8,128)(2,1)S(1)} %copy-done, s32[1024,8]{1,0:T(8,128)S(1)} %get-tuple-element.65.nbrs, bf16[1024,512]{1,0:T(8,128)(2,1)S(1)} %copy-done.1, f32[1,512]{1,0:T(1,128)S(1)} %bitcast.17, ...), custom_call_target="tpu_custom_call" | custom-call | flops 5100000256 | bytes 9000000 | tf_op jit(solution)/shard_map/pallas_call | solution.py:272
  60.3 1.5 %collective-permute-start.17 = (bf16[256,512]{1,0:T(8,128)(2,1)S(1)}, bf16[256,512]{1,0:T(8,128)(2,1)S(1)}, u32[]{:S(2)}, u32[]{:S(2)}) collective-permute-start(bf16[256,512]{1,0:T(8,128)(2,1)S(1)} %slice.17), channel_id=1, source_target_pairs={{0,12},{1,13},{2,14},{3,15},{4,0},{5,1},{6,2},{7,3},{8,4},{9,5},{1... | collective-permute-start | bytes 786440 | tf_op jit(solution)/shard_map/ppermute | solution.py:253
  61.8 8.4 %shard_map.260.rest_1_ = f32[384,512]{1,0:T(8,128)S(1)} custom-call(bf16[1792,512]{1,0:T(8,128)(2,1)S(1)} %get-tuple-element.79.table, bf16[1024,512]{1,0:T(8,128)(2,1)S(1)} %copy-done, s32[1024,8]{1,0:T(8,128)S(1)} %get-tuple-element.65.nbrs, bf16[1024,512]{1,0:T(8,128)(2,1)S(1)} %copy-done.1, f32[1,512]{1,0:T(1,128)S(1)} %bitcast.18, ...), custom_call_target="tpu_custom_call" | custom-call | flops 5100000256 | bytes 9000000 | tf_op jit(solution)/shard_map/pallas_call | solution.py:272
  71.2 2.4 %shard_map.261.found = bf16[1024,512]{1,0:T(8,128)(2,1)S(1)} custom-call(s32[16,64]{1,0:T(8,128)S(1)} %get-tuple-element.42.slots, bf16[512,512]{1,0:T(8,128)(2,1)S(1)} %constant_dynamic-update-slice_fusion.5.m0, bf16[512,512]{1,0:T(8,128)(2,1)S(1)} %collective-permute-done.14.m1, bf16[512,512]{1,0:T(8,128)(2,1)S(1)} %collective-permute-done.15.m2, ...), custom_call_target="tpu_custom_call" | custom-call | flops 2000000000 | bytes 4000000 | tf_op jit(solution)/shard_map/pallas_call | solution.py:272
  73.6 5.6 %shard_map.262.rest_2_ = f32[256,512]{1,0:T(8,128)S(1)} custom-call(bf16[1792,512]{1,0:T(8,128)(2,1)S(1)} %get-tuple-element.79.table, bf16[1024,512]{1,0:T(8,128)(2,1)S(1)} %copy-done, s32[1024,8]{1,0:T(8,128)S(1)} %get-tuple-element.65.nbrs, bf16[1024,512]{1,0:T(8,128)(2,1)S(1)} %copy-done.1, f32[1,512]{1,0:T(1,128)S(1)} %bitcast.19, ...), custom_call_target="tpu_custom_call" | custom-call | flops 3400000000 | bytes 6000000 | tf_op jit(solution)/shard_map/pallas_call | solution.py:272
  79.3 6.7 %shard_map.263 = (bf16[1024,512]{1,0:T(8,128)(2,1)}, bf16[128,512]{1,0:T(8,128)(2,1)}, bf16[16,512]{1,0:T(8,128)(2,1)}) custom-call(bf16[1024,512]{1,0:T(8,128)(2,1)} %copy-done.2, bf16[512,512]{1,0:T(8,128)(2,1)S(1)} %collective-permute-done.18.o0, bf16[512,512]{1,0:T(8,128)(2,1)S(1)} %collective-permute-done.19.o1, ...), custom_call_target="tpu_custom_call" | custom-call | tf_op jit(solution)/shard_map/pallas_call | solution.py:272
  (79 shorter events, 5.3 us)
Async XLA Ops:
  3.0 10.7 %collective-permute-start = (bf16[16,512]{1,0:T(8,128)(2,1)S(1)}, bf16[16,512]{1,0:T(8,128)(2,1)S(1)}, u32[]{:S(2)}, u32[]{:S(2)}) collective-permute-start(bf16[16,512]{1,0:T(8,128)(2,1)S(1)} %get-tuple-element.45), channel_id=1, source_target_pairs={{0,1},{1,2},{2,3},{3,32},{4,5},{5,6},{6,7},{7,36},{8,9},{9,10},{10... | collective-permute-start | bytes 49160 | tf_op jit(solution)/shard_map/ppermute | solution.py:253
  5.5 8.1 %collective-permute-start.1 = (bf16[16,512]{1,0:T(8,128)(2,1)S(1)}, bf16[16,512]{1,0:T(8,128)(2,1)S(1)}, u32[]{:S(2)}, u32[]{:S(2)}) collective-permute-start(bf16[16,512]{1,0:T(8,128)(2,1)S(1)} %get-tuple-element.45), channel_id=1, source_target_pairs={{0,35},{1,0},{2,1},{3,2},{4,39},{5,4},{6,5},{7,6},{8,43},{9,8},{10... | collective-permute-start | bytes 49160 | tf_op jit(solution)/shard_map/ppermute | solution.py:253
  9.5 40.4 %copy-start.12 = (bf16[512,512]{1,0:T(8,128)(2,1)S(1)}, bf16[512,512]{1,0:T(8,128)(2,1)}, u32[]{:S(2)}) copy-start(bf16[512,512]{1,0:T(8,128)(2,1)} %node_out.5) | copy-start | bytes 1572868
  13.7 12.1 %collective-permute-start.4 = (bf16[48,512]{1,0:T(8,128)(2,1)S(1)}, bf16[48,512]{1,0:T(8,128)(2,1)S(1)}, u32[]{:S(2)}, u32[]{:S(2)}) collective-permute-start(bf16[48,512]{1,0:T(8,128)(2,1)S(1)} %pad_maximum_fusion), channel_id=1, source_target_pairs={{0,3},{1,32},{2,33},{3,34},{4,7},{5,36},{6,37},{7,38},{8,11},{9,40... | collective-permute-start | bytes 147464 | tf_op jit(solution)/shard_map/ppermute | solution.py:253
  15.3 10.5 %collective-permute-start.5 = (bf16[32,512]{1,0:T(8,128)(2,1)S(1)}, bf16[32,512]{1,0:T(8,128)(2,1)S(1)}, u32[]{:S(2)}, u32[]{:S(2)}) collective-permute-start(bf16[32,512]{1,0:T(8,128)(2,1)S(1)} %pad_maximum_fusion.1), channel_id=1, source_target_pairs={{0,33},{1,34},{2,35},{3,0},{4,37},{5,38},{6,39},{7,4},{8,41},{9,42... | collective-permute-start | bytes 98312 | tf_op jit(solution)/shard_map/ppermute | solution.py:253
  18.2 14.3 %collective-permute-start.2 = (bf16[1,128,512]{2,1,0:T(8,128)(2,1)S(1)}, bf16[1,128,512]{2,1,0:T(8,128)(2,1)S(1)}, u32[]{:S(2)}, u32[]{:S(2)}) collective-permute-start(bf16[1,128,512]{2,1,0:T(8,128)(2,1)S(1)} %get-tuple-element.48), channel_id=1, source_target_pairs={{0,16},{16,32},{32,48},{48,64},{64,80},{80,96},{96,112},{112,128},... | collective-permute-start | bytes 393224 | tf_op jit(solution)/shard_map/ppermute | solution.py:334
  25.8 8.0 %collective-permute-start.10 = (bf16[128,512]{1,0:T(8,128)(2,1)S(1)}, bf16[128,512]{1,0:T(8,128)(2,1)S(1)}, u32[]{:S(2)}, u32[]{:S(2)}) collective-permute-start(bf16[128,512]{1,0:T(8,128)(2,1)S(1)} %get-tuple-element.83), channel_id=1, source_target_pairs={{0,64},{1,65},{2,66},{3,67},{4,68},{5,69},{6,70},{7,71},{8,72},{9,... | collective-permute-start | bytes 393224 | tf_op jit(solution)/shard_map/ppermute | solution.py:253
  27.2 9.2 %collective-permute-start.11 = (bf16[128,512]{1,0:T(8,128)(2,1)S(1)}, bf16[128,512]{1,0:T(8,128)(2,1)S(1)}, u32[]{:S(2)}, u32[]{:S(2)}) collective-permute-start(bf16[128,512]{1,0:T(8,128)(2,1)S(1)} %get-tuple-element.83), channel_id=1, source_target_pairs={{0,192},{1,193},{2,194},{3,195},{4,196},{5,197},{6,198},{7,199},{8... | collective-permute-start | bytes 393224 | tf_op jit(solution)/shard_map/ppermute | solution.py:253
  28.7 10.7 %collective-permute-start.3 = (bf16[1,128,512]{2,1,0:T(8,128)(2,1)S(1)}, bf16[1,128,512]{2,1,0:T(8,128)(2,1)S(1)}, u32[]{:S(2)}, u32[]{:S(2)}) collective-permute-start(bf16[1,128,512]{2,1,0:T(8,128)(2,1)S(1)} %get-tuple-element.49), channel_id=1, source_target_pairs={{16,0},{32,16},{48,32},{64,48},{80,64},{96,80},{112,96},{128,112},... | collective-permute-start | bytes 393224 | tf_op jit(solution)/shard_map/ppermute | solution.py:334
  30.6 8.8 %collective-permute-start.6 = (bf16[1,128,512]{2,1,0:T(8,128)(2,1)S(1)}, bf16[1,128,512]{2,1,0:T(8,128)(2,1)S(1)}, u32[]{:S(2)}, u32[]{:S(2)}) collective-permute-start(bf16[1,128,512]{2,1,0:T(8,128)(2,1)S(1)} %get-tuple-element.56), channel_id=1, source_target_pairs={{0,4},{4,8},{8,12},{1,5},{5,9},{9,13},{2,6},{6,10},{10,14},{3,7},{... | collective-permute-start | bytes 393224 | tf_op jit(solution)/shard_map/ppermute | solution.py:334
  32.5 9.6 %collective-permute-start.7 = (bf16[1,128,512]{2,1,0:T(8,128)(2,1)S(1)}, bf16[1,128,512]{2,1,0:T(8,128)(2,1)S(1)}, u32[]{:S(2)}, u32[]{:S(2)}) collective-permute-start(bf16[1,128,512]{2,1,0:T(8,128)(2,1)S(1)} %get-tuple-element.57), channel_id=1, source_target_pairs={{4,0},{8,4},{12,8},{5,1},{9,5},{13,9},{6,2},{10,6},{14,10},{7,3},{... | collective-permute-start | bytes 393224 | tf_op jit(solution)/shard_map/ppermute | solution.py:334
  33.8 8.2 %collective-permute-start.8 = (bf16[1,128,512]{2,1,0:T(8,128)(2,1)S(1)}, bf16[1,128,512]{2,1,0:T(8,128)(2,1)S(1)}, u32[]{:S(2)}, u32[]{:S(2)}) collective-permute-start(bf16[1,128,512]{2,1,0:T(8,128)(2,1)S(1)} %get-tuple-element.58), channel_id=1, source_target_pairs={{0,1},{1,2},{2,3},{3,32},{4,5},{5,6},{6,7},{7,36},{8,9},{9,10},{10... | collective-permute-start | bytes 393224 | tf_op jit(solution)/shard_map/ppermute | solution.py:253
  36.3 5.7 %collective-permute-start.9 = (bf16[1,128,512]{2,1,0:T(8,128)(2,1)S(1)}, bf16[1,128,512]{2,1,0:T(8,128)(2,1)S(1)}, u32[]{:S(2)}, u32[]{:S(2)}) collective-permute-start(bf16[1,128,512]{2,1,0:T(8,128)(2,1)S(1)} %get-tuple-element.59), channel_id=1, source_target_pairs={{0,35},{1,0},{2,1},{3,2},{4,39},{5,4},{6,5},{7,6},{8,43},{9,8},{10... | collective-permute-start | bytes 393224 | tf_op jit(solution)/shard_map/ppermute | solution.py:253
  39.4 4.6 %collective-permute-start.12 = (bf16[64,512]{1,0:T(8,128)(2,1)S(1)}, bf16[64,512]{1,0:T(8,128)(2,1)S(1)}, u32[]{:S(2)}, u32[]{:S(2)}) collective-permute-start(bf16[64,512]{1,0:T(8,128)(2,1)S(1)} %slice.18), channel_id=1, source_target_pairs={{0,64},{1,65},{2,66},{3,67},{4,68},{5,69},{6,70},{7,71},{8,72},{9,... | collective-permute-start | bytes 196616 | tf_op jit(solution)/shard_map/ppermute | solution.py:253
  39.4 4.6 %collective-permute-start.13 = (bf16[64,512]{1,0:T(8,128)(2,1)S(1)}, bf16[64,512]{1,0:T(8,128)(2,1)S(1)}, u32[]{:S(2)}, u32[]{:S(2)}) collective-permute-start(bf16[64,512]{1,0:T(8,128)(2,1)S(1)} %slice.19), channel_id=1, source_target_pairs={{0,192},{1,193},{2,194},{3,195},{4,196},{5,197},{6,198},{7,199},{8... | collective-permute-start | bytes 196616 | tf_op jit(solution)/shard_map/ppermute | solution.py:253
  44.0 14.3 %collective-permute-start.14 = (bf16[512,512]{1,0:T(8,128)(2,1)S(1)}, bf16[512,512]{1,0:T(8,128)(2,1)S(1)}, u32[]{:S(2)}, u32[]{:S(2)}) collective-permute-start(bf16[512,512]{1,0:T(8,128)(2,1)S(1)} %constant_dynamic-update-slice_fusion.5.m0), channel_id=1, source_target_pairs={{0,4},{1,5},{2,6},{3,7},{4,8},{5,9},{6,10},{7,11},{8,12},{9,13},{1... | collective-permute-start | bytes 1572872 | tf_op jit(solution)/shard_map/ppermute | solution.py:253
  46.8 11.5 %collective-permute-start.15 = (bf16[512,512]{1,0:T(8,128)(2,1)S(1)}, bf16[512,512]{1,0:T(8,128)(2,1)S(1)}, u32[]{:S(2)}, u32[]{:S(2)}) collective-permute-start(bf16[512,512]{1,0:T(8,128)(2,1)S(1)} %constant_dynamic-update-slice_fusion.5.m0), channel_id=1, source_target_pairs={{0,12},{1,13},{2,14},{3,15},{4,0},{5,1},{6,2},{7,3},{8,4},{9,5},{1... | collective-permute-start | bytes 1572872 | tf_op jit(solution)/shard_map/ppermute | solution.py:253
  48.2 31.0 %collective-permute-start.18 = (bf16[512,512]{1,0:T(8,128)(2,1)S(1)}, bf16[512,512]{1,0:T(8,128)(2,1)S(1)}, u32[]{:S(2)}, u32[]{:S(2)}) collective-permute-start(bf16[512,512]{1,0:T(8,128)(2,1)S(1)} %constant_dynamic-update-slice_fusion.5.m0), channel_id=1, source_target_pairs={{0,16},{1,17},{2,18},{3,19},{4,20},{5,21},{6,22},{7,23},{8,24},{9,... | collective-permute-start | bytes 1572872 | tf_op jit(solution)/shard_map/ppermute | solution.py:253
  58.4 20.9 %collective-permute-start.19 = (bf16[512,512]{1,0:T(8,128)(2,1)S(1)}, bf16[512,512]{1,0:T(8,128)(2,1)S(1)}, u32[]{:S(2)}, u32[]{:S(2)}) collective-permute-start(bf16[512,512]{1,0:T(8,128)(2,1)S(1)} %collective-permute-done.14.m1), channel_id=1, source_target_pairs={{0,16},{1,17},{2,18},{3,19},{4,20},{5,21},{6,22},{7,23},{8,24},{9,... | collective-permute-start | bytes 1572872 | tf_op jit(solution)/shard_map/ppermute | solution.py:253
  58.5 20.8 %collective-permute-start.20 = (bf16[512,512]{1,0:T(8,128)(2,1)S(1)}, bf16[512,512]{1,0:T(8,128)(2,1)S(1)}, u32[]{:S(2)}, u32[]{:S(2)}) collective-permute-start(bf16[512,512]{1,0:T(8,128)(2,1)S(1)} %collective-permute-done.15.m2), channel_id=1, source_target_pairs={{0,16},{1,17},{2,18},{3,19},{4,20},{5,21},{6,22},{7,23},{8,24},{9,... | collective-permute-start | bytes 1572872 | tf_op jit(solution)/shard_map/ppermute | solution.py:253
  59.1 11.0 %collective-permute-start.16 = (bf16[256,512]{1,0:T(8,128)(2,1)S(1)}, bf16[256,512]{1,0:T(8,128)(2,1)S(1)}, u32[]{:S(2)}, u32[]{:S(2)}) collective-permute-start(bf16[256,512]{1,0:T(8,128)(2,1)S(1)} %slice.16), channel_id=1, source_target_pairs={{0,4},{1,5},{2,6},{3,7},{4,8},{5,9},{6,10},{7,11},{8,12},{9,13},{1... | collective-permute-start | bytes 786440 | tf_op jit(solution)/shard_map/ppermute | solution.py:253
  60.3 9.8 %collective-permute-start.17 = (bf16[256,512]{1,0:T(8,128)(2,1)S(1)}, bf16[256,512]{1,0:T(8,128)(2,1)S(1)}, u32[]{:S(2)}, u32[]{:S(2)}) collective-permute-start(bf16[256,512]{1,0:T(8,128)(2,1)S(1)} %slice.17), channel_id=1, source_target_pairs={{0,12},{1,13},{2,14},{3,15},{4,0},{5,1},{6,2},{7,3},{8,4},{9,5},{1... | collective-permute-start | bytes 786440 | tf_op jit(solution)/shard_map/ppermute | solution.py:253
  70.1 9.1 %collective-permute-start.21 = (bf16[256,512]{1,0:T(8,128)(2,1)S(1)}, bf16[256,512]{1,0:T(8,128)(2,1)S(1)}, u32[]{:S(2)}, u32[]{:S(2)}) collective-permute-start(bf16[256,512]{1,0:T(8,128)(2,1)S(1)} %collective-permute-done.16.m3), channel_id=1, source_target_pairs={{0,16},{1,17},{2,18},{3,19},{4,20},{5,21},{6,22},{7,23},{8,24},{9,... | collective-permute-start | bytes 786440 | tf_op jit(solution)/shard_map/ppermute | solution.py:253
  70.9 8.4 %collective-permute-start.22 = (bf16[256,512]{1,0:T(8,128)(2,1)S(1)}, bf16[256,512]{1,0:T(8,128)(2,1)S(1)}, u32[]{:S(2)}, u32[]{:S(2)}) collective-permute-start(bf16[256,512]{1,0:T(8,128)(2,1)S(1)} %collective-permute-done.17.m4), channel_id=1, source_target_pairs={{0,16},{1,17},{2,18},{3,19},{4,20},{5,21},{6,22},{7,23},{8,24},{9,... | collective-permute-start | bytes 786440 | tf_op jit(solution)/shard_map/ppermute | solution.py:253
  (16 other events, 339.0 us)

commit v6 on v5

--- a/solution.py
+++ b/solution.py
@@ -16,7 +16,7 @@
 BF16 = jnp.bfloat16
 D = 512
 BLOCK = 128
-SHARES = (3, 3, 2)
+SHARES = (4, 2, 2)
 
 
 def linear(place):
@@ -120,13 +120,13 @@
 
 
 def face_kernel(
-    pool, fine_h, rows_h, counts, weight_h, edge_out_h, coarse_in_h, coarse_bias,
-    sender_out, centred_out, received_out, f0, f1, f2, f3, f4, f5,
-    fine, rows, weight, edge_out, coarse_in, sems,
+    pool, fine_h, rows_h, counts, weight_h, edge_out_h, coarse_in_h, coarse_bias, nbrs_h,
+    sender_out, centred_out, received_out, near_out, f0, f1, f2, f3, f4, f5,
+    fine, rows, weight, edge_out, coarse_in, nbrs, sems,
 ):
     pairs = (
         (rows_h, rows), (fine_h, fine), (weight_h.at[pl.ds(0, D)], weight), (edge_out_h, edge_out),
-        (coarse_in_h.at[pl.ds(D, D)], coarse_in),
+        (coarse_in_h.at[pl.ds(D, D)], coarse_in), (nbrs_h, nbrs),
     )
     copies = [pltpu.make_async_copy(source, target, sems.at[k]) for k, (source, target) in enumerate(pairs)]
     for copy in copies:
@@ -138,6 +138,9 @@
     received_out[...] = dot(pool[...], coarse_in[...]) + coarse_bias[...]
     wide = edge_out[...].astype(F32)
     centred_out[...] = (wide - jnp.mean(wide, axis=1, keepdims=True)).astype(BF16)
+    padded = jnp.concatenate([nbrs[...], jnp.zeros((2, 1024), jnp.int32)], axis=0)
+    for block in range(8):
+        near_out[block * 128 : (block + 1) * 128, :] = padded[:, block * 128 : (block + 1) * 128].T
     flat = jnp.concatenate(
         [rows[:, 128 * face : 128 * (face + 1)] for face in range(6)] + [jnp.zeros((2, 128), jnp.int32)], axis=0
     )
@@ -149,7 +152,7 @@
         face_out[0] = dot(picked, sender).astype(BF16)
 
 
-def table_kernel(sender, g0, g1, g2, g3, g4, g5, nbrs, table_out, near_out, sems):
+def table_kernel(sender, g0, g1, g2, g3, g4, g5, table_out, sems):
     copies = [pltpu.make_async_copy(sender, table_out.at[pl.ds(0, 1024)], sems.at[0])]
     for k, ghost in enumerate((g0, g1, g2, g3, g4, g5)):
         copies.append(
@@ -157,9 +160,6 @@
         )
     for copy in copies:
         copy.start()
-    padded = jnp.concatenate([nbrs[...], jnp.zeros((2, 1024), jnp.int32)], axis=0)
-    for block in range(8):
-        near_out[block * 128 : (block + 1) * 128, :] = padded[:, block * 128 : (block + 1) * 128].T
     for copy in copies:
         copy.wait()
 
@@ -170,21 +170,17 @@
     picked, hidden,
     *, first,
 ):
-    blocks = new_out.shape[0] // BLOCK
-
-    def step(block, carry):
-        here = pl.ds(pl.multiple_of(block * BLOCK, BLOCK), BLOCK)
+    def block_rows(block, lane):
         span = pl.ds(pl.multiple_of((first + block) * BLOCK, BLOCK), BLOCK)
         own = fine[span, :]
         near = nbrs[span, :]
         received = dot(own, receive[...]) + bias[...]
         for k in range(6):
-            wanted = near[:, k : k + 1]
-            match = wanted == lax.broadcasted_iota(jnp.int32, (BLOCK, 1792), 1)
-            picked[k * BLOCK : (k + 1) * BLOCK, :] = match.astype(F32).astype(BF16)
-        found = dot(picked[...], table[...]).astype(BF16).astype(F32)
-        hidden[...] = jnp.maximum(found + jnp.concatenate([received] * 6, axis=0), 0.0).astype(BF16)
-        out = dot(hidden[...], centred[...])
+            match = near[:, k : k + 1] == lax.broadcasted_iota(jnp.int32, (BLOCK, 1792), 1)
+            picked[lane, k * BLOCK : (k + 1) * BLOCK, :] = match.astype(F32).astype(BF16)
+        found = dot(picked[lane], table[...]).astype(BF16).astype(F32)
+        hidden[lane] = jnp.maximum(found + jnp.concatenate([received] * 6, axis=0), 0.0).astype(BF16)
+        out = dot(hidden[lane], centred[...])
         out = out * lax.rsqrt(jnp.mean(out * out, axis=-1, keepdims=True) + EPS)
         total = jnp.zeros((BLOCK, D), F32)
         for k in range(6):
@@ -192,10 +188,15 @@
         incoming = (total * gain[...]).astype(BF16)
         both = jnp.concatenate([own, incoming], axis=1)
         node = jnp.maximum(dot(both, node_in[...]) + node_bias[...], 0.0).astype(BF16)
+        here = pl.ds(pl.multiple_of(block * BLOCK, BLOCK), BLOCK)
         new_out[here, :] = own.astype(F32) + normed(dot(node, node_out[...])) * node_gain[...]
+
+    def step(pair, carry):
+        block_rows(pair * 2, 0)
+        block_rows(pair * 2 + 1, 1)
         return carry
 
-    lax.fori_loop(0, blocks, step, 0)
+    lax.fori_loop(0, new_out.shape[0] // (2 * BLOCK), step, 0)
 
 
 def columns_of(slots):
@@ -309,13 +310,15 @@
             pltpu.SemaphoreType.DMA((7,)),
         ],
     )
-    fine_sender, centred, received, *faces = kernel(
+    fine_sender, centred, received, near, *faces = kernel(
         face_kernel,
-        [shaped((1024, D), BF16), shaped((D, D), BF16), shaped((16, D), F32)] + [shaped((1, 128, D), BF16)] * 6,
-        [held, far, far, scalars, far, far, far, held],
+        [shaped((1024, D), BF16), shaped((D, D), BF16), shaped((16, D), F32), shaped((1024, 8), jnp.int32)]
+        + [shaped((1, 128, D), BF16)] * 6,
+        [held, far, far, scalars, far, far, far, held, far],
         (
             pool, distant(fine_state), distant(send_rows.reshape(1, 768)), ghost_counts, distant(fine_edge_in),
             distant(fine_edge_out), distant(coarse_edge_in), row(coarse_edge_bias),
+            distant(fine_nbrs.T),
         ),
         [
             pltpu.VMEM((1024, D), BF16),
@@ -323,7 +326,8 @@
             pltpu.VMEM((D, D), BF16),
             pltpu.VMEM((D, D), BF16),
             pltpu.VMEM((D, D), BF16),
-            pltpu.SemaphoreType.DMA((5,)),
+            pltpu.VMEM((6, 1024), jnp.int32),
+            pltpu.SemaphoreType.DMA((6,)),
         ],
     )
 
@@ -344,11 +348,11 @@
     low_y, high_y = faced(3), faced(2)
     low_z, high_z = sent(faces[5], UP_Z), sent(faces[4], DOWN_Z)
     near_faces = [low_x, high_x, low_y, high_y, low_z, high_z]
-    table, near = kernel(
+    (table,) = kernel(
         table_kernel,
-        [shaped((1792, D), BF16), shaped((1024, 8), jnp.int32)],
-        [pl.BlockSpec(memory_space=pl.ANY)] * 7 + [held],
-        (fine_sender, *near_faces, fine_nbrs.T),
+        [shaped((1792, D), BF16)],
+        [pl.BlockSpec(memory_space=pl.ANY)] * 7,
+        (fine_sender, *near_faces),
         [pltpu.SemaphoreType.DMA((7,))],
     )
     news = []
@@ -364,7 +368,7 @@
                     table, fine_state, near, fine_edge_in, row(fine_edge_bias), centred, row(fine_edge_gain),
                     fine_node_in, row(fine_node_bias), fine_node_out, row(fine_node_gain),
                 ),
-                [pltpu.VMEM((6 * BLOCK, 1792), BF16), pltpu.VMEM((6 * BLOCK, D), BF16)],
+                [pltpu.VMEM((2, 6 * BLOCK, 1792), BF16), pltpu.VMEM((2, 6 * BLOCK, D), BF16)],
                 cost=pl.CostEstimate(
                     flops=blocks * 1_700_000_000, bytes_accessed=blocks * 3_000_000, transcendentals=0
                 ),
@@ -375,16 +379,14 @@
     line = joined(column, up, down, *rest)
     table, line = tied((table, line))
     up, down = sent(line, UP_SECOND), sent(line, DOWN_SECOND)
-    others = [sent(line, SWAP)]
     edges(SHARES[0])
     up, down, news[-1] = tied((up, down, news[-1]))
     table, up = tied((table, up))
     rest = [sent(up[:256], UP_SECOND), sent(down[256:], DOWN_SECOND)]
-    others += [sent(up, SWAP), sent(down, SWAP)]
     edges(SHARES[1])
-    *rest, news[-1] = tied((*rest, news[-1]))
+    line, up, down, *rest, news[-1] = tied((line, up, down, *rest, news[-1]))
     table, rest[0] = tied((table, rest[0]))
-    others += [sent(part, SWAP) for part in rest]
+    others = [sent(part, SWAP) for part in (line, up, down, *rest)]
     edges(SHARES[2])
     (found,) = kernel(
         gather_kernel, [shaped((1024, D), BF16)], [held] * 6, (slots, line, up, down, *rest), limit=40,

time: 86.3 us -> 85.2 us (0.987)
  Pallas kernels: 39 us -> 37.5 us
    pallas_call x8, Pallas kernels: 39 us -> 37.5 us  [kernel(): pl.pallas_call(body, grid=(1,), out_shape=outs, in_specs=specs, out_specs...]
  transfers between devices with their start and end apart: 23 -> 23, of which waited for: 2 -> 2; matrix products, arithmetic and copies ran while one was open for 0% -> 0% of each run, Pallas kernels for 35% -> 34%
where the time goes in v6:
time: 85.2 us; the launch traced here: 84.9 us
  starting transfers between devices  42.6 us (50%)
  Pallas kernels  37.5 us (44%)
  waiting for transfers between devices  3.45 us (4%)
  between operations  1.17 us (1%)
    pallas_call x8, Pallas kernels, kernel(): pl.pallas_call(body, grid=(1,), out_shape=outs, in_specs=specs, out_specs...  37.5 us
    ppermute x19, starting transfers between devices, sent(): return lax.ppermute(rows, AXES, pairs)  30 us
    ppermute x4, starting transfers between devices, faced(): lax.ppermute(faces[face], axes, [(b, a) for a, b in pairs] if face % 2 ==...  12.6 us
    ppermute x4, waiting for transfers between devices, faced(): lax.ppermute(faces[face], axes, [(b, a) for a, b in pairs] if face % 2 ==...  2.76 us
  transfers between devices with their start and end apart: 23, of which 2 were waited for; matrix products, arithmetic and copies ran while one was open for 0% of the time, Pallas kernels for 34%

profile of v6, /device:TPU:1, one launch (start us, length us, event | category | flops | bytes accessed | tf_op | source)
XLA Modules:
  0.0 84.9 jit_solution(15082118270101630488)
XLA Ops:
  0.7 2.3 %shard_map.256 = (bf16[16,512]{1,0:T(8,128)(2,1)S(1)}, bf16[16,512]{1,0:T(8,128)(2,1)S(1)}, f32[128,512]{1,0:T(8,128)S(1)}, s32[16,64]{1,0:T(8,128)S(1)}, bf16[3...) custom-call(bf16[1024,512]{1,0:T(8,128)(2,1)} %fine.5, s32[1,1024]{1,0:T(1,128)} %bitcast.29, ...), custom_call_target="tpu_custom_call" | custom-call | tf_op jit(solution)/shard_map/pallas_call | solution.py:273
  3.0 2.5 %collective-permute-start = (bf16[16,512]{1,0:T(8,128)(2,1)S(1)}, bf16[16,512]{1,0:T(8,128)(2,1)S(1)}, u32[]{:S(2)}, u32[]{:S(2)}) collective-permute-start(bf16[16,512]{1,0:T(8,128)(2,1)S(1)} %get-tuple-element.47), channel_id=1, source_target_pairs={{0,1},{1,2},{2,3},{3,32},{4,5},{5,6},{6,7},{7,36},{8,9},{9,10},{10... | collective-permute-start | bytes 49160 | tf_op jit(solution)/shard_map/ppermute | solution.py:254
  5.5 4.0 %collective-permute-start.1 = (bf16[16,512]{1,0:T(8,128)(2,1)S(1)}, bf16[16,512]{1,0:T(8,128)(2,1)S(1)}, u32[]{:S(2)}, u32[]{:S(2)}) collective-permute-start(bf16[16,512]{1,0:T(8,128)(2,1)S(1)} %get-tuple-element.47), channel_id=1, source_target_pairs={{0,35},{1,0},{2,1},{3,2},{4,39},{5,4},{6,5},{7,6},{8,43},{9,8},{10... | collective-permute-start | bytes 49160 | tf_op jit(solution)/shard_map/ppermute | solution.py:254
  9.5 4.0 %shard_map.257 = (bf16[1024,512]{1,0:T(8,128)(2,1)S(1)}, bf16[512,512]{1,0:T(8,128)(2,1)S(1)}, f32[16,512]{1,0:T(8,128)S(1)}, s32[1024,8]{1,0:T(8,128)S(1)}, bf1...) custom-call(bf16[16,512]{1,0:T(8,128)(2,1)S(1)} %get-tuple-element.4, ...), custom_call_target="tpu_custom_call" | custom-call | tf_op jit(solution)/shard_map/pallas_call | solution.py:273
  13.6 1.6 %collective-permute-start.4 = (bf16[48,512]{1,0:T(8,128)(2,1)S(1)}, bf16[48,512]{1,0:T(8,128)(2,1)S(1)}, u32[]{:S(2)}, u32[]{:S(2)}) collective-permute-start(bf16[48,512]{1,0:T(8,128)(2,1)S(1)} %pad_maximum_fusion), channel_id=1, source_target_pairs={{0,3},{1,32},{2,33},{3,34},{4,7},{5,36},{6,37},{7,38},{8,11},{9,40... | collective-permute-start | bytes 147464 | tf_op jit(solution)/shard_map/ppermute | solution.py:254
  15.2 2.9 %collective-permute-start.5 = (bf16[32,512]{1,0:T(8,128)(2,1)S(1)}, bf16[32,512]{1,0:T(8,128)(2,1)S(1)}, u32[]{:S(2)}, u32[]{:S(2)}) collective-permute-start(bf16[32,512]{1,0:T(8,128)(2,1)S(1)} %pad_maximum_fusion.1), channel_id=1, source_target_pairs={{0,33},{1,34},{2,35},{3,0},{4,37},{5,38},{6,39},{7,4},{8,41},{9,42... | collective-permute-start | bytes 98312 | tf_op jit(solution)/shard_map/ppermute | solution.py:254
  18.1 7.5 %collective-permute-start.2 = (bf16[1,128,512]{2,1,0:T(8,128)(2,1)S(1)}, bf16[1,128,512]{2,1,0:T(8,128)(2,1)S(1)}, u32[]{:S(2)}, u32[]{:S(2)}) collective-permute-start(bf16[1,128,512]{2,1,0:T(8,128)(2,1)S(1)} %get-tuple-element.50), channel_id=1, source_target_pairs={{0,16},{16,32},{32,48},{48,64},{64,80},{80,96},{96,112},{112,128},... | collective-permute-start | bytes 393224 | tf_op jit(solution)/shard_map/ppermute | solution.py:338
  25.7 1.4 %collective-permute-start.10 = (bf16[128,512]{1,0:T(8,128)(2,1)S(1)}, bf16[128,512]{1,0:T(8,128)(2,1)S(1)}, u32[]{:S(2)}, u32[]{:S(2)}) collective-permute-start(bf16[128,512]{1,0:T(8,128)(2,1)S(1)} %get-tuple-element.87), channel_id=1, source_target_pairs={{0,64},{1,65},{2,66},{3,67},{4,68},{5,69},{6,70},{7,71},{8,72},{9,... | collective-permute-start | bytes 393224 | tf_op jit(solution)/shard_map/ppermute | solution.py:254
  27.1 1.5 %collective-permute-start.11 = (bf16[128,512]{1,0:T(8,128)(2,1)S(1)}, bf16[128,512]{1,0:T(8,128)(2,1)S(1)}, u32[]{:S(2)}, u32[]{:S(2)}) collective-permute-start(bf16[128,512]{1,0:T(8,128)(2,1)S(1)} %get-tuple-element.87), channel_id=1, source_target_pairs={{0,192},{1,193},{2,194},{3,195},{4,196},{5,197},{6,198},{7,199},{8... | collective-permute-start | bytes 393224 | tf_op jit(solution)/shard_map/ppermute | solution.py:254
  28.6 1.9 %collective-permute-start.3 = (bf16[1,128,512]{2,1,0:T(8,128)(2,1)S(1)}, bf16[1,128,512]{2,1,0:T(8,128)(2,1)S(1)}, u32[]{:S(2)}, u32[]{:S(2)}) collective-permute-start(bf16[1,128,512]{2,1,0:T(8,128)(2,1)S(1)} %get-tuple-element.51), channel_id=1, source_target_pairs={{16,0},{32,16},{48,32},{64,48},{80,64},{96,80},{112,96},{128,112},... | collective-permute-start | bytes 393224 | tf_op jit(solution)/shard_map/ppermute | solution.py:338
  30.5 1.8 %collective-permute-start.6 = (bf16[1,128,512]{2,1,0:T(8,128)(2,1)S(1)}, bf16[1,128,512]{2,1,0:T(8,128)(2,1)S(1)}, u32[]{:S(2)}, u32[]{:S(2)}) collective-permute-start(bf16[1,128,512]{2,1,0:T(8,128)(2,1)S(1)} %get-tuple-element.58), channel_id=1, source_target_pairs={{0,4},{4,8},{8,12},{1,5},{5,9},{9,13},{2,6},{6,10},{10,14},{3,7},{... | collective-permute-start | bytes 393224 | tf_op jit(solution)/shard_map/ppermute | solution.py:338
  32.4 1.3 %collective-permute-start.7 = (bf16[1,128,512]{2,1,0:T(8,128)(2,1)S(1)}, bf16[1,128,512]{2,1,0:T(8,128)(2,1)S(1)}, u32[]{:S(2)}, u32[]{:S(2)}) collective-permute-start(bf16[1,128,512]{2,1,0:T(8,128)(2,1)S(1)} %get-tuple-element.59), channel_id=1, source_target_pairs={{4,0},{8,4},{12,8},{5,1},{9,5},{13,9},{6,2},{10,6},{14,10},{7,3},{... | collective-permute-start | bytes 393224 | tf_op jit(solution)/shard_map/ppermute | solution.py:338
  33.7 2.6 %collective-permute-start.8 = (bf16[1,128,512]{2,1,0:T(8,128)(2,1)S(1)}, bf16[1,128,512]{2,1,0:T(8,128)(2,1)S(1)}, u32[]{:S(2)}, u32[]{:S(2)}) collective-permute-start(bf16[1,128,512]{2,1,0:T(8,128)(2,1)S(1)} %get-tuple-element.60), channel_id=1, source_target_pairs={{0,1},{1,2},{2,3},{3,32},{4,5},{5,6},{6,7},{7,36},{8,9},{9,10},{10... | collective-permute-start | bytes 393224 | tf_op jit(solution)/shard_map/ppermute | solution.py:254
  36.5 2.8 %collective-permute-done.3.g1 = bf16[1,128,512]{2,1,0:T(8,128)(2,1)S(1)} collective-permute-done((bf16[1,128,512]{2,1,0:T(8,128)(2,1)S(1)}, bf16[1,128,512]{2,1,0:T(8,128)(2,1)S(1)}, u32[]{:S(2)}, u32[]{:S(2)}) %collective-permute-start.3) | collective-permute-done | bytes 131104 | tf_op jit(solution)/shard_map/ppermute | solution.py:338
  39.3 2.7 %collective-permute-start.13 = (bf16[64,512]{1,0:T(8,128)(2,1)S(1)}, bf16[64,512]{1,0:T(8,128)(2,1)S(1)}, u32[]{:S(2)}, u32[]{:S(2)}) collective-permute-start(bf16[64,512]{1,0:T(8,128)(2,1)S(1)} %slice.19), channel_id=1, source_target_pairs={{0,192},{1,193},{2,194},{3,195},{4,196},{5,197},{6,198},{7,199},{8... | collective-permute-start | bytes 196616 | tf_op jit(solution)/shard_map/ppermute | solution.py:254
  43.9 2.9 %collective-permute-start.14 = (bf16[512,512]{1,0:T(8,128)(2,1)S(1)}, bf16[512,512]{1,0:T(8,128)(2,1)S(1)}, u32[]{:S(2)}, u32[]{:S(2)}) collective-permute-start(bf16[512,512]{1,0:T(8,128)(2,1)S(1)} %constant_dynamic-update-slice_fusion.5.m0), channel_id=1, source_target_pairs={{0,4},{1,5},{2,6},{3,7},{4,8},{5,9},{6,10},{7,11},{8,12},{9,13},{1... | collective-permute-start | bytes 1572872 | tf_op jit(solution)/shard_map/ppermute | solution.py:254
  46.8 1.5 %collective-permute-start.15 = (bf16[512,512]{1,0:T(8,128)(2,1)S(1)}, bf16[512,512]{1,0:T(8,128)(2,1)S(1)}, u32[]{:S(2)}, u32[]{:S(2)}) collective-permute-start(bf16[512,512]{1,0:T(8,128)(2,1)S(1)} %constant_dynamic-update-slice_fusion.5.m0), channel_id=1, source_target_pairs={{0,12},{1,13},{2,14},{3,15},{4,0},{5,1},{6,2},{7,3},{8,4},{9,5},{1... | collective-permute-start | bytes 1572872 | tf_op jit(solution)/shard_map/ppermute | solution.py:254
  48.4 10.5 %shard_map.259.rest_0_ = f32[512,512]{1,0:T(8,128)S(1)} custom-call(bf16[1792,512]{1,0:T(8,128)(2,1)S(1)} %shard_map.258.table, bf16[1024,512]{1,0:T(8,128)(2,1)S(1)} %copy-done, s32[1024,8]{1,0:T(8,128)S(1)} %get-tuple-element.66.nbrs, bf16[1024,512]{1,0:T(8,128)(2,1)S(1)} %copy-done.1, f32[1,512]{1,0:T(1,128)S(1)} %bitcast.16, ...), custom_call_target="tpu_custom_call" | custom-call | flops 6800000000 | bytes 12000000 | tf_op jit(solution)/shard_map/pallas_call | solution.py:273
  59.1 2.7 %collective-permute-start.17 = (bf16[256,512]{1,0:T(8,128)(2,1)S(1)}, bf16[256,512]{1,0:T(8,128)(2,1)S(1)}, u32[]{:S(2)}, u32[]{:S(2)}) collective-permute-start(bf16[256,512]{1,0:T(8,128)(2,1)S(1)} %slice.17), channel_id=1, source_target_pairs={{0,12},{1,13},{2,14},{3,15},{4,0},{5,1},{6,2},{7,3},{8,4},{9,5},{1... | collective-permute-start | bytes 786440 | tf_op jit(solution)/shard_map/ppermute | solution.py:254
  61.8 5.2 %shard_map.260.rest_1_ = f32[256,512]{1,0:T(8,128)S(1)} custom-call(bf16[1792,512]{1,0:T(8,128)(2,1)S(1)} %shard_map.258.table, bf16[1024,512]{1,0:T(8,128)(2,1)S(1)} %copy-done, s32[1024,8]{1,0:T(8,128)S(1)} %get-tuple-element.66.nbrs, bf16[1024,512]{1,0:T(8,128)(2,1)S(1)} %copy-done.1, f32[1,512]{1,0:T(1,128)S(1)} %bitcast.17, ...), custom_call_target="tpu_custom_call" | custom-call | flops 3400000000 | bytes 6000000 | tf_op jit(solution)/shard_map/pallas_call | solution.py:273
  67.1 2.3 %collective-permute-start.18 = (bf16[512,512]{1,0:T(8,128)(2,1)S(1)}, bf16[512,512]{1,0:T(8,128)(2,1)S(1)}, u32[]{:S(2)}, u32[]{:S(2)}) collective-permute-start(bf16[512,512]{1,0:T(8,128)(2,1)S(1)} %constant_dynamic-update-slice_fusion.5.m0), channel_id=1, source_target_pairs={{0,16},{1,17},{2,18},{3,19},{4,20},{5,21},{6,22},{7,23},{8,24},{9,... | collective-permute-start | bytes 1572872 | tf_op jit(solution)/shard_map/ppermute | solution.py:254
  70.4 2.4 %shard_map.261.found = bf16[1024,512]{1,0:T(8,128)(2,1)S(1)} custom-call(s32[16,64]{1,0:T(8,128)S(1)} %get-tuple-element.44.slots, bf16[512,512]{1,0:T(8,128)(2,1)S(1)} %constant_dynamic-update-slice_fusion.5.m0, bf16[512,512]{1,0:T(8,128)(2,1)S(1)} %collective-permute-done.14.m1, bf16[512,512]{1,0:T(8,128)(2,1)S(1)} %collective-permute-done.15.m2, ...), custom_call_target="tpu_custom_call" | custom-call | flops 2000000000 | bytes 4000000 | tf_op jit(solution)/shard_map/pallas_call | solution.py:273
  72.8 5.3 %shard_map.262.rest_2_ = f32[256,512]{1,0:T(8,128)S(1)} custom-call(bf16[1792,512]{1,0:T(8,128)(2,1)S(1)} %shard_map.258.table, bf16[1024,512]{1,0:T(8,128)(2,1)S(1)} %copy-done, s32[1024,8]{1,0:T(8,128)S(1)} %get-tuple-element.66.nbrs, bf16[1024,512]{1,0:T(8,128)(2,1)S(1)} %copy-done.1, f32[1,512]{1,0:T(1,128)S(1)} %bitcast.18, ...), custom_call_target="tpu_custom_call" | custom-call | flops 3400000000 | bytes 6000000 | tf_op jit(solution)/shard_map/pallas_call | solution.py:273
  78.2 6.7 %shard_map.263 = (bf16[1024,512]{1,0:T(8,128)(2,1)}, bf16[128,512]{1,0:T(8,128)(2,1)}, bf16[16,512]{1,0:T(8,128)(2,1)}) custom-call(bf16[1024,512]{1,0:T(8,128)(2,1)S(1)} %shard_map.261.found, bf16[512,512]{1,0:T(8,128)(2,1)S(1)} %collective-permute-done.18.o0, bf16[512,512]{1,0:T(8,128)(2,1)S(1)} %collective-permute-done.19.o1, ...), custom_call_target="tpu_custom_call" | custom-call | tf_op jit(solution)/shard_map/pallas_call | solution.py:273
  (77 shorter events, 3.4 us)
Async XLA Ops:
  0.6 8.9 %copy-start.5 = (f32[512]{0:T(512)S(1)}, f32[512]{0:T(512)}, u32[]{:S(2)}) copy-start(f32[512]{0:T(512)} %param.43) | copy-start | bytes 6148
  3.0 10.6 %collective-permute-start = (bf16[16,512]{1,0:T(8,128)(2,1)S(1)}, bf16[16,512]{1,0:T(8,128)(2,1)S(1)}, u32[]{:S(2)}, u32[]{:S(2)}) collective-permute-start(bf16[16,512]{1,0:T(8,128)(2,1)S(1)} %get-tuple-element.47), channel_id=1, source_target_pairs={{0,1},{1,2},{2,3},{3,32},{4,5},{5,6},{6,7},{7,36},{8,9},{9,10},{10... | collective-permute-start | bytes 49160 | tf_op jit(solution)/shard_map/ppermute | solution.py:254
  5.5 8.0 %collective-permute-start.1 = (bf16[16,512]{1,0:T(8,128)(2,1)S(1)}, bf16[16,512]{1,0:T(8,128)(2,1)S(1)}, u32[]{:S(2)}, u32[]{:S(2)}) collective-permute-start(bf16[16,512]{1,0:T(8,128)(2,1)S(1)} %get-tuple-element.47), channel_id=1, source_target_pairs={{0,35},{1,0},{2,1},{3,2},{4,39},{5,4},{6,5},{7,6},{8,43},{9,8},{10... | collective-permute-start | bytes 49160 | tf_op jit(solution)/shard_map/ppermute | solution.py:254
  13.6 12.1 %collective-permute-start.4 = (bf16[48,512]{1,0:T(8,128)(2,1)S(1)}, bf16[48,512]{1,0:T(8,128)(2,1)S(1)}, u32[]{:S(2)}, u32[]{:S(2)}) collective-permute-start(bf16[48,512]{1,0:T(8,128)(2,1)S(1)} %pad_maximum_fusion), channel_id=1, source_target_pairs={{0,3},{1,32},{2,33},{3,34},{4,7},{5,36},{6,37},{7,38},{8,11},{9,40... | collective-permute-start | bytes 147464 | tf_op jit(solution)/shard_map/ppermute | solution.py:254
  15.2 10.5 %collective-permute-start.5 = (bf16[32,512]{1,0:T(8,128)(2,1)S(1)}, bf16[32,512]{1,0:T(8,128)(2,1)S(1)}, u32[]{:S(2)}, u32[]{:S(2)}) collective-permute-start(bf16[32,512]{1,0:T(8,128)(2,1)S(1)} %pad_maximum_fusion.1), channel_id=1, source_target_pairs={{0,33},{1,34},{2,35},{3,0},{4,37},{5,38},{6,39},{7,4},{8,41},{9,42... | collective-permute-start | bytes 98312 | tf_op jit(solution)/shard_map/ppermute | solution.py:254
  18.1 14.3 %collective-permute-start.2 = (bf16[1,128,512]{2,1,0:T(8,128)(2,1)S(1)}, bf16[1,128,512]{2,1,0:T(8,128)(2,1)S(1)}, u32[]{:S(2)}, u32[]{:S(2)}) collective-permute-start(bf16[1,128,512]{2,1,0:T(8,128)(2,1)S(1)} %get-tuple-element.50), channel_id=1, source_target_pairs={{0,16},{16,32},{32,48},{48,64},{64,80},{80,96},{96,112},{112,128},... | collective-permute-start | bytes 393224 | tf_op jit(solution)/shard_map/ppermute | solution.py:338
  25.7 8.0 %collective-permute-start.10 = (bf16[128,512]{1,0:T(8,128)(2,1)S(1)}, bf16[128,512]{1,0:T(8,128)(2,1)S(1)}, u32[]{:S(2)}, u32[]{:S(2)}) collective-permute-start(bf16[128,512]{1,0:T(8,128)(2,1)S(1)} %get-tuple-element.87), channel_id=1, source_target_pairs={{0,64},{1,65},{2,66},{3,67},{4,68},{5,69},{6,70},{7,71},{8,72},{9,... | collective-permute-start | bytes 393224 | tf_op jit(solution)/shard_map/ppermute | solution.py:254
  27.1 9.2 %collective-permute-start.11 = (bf16[128,512]{1,0:T(8,128)(2,1)S(1)}, bf16[128,512]{1,0:T(8,128)(2,1)S(1)}, u32[]{:S(2)}, u32[]{:S(2)}) collective-permute-start(bf16[128,512]{1,0:T(8,128)(2,1)S(1)} %get-tuple-element.87), channel_id=1, source_target_pairs={{0,192},{1,193},{2,194},{3,195},{4,196},{5,197},{6,198},{7,199},{8... | collective-permute-start | bytes 393224 | tf_op jit(solution)/shard_map/ppermute | solution.py:254
  28.6 10.6 %collective-permute-start.3 = (bf16[1,128,512]{2,1,0:T(8,128)(2,1)S(1)}, bf16[1,128,512]{2,1,0:T(8,128)(2,1)S(1)}, u32[]{:S(2)}, u32[]{:S(2)}) collective-permute-start(bf16[1,128,512]{2,1,0:T(8,128)(2,1)S(1)} %get-tuple-element.51), channel_id=1, source_target_pairs={{16,0},{32,16},{48,32},{64,48},{80,64},{96,80},{112,96},{128,112},... | collective-permute-start | bytes 393224 | tf_op jit(solution)/shard_map/ppermute | solution.py:338
  30.5 8.7 %collective-permute-start.6 = (bf16[1,128,512]{2,1,0:T(8,128)(2,1)S(1)}, bf16[1,128,512]{2,1,0:T(8,128)(2,1)S(1)}, u32[]{:S(2)}, u32[]{:S(2)}) collective-permute-start(bf16[1,128,512]{2,1,0:T(8,128)(2,1)S(1)} %get-tuple-element.58), channel_id=1, source_target_pairs={{0,4},{4,8},{8,12},{1,5},{5,9},{9,13},{2,6},{6,10},{10,14},{3,7},{... | collective-permute-start | bytes 393224 | tf_op jit(solution)/shard_map/ppermute | solution.py:338
  32.4 9.5 %collective-permute-start.7 = (bf16[1,128,512]{2,1,0:T(8,128)(2,1)S(1)}, bf16[1,128,512]{2,1,0:T(8,128)(2,1)S(1)}, u32[]{:S(2)}, u32[]{:S(2)}) collective-permute-start(bf16[1,128,512]{2,1,0:T(8,128)(2,1)S(1)} %get-tuple-element.59), channel_id=1, source_target_pairs={{4,0},{8,4},{12,8},{5,1},{9,5},{13,9},{6,2},{10,6},{14,10},{7,3},{... | collective-permute-start | bytes 393224 | tf_op jit(solution)/shard_map/ppermute | solution.py:338
  33.7 8.2 %collective-permute-start.8 = (bf16[1,128,512]{2,1,0:T(8,128)(2,1)S(1)}, bf16[1,128,512]{2,1,0:T(8,128)(2,1)S(1)}, u32[]{:S(2)}, u32[]{:S(2)}) collective-permute-start(bf16[1,128,512]{2,1,0:T(8,128)(2,1)S(1)} %get-tuple-element.60), channel_id=1, source_target_pairs={{0,1},{1,2},{2,3},{3,32},{4,5},{5,6},{6,7},{7,36},{8,9},{9,10},{10... | collective-permute-start | bytes 393224 | tf_op jit(solution)/shard_map/ppermute | solution.py:254
  36.3 5.7 %collective-permute-start.9 = (bf16[1,128,512]{2,1,0:T(8,128)(2,1)S(1)}, bf16[1,128,512]{2,1,0:T(8,128)(2,1)S(1)}, u32[]{:S(2)}, u32[]{:S(2)}) collective-permute-start(bf16[1,128,512]{2,1,0:T(8,128)(2,1)S(1)} %get-tuple-element.61), channel_id=1, source_target_pairs={{0,35},{1,0},{2,1},{3,2},{4,39},{5,4},{6,5},{7,6},{8,43},{9,8},{10... | collective-permute-start | bytes 393224 | tf_op jit(solution)/shard_map/ppermute | solution.py:254
  39.3 4.6 %collective-permute-start.12 = (bf16[64,512]{1,0:T(8,128)(2,1)S(1)}, bf16[64,512]{1,0:T(8,128)(2,1)S(1)}, u32[]{:S(2)}, u32[]{:S(2)}) collective-permute-start(bf16[64,512]{1,0:T(8,128)(2,1)S(1)} %slice.18), channel_id=1, source_target_pairs={{0,64},{1,65},{2,66},{3,67},{4,68},{5,69},{6,70},{7,71},{8,72},{9,... | collective-permute-start | bytes 196616 | tf_op jit(solution)/shard_map/ppermute | solution.py:254
  39.3 4.6 %collective-permute-start.13 = (bf16[64,512]{1,0:T(8,128)(2,1)S(1)}, bf16[64,512]{1,0:T(8,128)(2,1)S(1)}, u32[]{:S(2)}, u32[]{:S(2)}) collective-permute-start(bf16[64,512]{1,0:T(8,128)(2,1)S(1)} %slice.19), channel_id=1, source_target_pairs={{0,192},{1,193},{2,194},{3,195},{4,196},{5,197},{6,198},{7,199},{8... | collective-permute-start | bytes 196616 | tf_op jit(solution)/shard_map/ppermute | solution.py:254
  43.9 15.0 %collective-permute-start.14 = (bf16[512,512]{1,0:T(8,128)(2,1)S(1)}, bf16[512,512]{1,0:T(8,128)(2,1)S(1)}, u32[]{:S(2)}, u32[]{:S(2)}) collective-permute-start(bf16[512,512]{1,0:T(8,128)(2,1)S(1)} %constant_dynamic-update-slice_fusion.5.m0), channel_id=1, source_target_pairs={{0,4},{1,5},{2,6},{3,7},{4,8},{5,9},{6,10},{7,11},{8,12},{9,13},{1... | collective-permute-start | bytes 1572872 | tf_op jit(solution)/shard_map/ppermute | solution.py:254
  46.8 12.1 %collective-permute-start.15 = (bf16[512,512]{1,0:T(8,128)(2,1)S(1)}, bf16[512,512]{1,0:T(8,128)(2,1)S(1)}, u32[]{:S(2)}, u32[]{:S(2)}) collective-permute-start(bf16[512,512]{1,0:T(8,128)(2,1)S(1)} %constant_dynamic-update-slice_fusion.5.m0), channel_id=1, source_target_pairs={{0,12},{1,13},{2,14},{3,15},{4,0},{5,1},{6,2},{7,3},{8,4},{9,5},{1... | collective-permute-start | bytes 1572872 | tf_op jit(solution)/shard_map/ppermute | solution.py:254
  59.0 8.1 %collective-permute-start.16 = (bf16[256,512]{1,0:T(8,128)(2,1)S(1)}, bf16[256,512]{1,0:T(8,128)(2,1)S(1)}, u32[]{:S(2)}, u32[]{:S(2)}) collective-permute-start(bf16[256,512]{1,0:T(8,128)(2,1)S(1)} %slice.16), channel_id=1, source_target_pairs={{0,4},{1,5},{2,6},{3,7},{4,8},{5,9},{6,10},{7,11},{8,12},{9,13},{1... | collective-permute-start | bytes 786440 | tf_op jit(solution)/shard_map/ppermute | solution.py:254
  59.1 8.0 %collective-permute-start.17 = (bf16[256,512]{1,0:T(8,128)(2,1)S(1)}, bf16[256,512]{1,0:T(8,128)(2,1)S(1)}, u32[]{:S(2)}, u32[]{:S(2)}) collective-permute-start(bf16[256,512]{1,0:T(8,128)(2,1)S(1)} %slice.17), channel_id=1, source_target_pairs={{0,12},{1,13},{2,14},{3,15},{4,0},{5,1},{6,2},{7,3},{8,4},{9,5},{1... | collective-permute-start | bytes 786440 | tf_op jit(solution)/shard_map/ppermute | solution.py:254
  67.1 11.0 %collective-permute-start.18 = (bf16[512,512]{1,0:T(8,128)(2,1)S(1)}, bf16[512,512]{1,0:T(8,128)(2,1)S(1)}, u32[]{:S(2)}, u32[]{:S(2)}) collective-permute-start(bf16[512,512]{1,0:T(8,128)(2,1)S(1)} %constant_dynamic-update-slice_fusion.5.m0), channel_id=1, source_target_pairs={{0,16},{1,17},{2,18},{3,19},{4,20},{5,21},{6,22},{7,23},{8,24},{9,... | collective-permute-start | bytes 1572872 | tf_op jit(solution)/shard_map/ppermute | solution.py:254
  69.4 8.8 %collective-permute-start.19 = (bf16[512,512]{1,0:T(8,128)(2,1)S(1)}, bf16[512,512]{1,0:T(8,128)(2,1)S(1)}, u32[]{:S(2)}, u32[]{:S(2)}) collective-permute-start(bf16[512,512]{1,0:T(8,128)(2,1)S(1)} %collective-permute-done.14.m1), channel_id=1, source_target_pairs={{0,16},{1,17},{2,18},{3,19},{4,20},{5,21},{6,22},{7,23},{8,24},{9,... | collective-permute-start | bytes 1572872 | tf_op jit(solution)/shard_map/ppermute | solution.py:254
  69.5 8.7 %collective-permute-start.20 = (bf16[512,512]{1,0:T(8,128)(2,1)S(1)}, bf16[512,512]{1,0:T(8,128)(2,1)S(1)}, u32[]{:S(2)}, u32[]{:S(2)}) collective-permute-start(bf16[512,512]{1,0:T(8,128)(2,1)S(1)} %collective-permute-done.15.m2), channel_id=1, source_target_pairs={{0,16},{1,17},{2,18},{3,19},{4,20},{5,21},{6,22},{7,23},{8,24},{9,... | collective-permute-start | bytes 1572872 | tf_op jit(solution)/shard_map/ppermute | solution.py:254
  69.9 8.2 %collective-permute-start.21 = (bf16[256,512]{1,0:T(8,128)(2,1)S(1)}, bf16[256,512]{1,0:T(8,128)(2,1)S(1)}, u32[]{:S(2)}, u32[]{:S(2)}) collective-permute-start(bf16[256,512]{1,0:T(8,128)(2,1)S(1)} %collective-permute-done.16.m3), channel_id=1, source_target_pairs={{0,16},{1,17},{2,18},{3,19},{4,20},{5,21},{6,22},{7,23},{8,24},{9,... | collective-permute-start | bytes 786440 | tf_op jit(solution)/shard_map/ppermute | solution.py:254
  70.0 8.1 %collective-permute-start.22 = (bf16[256,512]{1,0:T(8,128)(2,1)S(1)}, bf16[256,512]{1,0:T(8,128)(2,1)S(1)}, u32[]{:S(2)}, u32[]{:S(2)}) collective-permute-start(bf16[256,512]{1,0:T(8,128)(2,1)S(1)} %collective-permute-done.17.m4), channel_id=1, source_target_pairs={{0,16},{1,17},{2,18},{3,19},{4,20},{5,21},{6,22},{7,23},{8,24},{9,... | collective-permute-start | bytes 786440 | tf_op jit(solution)/shard_map/ppermute | solution.py:254
  (15 other events, 95.1 us)

commit v7 on v6

--- a/solution.py
+++ b/solution.py
@@ -71,19 +71,24 @@
     return center * lax.rsqrt(spread + EPS)
 
 
-def pool_kernel(
+def first_kernel(
     fine_h, parent_h, medium_h, medium_parent_h, coarse_h, nbrs_h, weight_h,
+    rows_h, counts_h, fine_in_h, edge_out_h, coarse_bias_h, fine_near_h,
     sender_out, pool_out, medium_out, slots_out, comp_out, member_out,
-    fine, parent, medium, medium_parent, coarse, nbrs, weight, sems,
+    fine_sender_out, centred_out, received_out, near_out, f0, f1, f2, f3, f4, f5,
+    fine, parent, medium, medium_parent, coarse, nbrs, weight, rows, fine_in, edge_out, coarse_in, fine_near,
+    counts, coarse_bias, sems,
 ):
     pairs = (
         (parent_h, parent), (fine_h, fine), (medium_h, medium), (medium_parent_h, medium_parent),
-        (coarse_h, coarse), (weight_h.at[pl.ds(0, D)], weight), (nbrs_h, nbrs),
+        (coarse_h, coarse), (weight_h.at[pl.ds(0, D)], weight), (nbrs_h, nbrs), (rows_h, rows),
+        (fine_in_h.at[pl.ds(0, D)], fine_in), (edge_out_h, edge_out), (weight_h.at[pl.ds(D, D)], coarse_in),
+        (fine_near_h, fine_near), (counts_h, counts), (coarse_bias_h, coarse_bias),
     )
     copies = [pltpu.make_async_copy(source, target, sems.at[k]) for k, (source, target) in enumerate(pairs)]
     for copy in copies:
         copy.start()
-    for copy in copies:
+    for copy in copies[:7]:
         copy.wait()
     member = (parent[...] == lax.broadcasted_iota(jnp.int32, (128, 1024), 0)).astype(F32)
     count = jnp.sum(member, axis=1, keepdims=True)
@@ -117,28 +122,14 @@
     order_y = jnp.where(step_y == 2, 3, jnp.where(step_y == 3, 2, step_y))
     at = at + jnp.where(stream == 0, order_x * 128 + order_y * 512, order_y * 128 + order_x * 512)
     slots_out[...] = at + jnp.where(stream == here["c"], 0, 2048)
-
-
-def face_kernel(
-    pool, fine_h, rows_h, counts, weight_h, edge_out_h, coarse_in_h, coarse_bias, nbrs_h,
-    sender_out, centred_out, received_out, near_out, f0, f1, f2, f3, f4, f5,
-    fine, rows, weight, edge_out, coarse_in, nbrs, sems,
-):
-    pairs = (
-        (rows_h, rows), (fine_h, fine), (weight_h.at[pl.ds(0, D)], weight), (edge_out_h, edge_out),
-        (coarse_in_h.at[pl.ds(D, D)], coarse_in), (nbrs_h, nbrs),
-    )
-    copies = [pltpu.make_async_copy(source, target, sems.at[k]) for k, (source, target) in enumerate(pairs)]
-    for copy in copies:
-        copy.start()
-    for copy in copies:
+    for copy in copies[7:]:
         copy.wait()
-    sender = dot(fine[...], weight[...]).astype(BF16)
-    sender_out[...] = sender
-    received_out[...] = dot(pool[...], coarse_in[...]) + coarse_bias[...]
+    fine_sender = dot(fine[...], fine_in[...]).astype(BF16)
+    fine_sender_out[...] = fine_sender
+    received_out[...] = dot(pool, coarse_in[...]) + coarse_bias[...]
     wide = edge_out[...].astype(F32)
     centred_out[...] = (wide - jnp.mean(wide, axis=1, keepdims=True)).astype(BF16)
-    padded = jnp.concatenate([nbrs[...], jnp.zeros((2, 1024), jnp.int32)], axis=0)
+    padded = jnp.concatenate([fine_near[...], jnp.zeros((2, 1024), jnp.int32)], axis=0)
     for block in range(8):
         near_out[block * 128 : (block + 1) * 128, :] = padded[:, block * 128 : (block + 1) * 128].T
     flat = jnp.concatenate(
@@ -149,7 +140,7 @@
     for face, face_out in enumerate((f0, f1, f2, f3, f4, f5)):
         wanted = jnp.where(place < counts[0, face], columns[:, face : face + 1], -1)
         picked = (wanted == lax.broadcasted_iota(jnp.int32, (128, 1024), 1)).astype(F32).astype(BF16)
-        face_out[0] = dot(picked, sender).astype(BF16)
+        face_out[0] = dot(picked, fine_sender).astype(BF16)
 
 
 def table_kernel(sender, g0, g1, g2, g3, g4, g5, table_out, sems):
@@ -264,7 +255,6 @@
     shaped = jax.ShapeDtypeStruct
     held = pl.BlockSpec(memory_space=pltpu.VMEM)
     far = pl.BlockSpec(memory_space=pltpu.HBM)
-    scalars = pl.BlockSpec(memory_space=pltpu.SMEM)
     upper = pl.BlockSpec((D, D), lambda i: (1, 0), memory_space=pltpu.VMEM)
     tied = lax.optimization_barrier
     distant = functools.partial(pltpu.with_memory_space_constraint, memory_space=pltpu.HBM)
@@ -281,8 +271,8 @@
             cost_estimate=cost,
         )(*args)
 
-    sender, pool, medium_pool, slots, comp, member = kernel(
-        pool_kernel,
+    sender, pool, medium_pool, slots, comp, member, fine_sender, centred, received, near, *faces = kernel(
+        first_kernel,
         [
             shaped((16, D), BF16),
             shaped((16, D), BF16),
@@ -290,15 +280,19 @@
             shaped((16, 64), jnp.int32),
             shaped((32, 1024), BF16),
             shaped((32, 128), BF16),
-        ],
-        [far] * 7,
-        [
-            distant(value)
-            for value in (
-                fine_state, row(fine_parent), medium_state, row(medium_parent), coarse_state, coarse_nbrs,
-                coarse_edge_in,
-            )
-        ],
+            shaped((1024, D), BF16),
+            shaped((D, D), BF16),
+            shaped((16, D), F32),
+            shaped((1024, 8), jnp.int32),
+        ]
+        + [shaped((1, 128, D), BF16)] * 6,
+        [far] * 13,
+        (
+            distant(fine_state), distant(row(fine_parent)), distant(medium_state), distant(row(medium_parent)),
+            distant(coarse_state), distant(coarse_nbrs), distant(coarse_edge_in), distant(send_rows.reshape(1, 768)),
+            distant(ghost_counts), distant(fine_edge_in), distant(fine_edge_out), distant(row(coarse_edge_bias)),
+            distant(fine_nbrs.T),
+        ),
         [
             pltpu.VMEM((1024, D), BF16),
             pltpu.VMEM((1, 1024), jnp.int32),
@@ -307,27 +301,14 @@
             pltpu.VMEM((16, D), BF16),
             pltpu.VMEM((16, 64), jnp.int32),
             pltpu.VMEM((D, D), BF16),
-            pltpu.SemaphoreType.DMA((7,)),
-        ],
-    )
-    fine_sender, centred, received, near, *faces = kernel(
-        face_kernel,
-        [shaped((1024, D), BF16), shaped((D, D), BF16), shaped((16, D), F32), shaped((1024, 8), jnp.int32)]
-        + [shaped((1, 128, D), BF16)] * 6,
-        [held, far, far, scalars, far, far, far, held, far],
-        (
-            pool, distant(fine_state), distant(send_rows.reshape(1, 768)), ghost_counts, distant(fine_edge_in),
-            distant(fine_edge_out), distant(coarse_edge_in), row(coarse_edge_bias),
-            distant(fine_nbrs.T),
-        ),
-        [
-            pltpu.VMEM((1024, D), BF16),
             pltpu.VMEM((1, 768), jnp.int32),
             pltpu.VMEM((D, D), BF16),
             pltpu.VMEM((D, D), BF16),
             pltpu.VMEM((D, D), BF16),
             pltpu.VMEM((6, 1024), jnp.int32),
-            pltpu.SemaphoreType.DMA((6,)),
+            pltpu.SMEM((1, 6), jnp.int32),
+            pltpu.VMEM((1, D), F32),
+            pltpu.SemaphoreType.DMA((14,)),
         ],
     )
 
@@ -338,10 +319,11 @@
         return lax.ppermute(faces[face], axes, [(b, a) for a, b in pairs] if face % 2 == 0 else pairs)
 
     low, high = sent(sender, UP_Z), sent(sender, DOWN_Z)
-    low, high, faces[0], faces[1] = tied((low, high, faces[0], faces[1]))
+    low_x = faced(1)
+    low, high, faces[0] = tied((low, high, faces[0]))
     three = joined(high, sender, low)
     lower, higher = sent(three, UP_3Z), sent(three[16:], DOWN_3Z)
-    low_x, high_x = faced(1), faced(0)
+    high_x = faced(0)
     lower, higher, *faces[2:] = tied((lower, higher, *faces[2:]))
     column = joined(three, lower, higher)
     up, down = sent(column, UP_FIRST), sent(column, DOWN_FIRST)

time: 85.2 us -> 87.8 us (1.031)
  starting transfers between devices: 42.6 us -> 47.8 us
  Pallas kernels: 37.5 us -> 35.2 us
    ppermute x19, starting transfers between devices: 30 us -> 33.7 us  [sent(): return lax.ppermute(rows, AXES, pairs)]
    pallas_call x8 -> x7, Pallas kernels: 37.5 us -> 35.2 us  [kernel(): pl.pallas_call(body, grid=(1,), out_shape=outs, in_specs=specs, out_specs...]
    ppermute x4, waiting for transfers between devices: 2.76 us -> 0.69 us  [faced(): lax.ppermute(faces[face], axes, [(b, a) for a, b in pairs] if face % 2 ==...]
    ppermute x19, waiting for transfers between devices: 0.69 us -> 2.54 us  [sent(): return lax.ppermute(rows, AXES, pairs)]
    ppermute x4, starting transfers between devices: 12.6 us -> 14.1 us  [faced(): lax.ppermute(faces[face], axes, [(b, a) for a, b in pairs] if face % 2 ==...]
  transfers between devices with their start and end apart: 23 -> 23, of which waited for: 2 -> 4; matrix products, arithmetic and copies ran while one was open for 0% -> 0% of each run, Pallas kernels for 34% -> 28%
where the time goes in v7:
time: 87.8 us; the launch traced here: 87.6 us
  starting transfers between devices  47.8 us (54%)
  Pallas kernels  35.2 us (40%)
  waiting for transfers between devices  3.23 us (4%)
  between operations  1.12 us (1%)
    pallas_call x7, Pallas kernels, kernel(): pl.pallas_call(body, grid=(1,), out_shape=outs, in_specs=specs, out_specs...  35.2 us
    ppermute x19, starting transfers between devices, sent(): return lax.ppermute(rows, AXES, pairs)  33.7 us
    ppermute x4, starting transfers between devices, faced(): lax.ppermute(faces[face], axes, [(b, a) for a, b in pairs] if face % 2 ==...  14.1 us
    ppermute x19, waiting for transfers between devices, sent(): return lax.ppermute(rows, AXES, pairs)  2.54 us
  transfers between devices with their start and end apart: 23, of which 4 were waited for; matrix products, arithmetic and copies ran while one was open for 0% of the time, Pallas kernels for 28%

profile of v7, /device:TPU:1, one launch (start us, length us, event | category | flops | bytes accessed | tf_op | source)
XLA Modules:
  0.0 87.6 jit_solution(15288322141597972070)
XLA Ops:
  0.6 4.1 %shard_map.256 = (bf16[16,512]{1,0:T(8,128)(2,1)S(1)}, bf16[16,512]{1,0:T(8,128)(2,1)S(1)}, f32[128,512]{1,0:T(8,128)S(1)}, s32[16,64]{1,0:T(8,128)S(1)}, bf16[3...) custom-call(bf16[1024,512]{1,0:T(8,128)(2,1)} %fine.5, ...), custom_call_target="tpu_custom_call" | custom-call | tf_op jit(solution)/shard_map/pallas_call | solution.py:263
  4.7 2.5 %collective-permute-start.1 = (bf16[16,512]{1,0:T(8,128)(2,1)S(1)}, bf16[16,512]{1,0:T(8,128)(2,1)S(1)}, u32[]{:S(2)}, u32[]{:S(2)}) collective-permute-start(bf16[16,512]{1,0:T(8,128)(2,1)S(1)} %get-tuple-element.46), channel_id=1, source_target_pairs={{0,1},{1,2},{2,3},{3,32},{4,5},{5,6},{6,7},{7,36},{8,9},{9,10},{10... | collective-permute-start | bytes 49160 | tf_op jit(solution)/shard_map/ppermute | solution.py:245
  7.3 4.0 %collective-permute-start.2 = (bf16[16,512]{1,0:T(8,128)(2,1)S(1)}, bf16[16,512]{1,0:T(8,128)(2,1)S(1)}, u32[]{:S(2)}, u32[]{:S(2)}) collective-permute-start(bf16[16,512]{1,0:T(8,128)(2,1)S(1)} %get-tuple-element.46), channel_id=1, source_target_pairs={{0,35},{1,0},{2,1},{3,2},{4,39},{5,4},{6,5},{7,6},{8,43},{9,8},{10... | collective-permute-start | bytes 49160 | tf_op jit(solution)/shard_map/ppermute | solution.py:245
  11.3 7.0 %collective-permute-start = (bf16[1,128,512]{2,1,0:T(8,128)(2,1)S(1)}, bf16[1,128,512]{2,1,0:T(8,128)(2,1)S(1)}, u32[]{:S(2)}, u32[]{:S(2)}) collective-permute-start(bf16[1,128,512]{2,1,0:T(8,128)(2,1)S(1)} %get-tuple-element.45), channel_id=1, source_target_pairs={{0,16},{16,32},{32,48},{48,64},{64,80},{80,96},{96,112},{112,128},... | collective-permute-start | bytes 393224 | tf_op jit(solution)/shard_map/ppermute | solution.py:319
  18.8 4.0 %collective-permute-start.5 = (bf16[32,512]{1,0:T(8,128)(2,1)S(1)}, bf16[32,512]{1,0:T(8,128)(2,1)S(1)}, u32[]{:S(2)}, u32[]{:S(2)}) collective-permute-start(bf16[32,512]{1,0:T(8,128)(2,1)S(1)} %pad_maximum_fusion.1), channel_id=1, source_target_pairs={{0,33},{1,34},{2,35},{3,0},{4,37},{5,38},{6,39},{7,4},{8,41},{9,42... | collective-permute-start | bytes 98312 | tf_op jit(solution)/shard_map/ppermute | solution.py:245
  22.9 1.2 %collective-permute-done.5 = bf16[32,512]{1,0:T(8,128)(2,1)S(1)} collective-permute-done((bf16[32,512]{1,0:T(8,128)(2,1)S(1)}, bf16[32,512]{1,0:T(8,128)(2,1)S(1)}, u32[]{:S(2)}, u32[]{:S(2)}) %collective-permute-start.5) | collective-permute-done | bytes 32800 | tf_op jit(solution)/shard_map/ppermute | solution.py:245
  24.5 1.4 %collective-permute-start.10 = (bf16[128,512]{1,0:T(8,128)(2,1)S(1)}, bf16[128,512]{1,0:T(8,128)(2,1)S(1)}, u32[]{:S(2)}, u32[]{:S(2)}) collective-permute-start(bf16[128,512]{1,0:T(8,128)(2,1)S(1)} %get-tuple-element.85), channel_id=1, source_target_pairs={{0,64},{1,65},{2,66},{3,67},{4,68},{5,69},{6,70},{7,71},{8,72},{9,... | collective-permute-start | bytes 393224 | tf_op jit(solution)/shard_map/ppermute | solution.py:245
  25.9 1.5 %collective-permute-start.11 = (bf16[128,512]{1,0:T(8,128)(2,1)S(1)}, bf16[128,512]{1,0:T(8,128)(2,1)S(1)}, u32[]{:S(2)}, u32[]{:S(2)}) collective-permute-start(bf16[128,512]{1,0:T(8,128)(2,1)S(1)} %get-tuple-element.85), channel_id=1, source_target_pairs={{0,192},{1,193},{2,194},{3,195},{4,196},{5,197},{6,198},{7,199},{8... | collective-permute-start | bytes 393224 | tf_op jit(solution)/shard_map/ppermute | solution.py:245
  27.4 2.7 %collective-permute-start.3 = (bf16[1,128,512]{2,1,0:T(8,128)(2,1)S(1)}, bf16[1,128,512]{2,1,0:T(8,128)(2,1)S(1)}, u32[]{:S(2)}, u32[]{:S(2)}) collective-permute-start(bf16[1,128,512]{2,1,0:T(8,128)(2,1)S(1)} %get-tuple-element.48), channel_id=1, source_target_pairs={{16,0},{32,16},{48,32},{64,48},{80,64},{96,80},{112,96},{128,112},... | collective-permute-start | bytes 393224 | tf_op jit(solution)/shard_map/ppermute | solution.py:319
  30.1 3.2 %collective-permute-start.6 = (bf16[1,128,512]{2,1,0:T(8,128)(2,1)S(1)}, bf16[1,128,512]{2,1,0:T(8,128)(2,1)S(1)}, u32[]{:S(2)}, u32[]{:S(2)}) collective-permute-start(bf16[1,128,512]{2,1,0:T(8,128)(2,1)S(1)} %get-tuple-element.55), channel_id=1, source_target_pairs={{0,4},{4,8},{8,12},{1,5},{5,9},{9,13},{2,6},{6,10},{10,14},{3,7},{... | collective-permute-start | bytes 393224 | tf_op jit(solution)/shard_map/ppermute | solution.py:319
  33.3 1.3 %collective-permute-start.7 = (bf16[1,128,512]{2,1,0:T(8,128)(2,1)S(1)}, bf16[1,128,512]{2,1,0:T(8,128)(2,1)S(1)}, u32[]{:S(2)}, u32[]{:S(2)}) collective-permute-start(bf16[1,128,512]{2,1,0:T(8,128)(2,1)S(1)} %get-tuple-element.56), channel_id=1, source_target_pairs={{4,0},{8,4},{12,8},{5,1},{9,5},{13,9},{6,2},{10,6},{14,10},{7,3},{... | collective-permute-start | bytes 393224 | tf_op jit(solution)/shard_map/ppermute | solution.py:319
  34.6 2.0 %collective-permute-start.8 = (bf16[1,128,512]{2,1,0:T(8,128)(2,1)S(1)}, bf16[1,128,512]{2,1,0:T(8,128)(2,1)S(1)}, u32[]{:S(2)}, u32[]{:S(2)}) collective-permute-start(bf16[1,128,512]{2,1,0:T(8,128)(2,1)S(1)} %get-tuple-element.57), channel_id=1, source_target_pairs={{0,1},{1,2},{2,3},{3,32},{4,5},{5,6},{6,7},{7,36},{8,9},{9,10},{10... | collective-permute-start | bytes 393224 | tf_op jit(solution)/shard_map/ppermute | solution.py:245
  38.1 1.5 %collective-permute-start.12 = (bf16[64,512]{1,0:T(8,128)(2,1)S(1)}, bf16[64,512]{1,0:T(8,128)(2,1)S(1)}, u32[]{:S(2)}, u32[]{:S(2)}) collective-permute-start(bf16[64,512]{1,0:T(8,128)(2,1)S(1)} %slice.18), channel_id=1, source_target_pairs={{0,64},{1,65},{2,66},{3,67},{4,68},{5,69},{6,70},{7,71},{8,72},{9,... | collective-permute-start | bytes 196616 | tf_op jit(solution)/shard_map/ppermute | solution.py:245
  39.6 1.5 %collective-permute-start.13 = (bf16[64,512]{1,0:T(8,128)(2,1)S(1)}, bf16[64,512]{1,0:T(8,128)(2,1)S(1)}, u32[]{:S(2)}, u32[]{:S(2)}) collective-permute-start(bf16[64,512]{1,0:T(8,128)(2,1)S(1)} %slice.19), channel_id=1, source_target_pairs={{0,192},{1,193},{2,194},{3,195},{4,196},{5,197},{6,198},{7,199},{8... | collective-permute-start | bytes 196616 | tf_op jit(solution)/shard_map/ppermute | solution.py:245
  41.1 0.9 %collective-permute-done.8.g4 = bf16[1,128,512]{2,1,0:T(8,128)(2,1)S(1)} collective-permute-done((bf16[1,128,512]{2,1,0:T(8,128)(2,1)S(1)}, bf16[1,128,512]{2,1,0:T(8,128)(2,1)S(1)}, u32[]{:S(2)}, u32[]{:S(2)}) %collective-permute-start.8) | collective-permute-done | bytes 131104 | tf_op jit(solution)/shard_map/ppermute | solution.py:245
  42.1 1.2 %shard_map.257.table = bf16[1792,512]{1,0:T(8,128)(2,1)S(1)} custom-call(bf16[1024,512]{1,0:T(8,128)(2,1)S(1)} %get-tuple-element.44.sender, bf16[1,128,512]{2,1,0:T(8,128)(2,1)S(1)} %collective-permute-done.g0, bf16[1,128,512]{2,1,0:T(8,128)(2,1)S(1)} %collective-permute-done.3.g1, bf16[1,128,512]{2,1,0:T(8,128)(2,1)S(1)} %collective-permute-done.6.g2, ...), custom_call_target="tpu_custom_call" | custom-call | tf_op jit(solution)/shard_map/pallas_call | solution.py:263
  43.7 2.4 %collective-permute-start.15 = (bf16[512,512]{1,0:T(8,128)(2,1)S(1)}, bf16[512,512]{1,0:T(8,128)(2,1)S(1)}, u32[]{:S(2)}, u32[]{:S(2)}) collective-permute-start(bf16[512,512]{1,0:T(8,128)(2,1)S(1)} %constant_dynamic-update-slice_fusion.5.m0), channel_id=1, source_target_pairs={{0,12},{1,13},{2,14},{3,15},{4,0},{5,1},{6,2},{7,3},{8,4},{9,5},{1... | collective-permute-start | bytes 1572872 | tf_op jit(solution)/shard_map/ppermute | solution.py:245
  46.1 10.5 %shard_map.258.rest_0_ = f32[512,512]{1,0:T(8,128)S(1)} custom-call(bf16[1792,512]{1,0:T(8,128)(2,1)S(1)} %shard_map.257.table, bf16[1024,512]{1,0:T(8,128)(2,1)S(1)} %copy-done, s32[1024,8]{1,0:T(8,128)S(1)} %get-tuple-element.63.nbrs, bf16[1024,512]{1,0:T(8,128)(2,1)S(1)} %copy-done.1, f32[1,512]{1,0:T(1,128)S(1)} %bitcast.15, ...), custom_call_target="tpu_custom_call" | custom-call | flops 6800000000 | bytes 12000000 | tf_op jit(solution)/shard_map/pallas_call | solution.py:263
  56.8 2.7 %collective-permute-start.17 = (bf16[256,512]{1,0:T(8,128)(2,1)S(1)}, bf16[256,512]{1,0:T(8,128)(2,1)S(1)}, u32[]{:S(2)}, u32[]{:S(2)}) collective-permute-start(bf16[256,512]{1,0:T(8,128)(2,1)S(1)} %slice.17), channel_id=1, source_target_pairs={{0,12},{1,13},{2,14},{3,15},{4,0},{5,1},{6,2},{7,3},{8,4},{9,5},{1... | collective-permute-start | bytes 786440 | tf_op jit(solution)/shard_map/ppermute | solution.py:245
  59.5 5.2 %shard_map.259.rest_1_ = f32[256,512]{1,0:T(8,128)S(1)} custom-call(bf16[1792,512]{1,0:T(8,128)(2,1)S(1)} %shard_map.257.table, bf16[1024,512]{1,0:T(8,128)(2,1)S(1)} %copy-done, s32[1024,8]{1,0:T(8,128)S(1)} %get-tuple-element.63.nbrs, bf16[1024,512]{1,0:T(8,128)(2,1)S(1)} %copy-done.1, f32[1,512]{1,0:T(1,128)S(1)} %bitcast.16, ...), custom_call_target="tpu_custom_call" | custom-call | flops 3400000000 | bytes 6000000 | tf_op jit(solution)/shard_map/pallas_call | solution.py:263
  64.8 7.3 %collective-permute-start.18 = (bf16[512,512]{1,0:T(8,128)(2,1)S(1)}, bf16[512,512]{1,0:T(8,128)(2,1)S(1)}, u32[]{:S(2)}, u32[]{:S(2)}) collective-permute-start(bf16[512,512]{1,0:T(8,128)(2,1)S(1)} %constant_dynamic-update-slice_fusion.5.m0), channel_id=1, source_target_pairs={{0,16},{1,17},{2,18},{3,19},{4,20},{5,21},{6,22},{7,23},{8,24},{9,... | collective-permute-start | bytes 1572872 | tf_op jit(solution)/shard_map/ppermute | solution.py:245
  73.1 2.4 %shard_map.260.found = bf16[1024,512]{1,0:T(8,128)(2,1)S(1)} custom-call(s32[16,64]{1,0:T(8,128)S(1)} %get-tuple-element.43.slots, bf16[512,512]{1,0:T(8,128)(2,1)S(1)} %constant_dynamic-update-slice_fusion.5.m0, bf16[512,512]{1,0:T(8,128)(2,1)S(1)} %collective-permute-done.14.m1, bf16[512,512]{1,0:T(8,128)(2,1)S(1)} %collective-permute-done.15.m2, ...), custom_call_target="tpu_custom_call" | custom-call | flops 2000000000 | bytes 4000000 | tf_op jit(solution)/shard_map/pallas_call | solution.py:263
  75.6 5.2 %shard_map.261.rest_2_ = f32[256,512]{1,0:T(8,128)S(1)} custom-call(bf16[1792,512]{1,0:T(8,128)(2,1)S(1)} %shard_map.257.table, bf16[1024,512]{1,0:T(8,128)(2,1)S(1)} %copy-done, s32[1024,8]{1,0:T(8,128)S(1)} %get-tuple-element.63.nbrs, bf16[1024,512]{1,0:T(8,128)(2,1)S(1)} %copy-done.1, f32[1,512]{1,0:T(1,128)S(1)} %bitcast.17, ...), custom_call_target="tpu_custom_call" | custom-call | flops 3400000000 | bytes 6000000 | tf_op jit(solution)/shard_map/pallas_call | solution.py:263
  80.9 6.7 %shard_map.262 = (bf16[1024,512]{1,0:T(8,128)(2,1)}, bf16[128,512]{1,0:T(8,128)(2,1)}, bf16[16,512]{1,0:T(8,128)(2,1)}) custom-call(bf16[1024,512]{1,0:T(8,128)(2,1)S(1)} %shard_map.260.found, bf16[512,512]{1,0:T(8,128)(2,1)S(1)} %collective-permute-done.18.o0, bf16[512,512]{1,0:T(8,128)(2,1)S(1)} %collective-permute-done.19.o1, ...), custom_call_target="tpu_custom_call" | custom-call | tf_op jit(solution)/shard_map/pallas_call | solution.py:263
  (72 shorter events, 4.0 us)
Async XLA Ops:
  4.7 13.5 %collective-permute-start.1 = (bf16[16,512]{1,0:T(8,128)(2,1)S(1)}, bf16[16,512]{1,0:T(8,128)(2,1)S(1)}, u32[]{:S(2)}, u32[]{:S(2)}) collective-permute-start(bf16[16,512]{1,0:T(8,128)(2,1)S(1)} %get-tuple-element.46), channel_id=1, source_target_pairs={{0,1},{1,2},{2,3},{3,32},{4,5},{5,6},{6,7},{7,36},{8,9},{9,10},{10... | collective-permute-start | bytes 49160 | tf_op jit(solution)/shard_map/ppermute | solution.py:245
  7.3 11.0 %collective-permute-start.2 = (bf16[16,512]{1,0:T(8,128)(2,1)S(1)}, bf16[16,512]{1,0:T(8,128)(2,1)S(1)}, u32[]{:S(2)}, u32[]{:S(2)}) collective-permute-start(bf16[16,512]{1,0:T(8,128)(2,1)S(1)} %get-tuple-element.46), channel_id=1, source_target_pairs={{0,35},{1,0},{2,1},{3,2},{4,39},{5,4},{6,5},{7,6},{8,43},{9,8},{10... | collective-permute-start | bytes 49160 | tf_op jit(solution)/shard_map/ppermute | solution.py:245
  11.3 22.0 %collective-permute-start = (bf16[1,128,512]{2,1,0:T(8,128)(2,1)S(1)}, bf16[1,128,512]{2,1,0:T(8,128)(2,1)S(1)}, u32[]{:S(2)}, u32[]{:S(2)}) collective-permute-start(bf16[1,128,512]{2,1,0:T(8,128)(2,1)S(1)} %get-tuple-element.45), channel_id=1, source_target_pairs={{0,16},{16,32},{32,48},{48,64},{64,80},{80,96},{96,112},{112,128},... | collective-permute-start | bytes 393224 | tf_op jit(solution)/shard_map/ppermute | solution.py:319
  18.3 6.2 %collective-permute-start.4 = (bf16[48,512]{1,0:T(8,128)(2,1)S(1)}, bf16[48,512]{1,0:T(8,128)(2,1)S(1)}, u32[]{:S(2)}, u32[]{:S(2)}) collective-permute-start(bf16[48,512]{1,0:T(8,128)(2,1)S(1)} %pad_maximum_fusion), channel_id=1, source_target_pairs={{0,3},{1,32},{2,33},{3,34},{4,7},{5,36},{6,37},{7,38},{8,11},{9,40... | collective-permute-start | bytes 147464 | tf_op jit(solution)/shard_map/ppermute | solution.py:245
  18.8 5.2 %collective-permute-start.5 = (bf16[32,512]{1,0:T(8,128)(2,1)S(1)}, bf16[32,512]{1,0:T(8,128)(2,1)S(1)}, u32[]{:S(2)}, u32[]{:S(2)}) collective-permute-start(bf16[32,512]{1,0:T(8,128)(2,1)S(1)} %pad_maximum_fusion.1), channel_id=1, source_target_pairs={{0,33},{1,34},{2,35},{3,0},{4,37},{5,38},{6,39},{7,4},{8,41},{9,42... | collective-permute-start | bytes 98312 | tf_op jit(solution)/shard_map/ppermute | solution.py:245
  24.5 10.1 %collective-permute-start.10 = (bf16[128,512]{1,0:T(8,128)(2,1)S(1)}, bf16[128,512]{1,0:T(8,128)(2,1)S(1)}, u32[]{:S(2)}, u32[]{:S(2)}) collective-permute-start(bf16[128,512]{1,0:T(8,128)(2,1)S(1)} %get-tuple-element.85), channel_id=1, source_target_pairs={{0,64},{1,65},{2,66},{3,67},{4,68},{5,69},{6,70},{7,71},{8,72},{9,... | collective-permute-start | bytes 393224 | tf_op jit(solution)/shard_map/ppermute | solution.py:245
  25.9 10.8 %collective-permute-start.11 = (bf16[128,512]{1,0:T(8,128)(2,1)S(1)}, bf16[128,512]{1,0:T(8,128)(2,1)S(1)}, u32[]{:S(2)}, u32[]{:S(2)}) collective-permute-start(bf16[128,512]{1,0:T(8,128)(2,1)S(1)} %get-tuple-element.85), channel_id=1, source_target_pairs={{0,192},{1,193},{2,194},{3,195},{4,196},{5,197},{6,198},{7,199},{8... | collective-permute-start | bytes 393224 | tf_op jit(solution)/shard_map/ppermute | solution.py:245
  27.4 10.7 %collective-permute-start.3 = (bf16[1,128,512]{2,1,0:T(8,128)(2,1)S(1)}, bf16[1,128,512]{2,1,0:T(8,128)(2,1)S(1)}, u32[]{:S(2)}, u32[]{:S(2)}) collective-permute-start(bf16[1,128,512]{2,1,0:T(8,128)(2,1)S(1)} %get-tuple-element.48), channel_id=1, source_target_pairs={{16,0},{32,16},{48,32},{64,48},{80,64},{96,80},{112,96},{128,112},... | collective-permute-start | bytes 393224 | tf_op jit(solution)/shard_map/ppermute | solution.py:319
  30.1 9.5 %collective-permute-start.6 = (bf16[1,128,512]{2,1,0:T(8,128)(2,1)S(1)}, bf16[1,128,512]{2,1,0:T(8,128)(2,1)S(1)}, u32[]{:S(2)}, u32[]{:S(2)}) collective-permute-start(bf16[1,128,512]{2,1,0:T(8,128)(2,1)S(1)} %get-tuple-element.55), channel_id=1, source_target_pairs={{0,4},{4,8},{8,12},{1,5},{5,9},{9,13},{2,6},{6,10},{10,14},{3,7},{... | collective-permute-start | bytes 393224 | tf_op jit(solution)/shard_map/ppermute | solution.py:319
  33.3 7.8 %collective-permute-start.7 = (bf16[1,128,512]{2,1,0:T(8,128)(2,1)S(1)}, bf16[1,128,512]{2,1,0:T(8,128)(2,1)S(1)}, u32[]{:S(2)}, u32[]{:S(2)}) collective-permute-start(bf16[1,128,512]{2,1,0:T(8,128)(2,1)S(1)} %get-tuple-element.56), channel_id=1, source_target_pairs={{4,0},{8,4},{12,8},{5,1},{9,5},{13,9},{6,2},{10,6},{14,10},{7,3},{... | collective-permute-start | bytes 393224 | tf_op jit(solution)/shard_map/ppermute | solution.py:319
  34.6 7.4 %collective-permute-start.8 = (bf16[1,128,512]{2,1,0:T(8,128)(2,1)S(1)}, bf16[1,128,512]{2,1,0:T(8,128)(2,1)S(1)}, u32[]{:S(2)}, u32[]{:S(2)}) collective-permute-start(bf16[1,128,512]{2,1,0:T(8,128)(2,1)S(1)} %get-tuple-element.57), channel_id=1, source_target_pairs={{0,1},{1,2},{2,3},{3,32},{4,5},{5,6},{6,7},{7,36},{8,9},{9,10},{10... | collective-permute-start | bytes 393224 | tf_op jit(solution)/shard_map/ppermute | solution.py:245
  36.7 5.3 %collective-permute-start.9 = (bf16[1,128,512]{2,1,0:T(8,128)(2,1)S(1)}, bf16[1,128,512]{2,1,0:T(8,128)(2,1)S(1)}, u32[]{:S(2)}, u32[]{:S(2)}) collective-permute-start(bf16[1,128,512]{2,1,0:T(8,128)(2,1)S(1)} %get-tuple-element.58), channel_id=1, source_target_pairs={{0,35},{1,0},{2,1},{3,2},{4,39},{5,4},{6,5},{7,6},{8,43},{9,8},{10... | collective-permute-start | bytes 393224 | tf_op jit(solution)/shard_map/ppermute | solution.py:245
  38.1 5.2 %collective-permute-start.12 = (bf16[64,512]{1,0:T(8,128)(2,1)S(1)}, bf16[64,512]{1,0:T(8,128)(2,1)S(1)}, u32[]{:S(2)}, u32[]{:S(2)}) collective-permute-start(bf16[64,512]{1,0:T(8,128)(2,1)S(1)} %slice.18), channel_id=1, source_target_pairs={{0,64},{1,65},{2,66},{3,67},{4,68},{5,69},{6,70},{7,71},{8,72},{9,... | collective-permute-start | bytes 196616 | tf_op jit(solution)/shard_map/ppermute | solution.py:245
  39.6 3.7 %collective-permute-start.13 = (bf16[64,512]{1,0:T(8,128)(2,1)S(1)}, bf16[64,512]{1,0:T(8,128)(2,1)S(1)}, u32[]{:S(2)}, u32[]{:S(2)}) collective-permute-start(bf16[64,512]{1,0:T(8,128)(2,1)S(1)} %slice.19), channel_id=1, source_target_pairs={{0,192},{1,193},{2,194},{3,195},{4,196},{5,197},{6,198},{7,199},{8... | collective-permute-start | bytes 196616 | tf_op jit(solution)/shard_map/ppermute | solution.py:245
  43.3 13.3 %collective-permute-start.14 = (bf16[512,512]{1,0:T(8,128)(2,1)S(1)}, bf16[512,512]{1,0:T(8,128)(2,1)S(1)}, u32[]{:S(2)}, u32[]{:S(2)}) collective-permute-start(bf16[512,512]{1,0:T(8,128)(2,1)S(1)} %constant_dynamic-update-slice_fusion.5.m0), channel_id=1, source_target_pairs={{0,4},{1,5},{2,6},{3,7},{4,8},{5,9},{6,10},{7,11},{8,12},{9,13},{1... | collective-permute-start | bytes 1572872 | tf_op jit(solution)/shard_map/ppermute | solution.py:245
  43.7 13.0 %collective-permute-start.15 = (bf16[512,512]{1,0:T(8,128)(2,1)S(1)}, bf16[512,512]{1,0:T(8,128)(2,1)S(1)}, u32[]{:S(2)}, u32[]{:S(2)}) collective-permute-start(bf16[512,512]{1,0:T(8,128)(2,1)S(1)} %constant_dynamic-update-slice_fusion.5.m0), channel_id=1, source_target_pairs={{0,12},{1,13},{2,14},{3,15},{4,0},{5,1},{6,2},{7,3},{8,4},{9,5},{1... | collective-permute-start | bytes 1572872 | tf_op jit(solution)/shard_map/ppermute | solution.py:245
  56.6 8.2 %copy-start.2 = (f32[512,512]{1,0:T(8,128)}, f32[512,512]{1,0:T(8,128)S(1)}, u32[]{:S(2)}) copy-start(f32[512,512]{1,0:T(8,128)S(1)} %shard_map.258.rest_0_) | copy-start | bytes 3145732
  56.7 8.1 %collective-permute-start.16 = (bf16[256,512]{1,0:T(8,128)(2,1)S(1)}, bf16[256,512]{1,0:T(8,128)(2,1)S(1)}, u32[]{:S(2)}, u32[]{:S(2)}) collective-permute-start(bf16[256,512]{1,0:T(8,128)(2,1)S(1)} %slice.16), channel_id=1, source_target_pairs={{0,4},{1,5},{2,6},{3,7},{4,8},{5,9},{6,10},{7,11},{8,12},{9,13},{1... | collective-permute-start | bytes 786440 | tf_op jit(solution)/shard_map/ppermute | solution.py:245
  56.8 8.0 %collective-permute-start.17 = (bf16[256,512]{1,0:T(8,128)(2,1)S(1)}, bf16[256,512]{1,0:T(8,128)(2,1)S(1)}, u32[]{:S(2)}, u32[]{:S(2)}) collective-permute-start(bf16[256,512]{1,0:T(8,128)(2,1)S(1)} %slice.17), channel_id=1, source_target_pairs={{0,12},{1,13},{2,14},{3,15},{4,0},{5,1},{6,2},{7,3},{8,4},{9,5},{1... | collective-permute-start | bytes 786440 | tf_op jit(solution)/shard_map/ppermute | solution.py:245
  64.8 16.0 %collective-permute-start.18 = (bf16[512,512]{1,0:T(8,128)(2,1)S(1)}, bf16[512,512]{1,0:T(8,128)(2,1)S(1)}, u32[]{:S(2)}, u32[]{:S(2)}) collective-permute-start(bf16[512,512]{1,0:T(8,128)(2,1)S(1)} %constant_dynamic-update-slice_fusion.5.m0), channel_id=1, source_target_pairs={{0,16},{1,17},{2,18},{3,19},{4,20},{5,21},{6,22},{7,23},{8,24},{9,... | collective-permute-start | bytes 1572872 | tf_op jit(solution)/shard_map/ppermute | solution.py:245
  72.1 8.7 %collective-permute-start.19 = (bf16[512,512]{1,0:T(8,128)(2,1)S(1)}, bf16[512,512]{1,0:T(8,128)(2,1)S(1)}, u32[]{:S(2)}, u32[]{:S(2)}) collective-permute-start(bf16[512,512]{1,0:T(8,128)(2,1)S(1)} %collective-permute-done.14.m1), channel_id=1, source_target_pairs={{0,16},{1,17},{2,18},{3,19},{4,20},{5,21},{6,22},{7,23},{8,24},{9,... | collective-permute-start | bytes 1572872 | tf_op jit(solution)/shard_map/ppermute | solution.py:245
  72.2 8.6 %collective-permute-start.20 = (bf16[512,512]{1,0:T(8,128)(2,1)S(1)}, bf16[512,512]{1,0:T(8,128)(2,1)S(1)}, u32[]{:S(2)}, u32[]{:S(2)}) collective-permute-start(bf16[512,512]{1,0:T(8,128)(2,1)S(1)} %collective-permute-done.15.m2), channel_id=1, source_target_pairs={{0,16},{1,17},{2,18},{3,19},{4,20},{5,21},{6,22},{7,23},{8,24},{9,... | collective-permute-start | bytes 1572872 | tf_op jit(solution)/shard_map/ppermute | solution.py:245
  72.6 8.2 %collective-permute-start.21 = (bf16[256,512]{1,0:T(8,128)(2,1)S(1)}, bf16[256,512]{1,0:T(8,128)(2,1)S(1)}, u32[]{:S(2)}, u32[]{:S(2)}) collective-permute-start(bf16[256,512]{1,0:T(8,128)(2,1)S(1)} %collective-permute-done.16.m3), channel_id=1, source_target_pairs={{0,16},{1,17},{2,18},{3,19},{4,20},{5,21},{6,22},{7,23},{8,24},{9,... | collective-permute-start | bytes 786440 | tf_op jit(solution)/shard_map/ppermute | solution.py:245
  72.7 8.1 %collective-permute-start.22 = (bf16[256,512]{1,0:T(8,128)(2,1)S(1)}, bf16[256,512]{1,0:T(8,128)(2,1)S(1)}, u32[]{:S(2)}, u32[]{:S(2)}) collective-permute-start(bf16[256,512]{1,0:T(8,128)(2,1)S(1)} %collective-permute-done.17.m4), channel_id=1, source_target_pairs={{0,16},{1,17},{2,18},{3,19},{4,20},{5,21},{6,22},{7,23},{8,24},{9,... | collective-permute-start | bytes 786440 | tf_op jit(solution)/shard_map/ppermute | solution.py:245
  (13 other events, 59.2 us)

commit v8 on v7

--- a/solution.py
+++ b/solution.py
@@ -319,15 +319,15 @@
         return lax.ppermute(faces[face], axes, [(b, a) for a, b in pairs] if face % 2 == 0 else pairs)
 
     low, high = sent(sender, UP_Z), sent(sender, DOWN_Z)
-    low_x = faced(1)
-    low, high, faces[0] = tied((low, high, faces[0]))
+    low_y = faced(3)
+    low, high, low_y, faces[0], faces[1] = tied((low, high, low_y, faces[0], faces[1]))
     three = joined(high, sender, low)
     lower, higher = sent(three, UP_3Z), sent(three[16:], DOWN_3Z)
-    high_x = faced(0)
-    lower, higher, *faces[2:] = tied((lower, higher, *faces[2:]))
+    low_x, high_x = faced(1), faced(0)
+    lower, higher, low_x, faces[2], faces[4], faces[5] = tied((lower, higher, low_x, faces[2], faces[4], faces[5]))
     column = joined(three, lower, higher)
     up, down = sent(column, UP_FIRST), sent(column, DOWN_FIRST)
-    low_y, high_y = faced(3), faced(2)
+    high_y = faced(2)
     low_z, high_z = sent(faces[5], UP_Z), sent(faces[4], DOWN_Z)
     near_faces = [low_x, high_x, low_y, high_y, low_z, high_z]
     (table,) = kernel(

time: 87.8 us -> 89.4 us (1.018)
  waiting for transfers between devices: 3.23 us -> 6.07 us
  starting transfers between devices: 47.8 us -> 46.6 us
    ppermute x19, starting transfers between devices: 33.7 us -> 27.5 us  [sent(): return lax.ppermute(rows, AXES, pairs)]
    ppermute x4, starting transfers between devices: 14.1 us -> 19.1 us  [faced(): lax.ppermute(faces[face], axes, [(b, a) for a, b in pairs] if face % 2 ==...]
    ppermute x19, waiting for transfers between devices: 2.54 us -> 4.01 us  [sent(): return lax.ppermute(rows, AXES, pairs)]
    ppermute x4, waiting for transfers between devices: 0.69 us -> 2.06 us  [faced(): lax.ppermute(faces[face], axes, [(b, a) for a, b in pairs] if face % 2 ==...]
  transfers between devices with their start and end apart: 23 -> 23, of which waited for: 4 -> 4; matrix products, arithmetic and copies ran while one was open for 0% -> 0% of each run, Pallas kernels for 28% -> 27%
where the time goes in v8:
time: 89.4 us; the launch traced here: 89.2 us
  starting transfers between devices  46.6 us (52%)
  Pallas kernels  35.2 us (39%)
  waiting for transfers between devices  6.07 us (7%)
  between operations  1.12 us (1%)
    pallas_call x7, Pallas kernels, kernel(): pl.pallas_call(body, grid=(1,), out_shape=outs, in_specs=specs, out_specs...  35.2 us
    ppermute x19, starting transfers between devices, sent(): return lax.ppermute(rows, AXES, pairs)  27.5 us
    ppermute x4, starting transfers between devices, faced(): lax.ppermute(faces[face], axes, [(b, a) for a, b in pairs] if face % 2 ==...  19.1 us
    ppermute x19, waiting for transfers between devices, sent(): return lax.ppermute(rows, AXES, pairs)  4.01 us
    ppermute x4, waiting for transfers between devices, faced(): lax.ppermute(faces[face], axes, [(b, a) for a, b in pairs] if face % 2 ==...  2.06 us
  transfers between devices with their start and end apart: 23, of which 4 were waited for; matrix products, arithmetic and copies ran while one was open for 0% of the time, Pallas kernels for 27%

profile of v8, /device:TPU:1, one launch (start us, length us, event | category | flops | bytes accessed | tf_op | source)
XLA Modules:
  0.0 89.2 jit_solution(2178421739137699029)
XLA Ops:
  0.6 4.1 %shard_map.256 = (bf16[16,512]{1,0:T(8,128)(2,1)S(1)}, bf16[16,512]{1,0:T(8,128)(2,1)S(1)}, f32[128,512]{1,0:T(8,128)S(1)}, s32[16,64]{1,0:T(8,128)S(1)}, bf16[3...) custom-call(bf16[1024,512]{1,0:T(8,128)(2,1)} %fine.5, ...), custom_call_target="tpu_custom_call" | custom-call | tf_op jit(solution)/shard_map/pallas_call | solution.py:263
  4.7 4.0 %collective-permute-start.2 = (bf16[1,128,512]{2,1,0:T(8,128)(2,1)S(1)}, bf16[1,128,512]{2,1,0:T(8,128)(2,1)S(1)}, u32[]{:S(2)}, u32[]{:S(2)}) collective-permute-start(bf16[1,128,512]{2,1,0:T(8,128)(2,1)S(1)} %get-tuple-element.48), channel_id=1, source_target_pairs={{0,4},{4,8},{8,12},{1,5},{5,9},{9,13},{2,6},{6,10},{10,14},{3,7},{... | collective-permute-start | bytes 393224 | tf_op jit(solution)/shard_map/ppermute | solution.py:319
  8.8 1.7 %collective-permute-start = (bf16[16,512]{1,0:T(8,128)(2,1)S(1)}, bf16[16,512]{1,0:T(8,128)(2,1)S(1)}, u32[]{:S(2)}, u32[]{:S(2)}) collective-permute-start(bf16[16,512]{1,0:T(8,128)(2,1)S(1)} %get-tuple-element.47), channel_id=1, source_target_pairs={{0,1},{1,2},{2,3},{3,32},{4,5},{5,6},{6,7},{7,36},{8,9},{9,10},{10... | collective-permute-start | bytes 49160 | tf_op jit(solution)/shard_map/ppermute | solution.py:245
  10.5 4.0 %collective-permute-start.1 = (bf16[16,512]{1,0:T(8,128)(2,1)S(1)}, bf16[16,512]{1,0:T(8,128)(2,1)S(1)}, u32[]{:S(2)}, u32[]{:S(2)}) collective-permute-start(bf16[16,512]{1,0:T(8,128)(2,1)S(1)} %get-tuple-element.47), channel_id=1, source_target_pairs={{0,35},{1,0},{2,1},{3,2},{4,39},{5,4},{6,5},{7,6},{8,43},{9,8},{10... | collective-permute-start | bytes 49160 | tf_op jit(solution)/shard_map/ppermute | solution.py:245
  15.6 4.4 %collective-permute-start.3 = (bf16[48,512]{1,0:T(8,128)(2,1)S(1)}, bf16[48,512]{1,0:T(8,128)(2,1)S(1)}, u32[]{:S(2)}, u32[]{:S(2)}) collective-permute-start(bf16[48,512]{1,0:T(8,128)(2,1)S(1)} %pad_maximum_fusion), channel_id=1, source_target_pairs={{0,3},{1,32},{2,33},{3,34},{4,7},{5,36},{6,37},{7,38},{8,11},{9,40... | collective-permute-start | bytes 147464 | tf_op jit(solution)/shard_map/ppermute | solution.py:245
  20.1 8.5 %collective-permute-start.5 = (bf16[1,128,512]{2,1,0:T(8,128)(2,1)S(1)}, bf16[1,128,512]{2,1,0:T(8,128)(2,1)S(1)}, u32[]{:S(2)}, u32[]{:S(2)}) collective-permute-start(bf16[1,128,512]{2,1,0:T(8,128)(2,1)S(1)} %get-tuple-element.53), channel_id=1, source_target_pairs={{0,16},{16,32},{32,48},{48,64},{64,80},{80,96},{96,112},{112,128},... | collective-permute-start | bytes 393224 | tf_op jit(solution)/shard_map/ppermute | solution.py:319
  28.7 1.9 %collective-permute-done.5.g0 = bf16[1,128,512]{2,1,0:T(8,128)(2,1)S(1)} collective-permute-done((bf16[1,128,512]{2,1,0:T(8,128)(2,1)S(1)}, bf16[1,128,512]{2,1,0:T(8,128)(2,1)S(1)}, u32[]{:S(2)}, u32[]{:S(2)}) %collective-permute-start.5) | collective-permute-done | bytes 131104 | tf_op jit(solution)/shard_map/ppermute | solution.py:319
  30.6 1.4 %collective-permute-start.10 = (bf16[128,512]{1,0:T(8,128)(2,1)S(1)}, bf16[128,512]{1,0:T(8,128)(2,1)S(1)}, u32[]{:S(2)}, u32[]{:S(2)}) collective-permute-start(bf16[128,512]{1,0:T(8,128)(2,1)S(1)} %get-tuple-element.89), channel_id=1, source_target_pairs={{0,64},{1,65},{2,66},{3,67},{4,68},{5,69},{6,70},{7,71},{8,72},{9,... | collective-permute-start | bytes 393224 | tf_op jit(solution)/shard_map/ppermute | solution.py:245
  31.9 1.4 %collective-permute-start.11 = (bf16[128,512]{1,0:T(8,128)(2,1)S(1)}, bf16[128,512]{1,0:T(8,128)(2,1)S(1)}, u32[]{:S(2)}, u32[]{:S(2)}) collective-permute-start(bf16[128,512]{1,0:T(8,128)(2,1)S(1)} %get-tuple-element.89), channel_id=1, source_target_pairs={{0,192},{1,193},{2,194},{3,195},{4,196},{5,197},{6,198},{7,199},{8... | collective-permute-start | bytes 393224 | tf_op jit(solution)/shard_map/ppermute | solution.py:245
  33.3 5.3 %collective-permute-start.6 = (bf16[1,128,512]{2,1,0:T(8,128)(2,1)S(1)}, bf16[1,128,512]{2,1,0:T(8,128)(2,1)S(1)}, u32[]{:S(2)}, u32[]{:S(2)}) collective-permute-start(bf16[1,128,512]{2,1,0:T(8,128)(2,1)S(1)} %get-tuple-element.58), channel_id=1, source_target_pairs={{16,0},{32,16},{48,32},{64,48},{80,64},{96,80},{112,96},{128,112},... | collective-permute-start | bytes 393224 | tf_op jit(solution)/shard_map/ppermute | solution.py:319
  38.6 1.3 %collective-permute-start.7 = (bf16[1,128,512]{2,1,0:T(8,128)(2,1)S(1)}, bf16[1,128,512]{2,1,0:T(8,128)(2,1)S(1)}, u32[]{:S(2)}, u32[]{:S(2)}) collective-permute-start(bf16[1,128,512]{2,1,0:T(8,128)(2,1)S(1)} %get-tuple-element.60), channel_id=1, source_target_pairs={{4,0},{8,4},{12,8},{5,1},{9,5},{13,9},{6,2},{10,6},{14,10},{7,3},{... | collective-permute-start | bytes 393224 | tf_op jit(solution)/shard_map/ppermute | solution.py:319
  40.0 2.7 %collective-permute-start.9 = (bf16[1,128,512]{2,1,0:T(8,128)(2,1)S(1)}, bf16[1,128,512]{2,1,0:T(8,128)(2,1)S(1)}, u32[]{:S(2)}, u32[]{:S(2)}) collective-permute-start(bf16[1,128,512]{2,1,0:T(8,128)(2,1)S(1)} %get-tuple-element.62), channel_id=1, source_target_pairs={{0,35},{1,0},{2,1},{3,2},{4,39},{5,4},{6,5},{7,6},{8,43},{9,8},{10... | collective-permute-start | bytes 393224 | tf_op jit(solution)/shard_map/ppermute | solution.py:245
  42.7 2.2 %collective-permute-start.12 = (bf16[64,512]{1,0:T(8,128)(2,1)S(1)}, bf16[64,512]{1,0:T(8,128)(2,1)S(1)}, u32[]{:S(2)}, u32[]{:S(2)}) collective-permute-start(bf16[64,512]{1,0:T(8,128)(2,1)S(1)} %slice.18), channel_id=1, source_target_pairs={{0,64},{1,65},{2,66},{3,67},{4,68},{5,69},{6,70},{7,71},{8,72},{9,... | collective-permute-start | bytes 196616 | tf_op jit(solution)/shard_map/ppermute | solution.py:245
  45.1 1.4 %collective-permute-start.13 = (bf16[64,512]{1,0:T(8,128)(2,1)S(1)}, bf16[64,512]{1,0:T(8,128)(2,1)S(1)}, u32[]{:S(2)}, u32[]{:S(2)}) collective-permute-start(bf16[64,512]{1,0:T(8,128)(2,1)S(1)} %slice.19), channel_id=1, source_target_pairs={{0,192},{1,193},{2,194},{3,195},{4,196},{5,197},{6,198},{7,199},{8... | collective-permute-start | bytes 196616 | tf_op jit(solution)/shard_map/ppermute | solution.py:245
  46.5 2.9 %collective-permute-done.8.g4 = bf16[1,128,512]{2,1,0:T(8,128)(2,1)S(1)} collective-permute-done((bf16[1,128,512]{2,1,0:T(8,128)(2,1)S(1)}, bf16[1,128,512]{2,1,0:T(8,128)(2,1)S(1)}, u32[]{:S(2)}, u32[]{:S(2)}) %collective-permute-start.8) | collective-permute-done | bytes 131104 | tf_op jit(solution)/shard_map/ppermute | solution.py:245
  49.5 1.2 %shard_map.257.table = bf16[1792,512]{1,0:T(8,128)(2,1)S(1)} custom-call(bf16[1024,512]{1,0:T(8,128)(2,1)S(1)} %get-tuple-element.46.sender, bf16[1,128,512]{2,1,0:T(8,128)(2,1)S(1)} %collective-permute-done.5.g0, bf16[1,128,512]{2,1,0:T(8,128)(2,1)S(1)} %collective-permute-done.6.g1, bf16[1,128,512]{2,1,0:T(8,128)(2,1)S(1)} %collective-permute-done.2.g2, ...), custom_call_target="tpu_custom_call" | custom-call | tf_op jit(solution)/shard_map/pallas_call | solution.py:263
  50.8 2.7 %collective-permute-start.15 = (bf16[512,512]{1,0:T(8,128)(2,1)S(1)}, bf16[512,512]{1,0:T(8,128)(2,1)S(1)}, u32[]{:S(2)}, u32[]{:S(2)}) collective-permute-start(bf16[512,512]{1,0:T(8,128)(2,1)S(1)} %constant_dynamic-update-slice_fusion.5.m0), channel_id=1, source_target_pairs={{0,12},{1,13},{2,14},{3,15},{4,0},{5,1},{6,2},{7,3},{8,4},{9,5},{1... | collective-permute-start | bytes 1572872 | tf_op jit(solution)/shard_map/ppermute | solution.py:245
  53.5 10.5 %shard_map.258.rest_0_ = f32[512,512]{1,0:T(8,128)S(1)} custom-call(bf16[1792,512]{1,0:T(8,128)(2,1)S(1)} %shard_map.257.table, bf16[1024,512]{1,0:T(8,128)(2,1)S(1)} %copy-done, s32[1024,8]{1,0:T(8,128)S(1)} %get-tuple-element.67.nbrs, bf16[1024,512]{1,0:T(8,128)(2,1)S(1)} %copy-done.1, f32[1,512]{1,0:T(1,128)S(1)} %bitcast.15, ...), custom_call_target="tpu_custom_call" | custom-call | flops 6800000000 | bytes 12000000 | tf_op jit(solution)/shard_map/pallas_call | solution.py:263
  64.1 2.7 %collective-permute-start.17 = (bf16[256,512]{1,0:T(8,128)(2,1)S(1)}, bf16[256,512]{1,0:T(8,128)(2,1)S(1)}, u32[]{:S(2)}, u32[]{:S(2)}) collective-permute-start(bf16[256,512]{1,0:T(8,128)(2,1)S(1)} %slice.17), channel_id=1, source_target_pairs={{0,12},{1,13},{2,14},{3,15},{4,0},{5,1},{6,2},{7,3},{8,4},{9,5},{1... | collective-permute-start | bytes 786440 | tf_op jit(solution)/shard_map/ppermute | solution.py:245
  66.9 5.2 %shard_map.259.rest_1_ = f32[256,512]{1,0:T(8,128)S(1)} custom-call(bf16[1792,512]{1,0:T(8,128)(2,1)S(1)} %shard_map.257.table, bf16[1024,512]{1,0:T(8,128)(2,1)S(1)} %copy-done, s32[1024,8]{1,0:T(8,128)S(1)} %get-tuple-element.67.nbrs, bf16[1024,512]{1,0:T(8,128)(2,1)S(1)} %copy-done.1, f32[1,512]{1,0:T(1,128)S(1)} %bitcast.16, ...), custom_call_target="tpu_custom_call" | custom-call | flops 3400000000 | bytes 6000000 | tf_op jit(solution)/shard_map/pallas_call | solution.py:263
  72.1 1.6 %collective-permute-start.18 = (bf16[512,512]{1,0:T(8,128)(2,1)S(1)}, bf16[512,512]{1,0:T(8,128)(2,1)S(1)}, u32[]{:S(2)}, u32[]{:S(2)}) collective-permute-start(bf16[512,512]{1,0:T(8,128)(2,1)S(1)} %constant_dynamic-update-slice_fusion.5.m0), channel_id=1, source_target_pairs={{0,16},{1,17},{2,18},{3,19},{4,20},{5,21},{6,22},{7,23},{8,24},{9,... | collective-permute-start | bytes 1572872 | tf_op jit(solution)/shard_map/ppermute | solution.py:245
  74.8 2.4 %shard_map.260.found = bf16[1024,512]{1,0:T(8,128)(2,1)S(1)} custom-call(s32[16,64]{1,0:T(8,128)S(1)} %get-tuple-element.45.slots, bf16[512,512]{1,0:T(8,128)(2,1)S(1)} %constant_dynamic-update-slice_fusion.5.m0, bf16[512,512]{1,0:T(8,128)(2,1)S(1)} %collective-permute-done.14.m1, bf16[512,512]{1,0:T(8,128)(2,1)S(1)} %collective-permute-done.15.m2, ...), custom_call_target="tpu_custom_call" | custom-call | flops 2000000000 | bytes 4000000 | tf_op jit(solution)/shard_map/pallas_call | solution.py:263
  77.2 5.2 %shard_map.261.rest_2_ = f32[256,512]{1,0:T(8,128)S(1)} custom-call(bf16[1792,512]{1,0:T(8,128)(2,1)S(1)} %shard_map.257.table, bf16[1024,512]{1,0:T(8,128)(2,1)S(1)} %copy-done, s32[1024,8]{1,0:T(8,128)S(1)} %get-tuple-element.67.nbrs, bf16[1024,512]{1,0:T(8,128)(2,1)S(1)} %copy-done.1, f32[1,512]{1,0:T(1,128)S(1)} %bitcast.17, ...), custom_call_target="tpu_custom_call" | custom-call | flops 3400000000 | bytes 6000000 | tf_op jit(solution)/shard_map/pallas_call | solution.py:263
  82.5 6.7 %shard_map.262 = (bf16[1024,512]{1,0:T(8,128)(2,1)}, bf16[128,512]{1,0:T(8,128)(2,1)}, bf16[16,512]{1,0:T(8,128)(2,1)}) custom-call(bf16[1024,512]{1,0:T(8,128)(2,1)S(1)} %shard_map.260.found, bf16[512,512]{1,0:T(8,128)(2,1)S(1)} %collective-permute-done.18.o0, bf16[512,512]{1,0:T(8,128)(2,1)S(1)} %collective-permute-done.19.o1, ...), custom_call_target="tpu_custom_call" | custom-call | tf_op jit(solution)/shard_map/pallas_call | solution.py:263
  (72 shorter events, 2.9 us)
Async XLA Ops:
  4.7 10.8 %collective-permute-start.2 = (bf16[1,128,512]{2,1,0:T(8,128)(2,1)S(1)}, bf16[1,128,512]{2,1,0:T(8,128)(2,1)S(1)}, u32[]{:S(2)}, u32[]{:S(2)}) collective-permute-start(bf16[1,128,512]{2,1,0:T(8,128)(2,1)S(1)} %get-tuple-element.48), channel_id=1, source_target_pairs={{0,4},{4,8},{8,12},{1,5},{5,9},{9,13},{2,6},{6,10},{10,14},{3,7},{... | collective-permute-start | bytes 393224 | tf_op jit(solution)/shard_map/ppermute | solution.py:319
  8.8 6.8 %collective-permute-start = (bf16[16,512]{1,0:T(8,128)(2,1)S(1)}, bf16[16,512]{1,0:T(8,128)(2,1)S(1)}, u32[]{:S(2)}, u32[]{:S(2)}) collective-permute-start(bf16[16,512]{1,0:T(8,128)(2,1)S(1)} %get-tuple-element.47), channel_id=1, source_target_pairs={{0,1},{1,2},{2,3},{3,32},{4,5},{5,6},{6,7},{7,36},{8,9},{9,10},{10... | collective-permute-start | bytes 49160 | tf_op jit(solution)/shard_map/ppermute | solution.py:245
  10.5 5.1 %collective-permute-start.1 = (bf16[16,512]{1,0:T(8,128)(2,1)S(1)}, bf16[16,512]{1,0:T(8,128)(2,1)S(1)}, u32[]{:S(2)}, u32[]{:S(2)}) collective-permute-start(bf16[16,512]{1,0:T(8,128)(2,1)S(1)} %get-tuple-element.47), channel_id=1, source_target_pairs={{0,35},{1,0},{2,1},{3,2},{4,39},{5,4},{6,5},{7,6},{8,43},{9,8},{10... | collective-permute-start | bytes 49160 | tf_op jit(solution)/shard_map/ppermute | solution.py:245
  15.6 13.1 %collective-permute-start.3 = (bf16[48,512]{1,0:T(8,128)(2,1)S(1)}, bf16[48,512]{1,0:T(8,128)(2,1)S(1)}, u32[]{:S(2)}, u32[]{:S(2)}) collective-permute-start(bf16[48,512]{1,0:T(8,128)(2,1)S(1)} %pad_maximum_fusion), channel_id=1, source_target_pairs={{0,3},{1,32},{2,33},{3,34},{4,7},{5,36},{6,37},{7,38},{8,11},{9,40... | collective-permute-start | bytes 147464 | tf_op jit(solution)/shard_map/ppermute | solution.py:245
  19.9 8.7 %collective-permute-start.4 = (bf16[32,512]{1,0:T(8,128)(2,1)S(1)}, bf16[32,512]{1,0:T(8,128)(2,1)S(1)}, u32[]{:S(2)}, u32[]{:S(2)}) collective-permute-start(bf16[32,512]{1,0:T(8,128)(2,1)S(1)} %pad_maximum_fusion.1), channel_id=1, source_target_pairs={{0,33},{1,34},{2,35},{3,0},{4,37},{5,38},{6,39},{7,4},{8,41},{9,42... | collective-permute-start | bytes 98312 | tf_op jit(solution)/shard_map/ppermute | solution.py:245
  20.1 10.4 %collective-permute-start.5 = (bf16[1,128,512]{2,1,0:T(8,128)(2,1)S(1)}, bf16[1,128,512]{2,1,0:T(8,128)(2,1)S(1)}, u32[]{:S(2)}, u32[]{:S(2)}) collective-permute-start(bf16[1,128,512]{2,1,0:T(8,128)(2,1)S(1)} %get-tuple-element.53), channel_id=1, source_target_pairs={{0,16},{16,32},{32,48},{48,64},{64,80},{80,96},{96,112},{112,128},... | collective-permute-start | bytes 393224 | tf_op jit(solution)/shard_map/ppermute | solution.py:319
  30.6 9.5 %collective-permute-start.10 = (bf16[128,512]{1,0:T(8,128)(2,1)S(1)}, bf16[128,512]{1,0:T(8,128)(2,1)S(1)}, u32[]{:S(2)}, u32[]{:S(2)}) collective-permute-start(bf16[128,512]{1,0:T(8,128)(2,1)S(1)} %get-tuple-element.89), channel_id=1, source_target_pairs={{0,64},{1,65},{2,66},{3,67},{4,68},{5,69},{6,70},{7,71},{8,72},{9,... | collective-permute-start | bytes 393224 | tf_op jit(solution)/shard_map/ppermute | solution.py:245
  31.9 10.8 %collective-permute-start.11 = (bf16[128,512]{1,0:T(8,128)(2,1)S(1)}, bf16[128,512]{1,0:T(8,128)(2,1)S(1)}, u32[]{:S(2)}, u32[]{:S(2)}) collective-permute-start(bf16[128,512]{1,0:T(8,128)(2,1)S(1)} %get-tuple-element.89), channel_id=1, source_target_pairs={{0,192},{1,193},{2,194},{3,195},{4,196},{5,197},{6,198},{7,199},{8... | collective-permute-start | bytes 393224 | tf_op jit(solution)/shard_map/ppermute | solution.py:245
  33.3 11.8 %collective-permute-start.6 = (bf16[1,128,512]{2,1,0:T(8,128)(2,1)S(1)}, bf16[1,128,512]{2,1,0:T(8,128)(2,1)S(1)}, u32[]{:S(2)}, u32[]{:S(2)}) collective-permute-start(bf16[1,128,512]{2,1,0:T(8,128)(2,1)S(1)} %get-tuple-element.58), channel_id=1, source_target_pairs={{16,0},{32,16},{48,32},{64,48},{80,64},{96,80},{112,96},{128,112},... | collective-permute-start | bytes 393224 | tf_op jit(solution)/shard_map/ppermute | solution.py:319
  38.6 7.8 %collective-permute-start.7 = (bf16[1,128,512]{2,1,0:T(8,128)(2,1)S(1)}, bf16[1,128,512]{2,1,0:T(8,128)(2,1)S(1)}, u32[]{:S(2)}, u32[]{:S(2)}) collective-permute-start(bf16[1,128,512]{2,1,0:T(8,128)(2,1)S(1)} %get-tuple-element.60), channel_id=1, source_target_pairs={{4,0},{8,4},{12,8},{5,1},{9,5},{13,9},{6,2},{10,6},{14,10},{7,3},{... | collective-permute-start | bytes 393224 | tf_op jit(solution)/shard_map/ppermute | solution.py:319
  39.9 9.4 %collective-permute-start.8 = (bf16[1,128,512]{2,1,0:T(8,128)(2,1)S(1)}, bf16[1,128,512]{2,1,0:T(8,128)(2,1)S(1)}, u32[]{:S(2)}, u32[]{:S(2)}) collective-permute-start(bf16[1,128,512]{2,1,0:T(8,128)(2,1)S(1)} %get-tuple-element.61), channel_id=1, source_target_pairs={{0,1},{1,2},{2,3},{3,32},{4,5},{5,6},{6,7},{7,36},{8,9},{9,10},{10... | collective-permute-start | bytes 393224 | tf_op jit(solution)/shard_map/ppermute | solution.py:245
  40.0 9.3 %collective-permute-start.9 = (bf16[1,128,512]{2,1,0:T(8,128)(2,1)S(1)}, bf16[1,128,512]{2,1,0:T(8,128)(2,1)S(1)}, u32[]{:S(2)}, u32[]{:S(2)}) collective-permute-start(bf16[1,128,512]{2,1,0:T(8,128)(2,1)S(1)} %get-tuple-element.62), channel_id=1, source_target_pairs={{0,35},{1,0},{2,1},{3,2},{4,39},{5,4},{6,5},{7,6},{8,43},{9,8},{10... | collective-permute-start | bytes 393224 | tf_op jit(solution)/shard_map/ppermute | solution.py:245
  42.7 7.9 %collective-permute-start.12 = (bf16[64,512]{1,0:T(8,128)(2,1)S(1)}, bf16[64,512]{1,0:T(8,128)(2,1)S(1)}, u32[]{:S(2)}, u32[]{:S(2)}) collective-permute-start(bf16[64,512]{1,0:T(8,128)(2,1)S(1)} %slice.18), channel_id=1, source_target_pairs={{0,64},{1,65},{2,66},{3,67},{4,68},{5,69},{6,70},{7,71},{8,72},{9,... | collective-permute-start | bytes 196616 | tf_op jit(solution)/shard_map/ppermute | solution.py:245
  45.1 5.6 %collective-permute-start.13 = (bf16[64,512]{1,0:T(8,128)(2,1)S(1)}, bf16[64,512]{1,0:T(8,128)(2,1)S(1)}, u32[]{:S(2)}, u32[]{:S(2)}) collective-permute-start(bf16[64,512]{1,0:T(8,128)(2,1)S(1)} %slice.19), channel_id=1, source_target_pairs={{0,192},{1,193},{2,194},{3,195},{4,196},{5,197},{6,198},{7,199},{8... | collective-permute-start | bytes 196616 | tf_op jit(solution)/shard_map/ppermute | solution.py:245
  50.7 13.3 %collective-permute-start.14 = (bf16[512,512]{1,0:T(8,128)(2,1)S(1)}, bf16[512,512]{1,0:T(8,128)(2,1)S(1)}, u32[]{:S(2)}, u32[]{:S(2)}) collective-permute-start(bf16[512,512]{1,0:T(8,128)(2,1)S(1)} %constant_dynamic-update-slice_fusion.5.m0), channel_id=1, source_target_pairs={{0,4},{1,5},{2,6},{3,7},{4,8},{5,9},{6,10},{7,11},{8,12},{9,13},{1... | collective-permute-start | bytes 1572872 | tf_op jit(solution)/shard_map/ppermute | solution.py:245
  50.8 13.2 %collective-permute-start.15 = (bf16[512,512]{1,0:T(8,128)(2,1)S(1)}, bf16[512,512]{1,0:T(8,128)(2,1)S(1)}, u32[]{:S(2)}, u32[]{:S(2)}) collective-permute-start(bf16[512,512]{1,0:T(8,128)(2,1)S(1)} %constant_dynamic-update-slice_fusion.5.m0), channel_id=1, source_target_pairs={{0,12},{1,13},{2,14},{3,15},{4,0},{5,1},{6,2},{7,3},{8,4},{9,5},{1... | collective-permute-start | bytes 1572872 | tf_op jit(solution)/shard_map/ppermute | solution.py:245
  64.0 8.2 %copy-start.2 = (f32[512,512]{1,0:T(8,128)}, f32[512,512]{1,0:T(8,128)S(1)}, u32[]{:S(2)}) copy-start(f32[512,512]{1,0:T(8,128)S(1)} %shard_map.258.rest_0_) | copy-start | bytes 3145732
  64.0 8.1 %collective-permute-start.16 = (bf16[256,512]{1,0:T(8,128)(2,1)S(1)}, bf16[256,512]{1,0:T(8,128)(2,1)S(1)}, u32[]{:S(2)}, u32[]{:S(2)}) collective-permute-start(bf16[256,512]{1,0:T(8,128)(2,1)S(1)} %slice.16), channel_id=1, source_target_pairs={{0,4},{1,5},{2,6},{3,7},{4,8},{5,9},{6,10},{7,11},{8,12},{9,13},{1... | collective-permute-start | bytes 786440 | tf_op jit(solution)/shard_map/ppermute | solution.py:245
  64.1 8.0 %collective-permute-start.17 = (bf16[256,512]{1,0:T(8,128)(2,1)S(1)}, bf16[256,512]{1,0:T(8,128)(2,1)S(1)}, u32[]{:S(2)}, u32[]{:S(2)}) collective-permute-start(bf16[256,512]{1,0:T(8,128)(2,1)S(1)} %slice.17), channel_id=1, source_target_pairs={{0,12},{1,13},{2,14},{3,15},{4,0},{5,1},{6,2},{7,3},{8,4},{9,5},{1... | collective-permute-start | bytes 786440 | tf_op jit(solution)/shard_map/ppermute | solution.py:245
  72.1 10.3 %collective-permute-start.18 = (bf16[512,512]{1,0:T(8,128)(2,1)S(1)}, bf16[512,512]{1,0:T(8,128)(2,1)S(1)}, u32[]{:S(2)}, u32[]{:S(2)}) collective-permute-start(bf16[512,512]{1,0:T(8,128)(2,1)S(1)} %constant_dynamic-update-slice_fusion.5.m0), channel_id=1, source_target_pairs={{0,16},{1,17},{2,18},{3,19},{4,20},{5,21},{6,22},{7,23},{8,24},{9,... | collective-permute-start | bytes 1572872 | tf_op jit(solution)/shard_map/ppermute | solution.py:245
  73.7 8.7 %collective-permute-start.19 = (bf16[512,512]{1,0:T(8,128)(2,1)S(1)}, bf16[512,512]{1,0:T(8,128)(2,1)S(1)}, u32[]{:S(2)}, u32[]{:S(2)}) collective-permute-start(bf16[512,512]{1,0:T(8,128)(2,1)S(1)} %collective-permute-done.14.m1), channel_id=1, source_target_pairs={{0,16},{1,17},{2,18},{3,19},{4,20},{5,21},{6,22},{7,23},{8,24},{9,... | collective-permute-start | bytes 1572872 | tf_op jit(solution)/shard_map/ppermute | solution.py:245
  73.8 8.6 %collective-permute-start.20 = (bf16[512,512]{1,0:T(8,128)(2,1)S(1)}, bf16[512,512]{1,0:T(8,128)(2,1)S(1)}, u32[]{:S(2)}, u32[]{:S(2)}) collective-permute-start(bf16[512,512]{1,0:T(8,128)(2,1)S(1)} %collective-permute-done.15.m2), channel_id=1, source_target_pairs={{0,16},{1,17},{2,18},{3,19},{4,20},{5,21},{6,22},{7,23},{8,24},{9,... | collective-permute-start | bytes 1572872 | tf_op jit(solution)/shard_map/ppermute | solution.py:245
  74.2 8.2 %collective-permute-start.21 = (bf16[256,512]{1,0:T(8,128)(2,1)S(1)}, bf16[256,512]{1,0:T(8,128)(2,1)S(1)}, u32[]{:S(2)}, u32[]{:S(2)}) collective-permute-start(bf16[256,512]{1,0:T(8,128)(2,1)S(1)} %collective-permute-done.16.m3), channel_id=1, source_target_pairs={{0,16},{1,17},{2,18},{3,19},{4,20},{5,21},{6,22},{7,23},{8,24},{9,... | collective-permute-start | bytes 786440 | tf_op jit(solution)/shard_map/ppermute | solution.py:245
  74.3 8.1 %collective-permute-start.22 = (bf16[256,512]{1,0:T(8,128)(2,1)S(1)}, bf16[256,512]{1,0:T(8,128)(2,1)S(1)}, u32[]{:S(2)}, u32[]{:S(2)}) collective-permute-start(bf16[256,512]{1,0:T(8,128)(2,1)S(1)} %collective-permute-done.17.m4), channel_id=1, source_target_pairs={{0,16},{1,17},{2,18},{3,19},{4,20},{5,21},{6,22},{7,23},{8,24},{9,... | collective-permute-start | bytes 786440 | tf_op jit(solution)/shard_map/ppermute | solution.py:245
  (13 other events, 59.2 us)
